TPU v7x, 32 devices: a whole 2x2x4 slice. The times are simulated.
32 devices in a mesh: expert: 8 (over y, x, core), tensor: 4 (over z).
Axes of the slice: x: 2, y: 2, z: 4, core: 2. Of those that a mesh axis runs over, the one named last changes fastest.
Arguments:
- inputs: bfloat16 [3072, 1024], P('expert'), may hold values from -6 to 6
- attention_gain: float32 [1024], replicated, may hold values from 0.5 to 1.5
- query_weight: bfloat16 [1024, 1024], P(None, 'tensor'), may hold values from -0.1875 to 0.1875
- key_weight: bfloat16 [1024, 512], P(None, 'tensor'), may hold values from -0.1875 to 0.1875
- value_weight: bfloat16 [1024, 512], P(None, 'tensor'), may hold values from -0.1875 to 0.1875
- out_weight: bfloat16 [1024, 1024], P('tensor'), may hold values from -1.5 to 1.5
- expert_gain: float32 [1024], replicated, may hold values from 0.5 to 1.5
- router_weight: bfloat16 [1024, 32], replicated, may hold values from -0.09375 to 0.09375
- gate_weight: bfloat16 [32, 1024, 512], P('expert', None, 'tensor'), may hold values from -0.1875 to 0.1875
- up_weight: bfloat16 [32, 1024, 512], P('expert', None, 'tensor'), may hold values from -0.1875 to 0.1875
- down_weight: bfloat16 [32, 512, 1024], P('expert', 'tensor'), may hold values from -1 to 1
- routes: int32 [3072, 8], P('expert'), may hold values from 0 to 31, all different within a row; in each aligned block of 384 rows (0 to 383, 384 to 767, ...) at most 192 rows name the same one
- seq_lens: int32 [2], replicated, may hold values from 384 to 1536, as said below
- cotangent: float32 [3072, 1024], P('expert'), may hold values from -6 to 6
Outputs:
- output: float32 [3072, 1024], P('expert')
- input_grad: float32 [3072, 1024], P('expert')
- balance_loss: float32 [], replicated
- expert_load: float32 [32], replicated
- attention_gain_grad: float32 [1024], replicated
- query_grad: float32 [1024, 1024], P(None, 'tensor')
- key_grad: float32 [1024, 512], P(None, 'tensor')
- value_grad: float32 [1024, 512], P(None, 'tensor')
- out_weight_grad: float32 [1024, 1024], P('tensor')
- expert_gain_grad: float32 [1024], replicated
- router_grad: float32 [1024, 32], replicated
- gate_grad: float32 [32, 1024, 512], P('expert', None, 'tensor')
- up_grad: float32 [32, 1024, 512], P('expert', None, 'tensor')
- down_grad: float32 [32, 512, 1024], P('expert', 'tensor')
Inputs may be any that keep to these rules, and one draw needn't show every extreme that they name: `routes`: in each aligned block of 384 rows (the rows of one device) no expert is named by more than 192 rows, a bound that some block reaches. `seq_lens`: one sequence has exactly 1536 valid tokens.
All inputs are finite; a program needn't handle non-finite values.
Results may differ from a plain program's by a relative error of at most 0.018.
Values may be sent and summed in bfloat16 or wider, within the bound.
A program may use at most 192 MiB of HBM per device.

v0:
```python
import math

import jax
import jax.numpy as jnp
from jax import lax
from jax.sharding import PartitionSpec as P

HD = 64
CAP = 192


EPS = 1e-06
THETA = 10000.0


def rope_tables(positions, head_size):
    half_size = head_size // 2
    frequency = THETA ** (-2.0 * jnp.arange(half_size, dtype=jnp.float32) / head_size)
    angles = positions.astype(jnp.float32)[:, None] * frequency[None, :]
    cosines = jnp.cos(angles)
    sine_table = jnp.sin(angles)
    return (jnp.concatenate([cosines, cosines], -1), jnp.concatenate([sine_table, sine_table], -1))


def rotate(values, cosines, sine_table, forward):
    half_size = values.shape[-1] // 2
    if forward:
        turned = jnp.concatenate([-values[..., half_size:], values[..., :half_size]], -1)
        return values * cosines[:, None, :] + turned * sine_table[:, None, :]
    scaled = values * sine_table[:, None, :]
    turned = jnp.concatenate([scaled[..., half_size:], -scaled[..., :half_size]], -1)
    return values * cosines[:, None, :] + turned


def head_total(partial_value):
    return lax.psum(partial_value, "tensor")


def shards(
    inputs,
    attention_gain,
    query_weight,
    key_weight,
    value_weight,
    out_weight,
    expert_gain,
    router_weight,
    gate_weight,
    up_weight,
    down_weight,
    routes,
    seq_lens,
    cotangent,
):
    f32 = jnp.float32
    bf16 = jnp.bfloat16
    tok_rows, model_width = inputs.shape
    expert_ranks = lax.axis_size("expert")
    tensor_ranks = lax.axis_size("tensor")
    expert_rank = lax.axis_index("expert")
    total_rows = tok_rows * expert_ranks
    seq_count = seq_lens.shape[0]
    seq_length = total_rows // seq_count
    span_rows = tok_rows // seq_count
    query_width = query_weight.shape[1]
    key_width = key_weight.shape[1]
    query_heads = query_width // HD
    key_heads = key_width // HD
    groups = query_heads // key_heads
    experts = router_weight.shape[1]
    chosen_count = routes.shape[1]
    local_experts = gate_weight.shape[0]
    hidden_units = gate_weight.shape[2]
    score_scale = HD ** (-0.5)
    col_share = model_width // tensor_ranks
    local_pos = expert_rank * span_rows + jnp.arange(span_rows, dtype=jnp.int32)
    row_pos = jnp.tile(local_pos, seq_count)
    key_block = math.gcd(seq_length, 2048)
    last_pos = expert_rank * span_rows + span_rows - 1
    used_blocks = last_pos // key_block + 1
    residual = inputs.astype(f32)
    norm_scale = lax.rsqrt(jnp.mean(residual * residual, -1, keepdims=True) + EPS)
    normed = (residual * norm_scale * attention_gain).astype(bf16)
    cosines, sine_table = rope_tables(row_pos, HD)
    query_lin = jnp.dot(normed, query_weight, preferred_element_type=f32)
    key_lin = jnp.dot(normed, key_weight, preferred_element_type=f32)
    value_lin = jnp.dot(normed, value_weight, preferred_element_type=f32)
    queries = rotate(
        query_lin.reshape(tok_rows, query_heads, HD), cosines, sine_table, True
    ).astype(bf16)
    keys_rot = rotate(key_lin.reshape(tok_rows, key_heads, HD), cosines, sine_table, True).astype(
        bf16
    )
    pair_local = jnp.concatenate(
        [keys_rot.reshape(tok_rows, key_width), value_lin.astype(bf16)], -1
    )
    flat = lax.all_gather(pair_local, "expert", axis=0, tiled=True)
    width_now = flat.shape[-1]
    shaped = flat.reshape(expert_ranks, seq_count, span_rows, width_now).transpose(1, 0, 2, 3)
    pairs_seq = shaped.reshape(seq_count, seq_length, width_now)
    query_groups = queries.reshape(seq_count, span_rows, key_heads, groups, HD)

    def block_scores(pairs_here, index):
        start = index * key_block
        pair_block = lax.dynamic_slice_in_dim(pairs_here, start, key_block, 1)
        pos_block = start + jnp.arange(key_block, dtype=jnp.int32)
        key_part = pair_block[..., :key_width].reshape(seq_count, key_block, key_heads, HD)
        value_part = pair_block[..., key_width:].reshape(seq_count, key_block, key_heads, HD)
        scores = (
            jnp.einsum("sqhgd,skhd->shgqk", query_groups, key_part, preferred_element_type=f32)
            * score_scale
        )
        allowed = (pos_block[None, None, :] <= local_pos[None, :, None]) & (
            pos_block[None, None, :] < seq_lens[:, None, None]
        )
        return (scores, allowed[:, None, None], key_part, value_part)

    def score_maxima(index, carry):
        running_max, running_sum = carry
        scores, allowed, _, _ = block_scores(pairs_seq, index)
        scores = jnp.where(allowed, scores, -1e30)
        new_max = jnp.maximum(running_max, jnp.max(scores, -1))
        weights_now = jnp.where(allowed, jnp.exp(scores - new_max[..., None]), 0.0)
        running_sum = running_sum * jnp.exp(running_max - new_max) + jnp.sum(weights_now, -1)
        return (new_max, running_sum)

    start_max = jnp.full((seq_count, key_heads, groups, span_rows), -1e30, f32)
    row_max, row_sum = lax.fori_loop(
        0, used_blocks, score_maxima, (start_max, jnp.zeros_like(start_max))
    )
    log_total = row_max + jnp.log(row_sum)

    def value_sums(index, totals):
        scores, allowed, _, value_part = block_scores(pairs_seq, index)
        probs_low = jnp.where(allowed, jnp.exp(scores - log_total[..., None]), 0.0).astype(bf16)
        return totals + jnp.einsum(
            "shgqk,skhd->shgqd", probs_low, value_part, preferred_element_type=f32
        )

    attended_raw = lax.fori_loop(
        0, used_blocks, value_sums, jnp.zeros((seq_count, key_heads, groups, span_rows, HD), f32)
    )
    attended = attended_raw.transpose(0, 3, 1, 2, 4).reshape(tok_rows, query_width).astype(bf16)
    middle = residual + head_total(jnp.dot(attended, out_weight, preferred_element_type=f32))
    norm_scale2 = lax.rsqrt(jnp.mean(middle * middle, -1, keepdims=True) + EPS)
    normed2 = (middle * norm_scale2 * expert_gain).astype(bf16)
    logits = jnp.dot(normed2, router_weight, preferred_element_type=f32)
    router_probs = jax.nn.softmax(logits, -1)
    onehot = (routes[:, :, None] == jnp.arange(experts, dtype=jnp.int32)[None, None, :]).astype(f32)
    chosen = jnp.einsum("tke,te->tk", onehot, logits)
    gates = jax.nn.softmax(chosen, -1)
    counts = jnp.sum(onehot, (0, 1))
    prob_sums = jnp.sum(router_probs, 0)
    counts_all, prob_all = lax.psum((counts, prob_sums), "expert")
    share = counts_all / (total_rows * chosen_count)
    expert_load = experts * experts * share * (prob_all / total_rows)
    balance_loss = jnp.mean(expert_load)
    flat_expert = routes.reshape(-1)
    flat_hot = (flat_expert[:, None] == jnp.arange(experts, dtype=jnp.int32)[None, :]).astype(
        jnp.int32
    )
    earlier = jnp.cumsum(flat_hot, 0) - flat_hot
    slot_index = jnp.sum(earlier * flat_hot, 1)
    dest = flat_expert * CAP + slot_index
    pair_count = tok_rows * chosen_count
    owner_of = (
        jnp.full((experts * CAP,), pair_count, jnp.int32)
        .at[dest]
        .set(jnp.arange(pair_count, dtype=jnp.int32))
    )
    rows_ext = jnp.concatenate([normed2, jnp.zeros((1, model_width), bf16)], 0)
    send_rows = rows_ext[owner_of // chosen_count].reshape(experts, CAP, model_width)

    def send_owners(buffer):
        got = lax.all_to_all(buffer, "expert", split_axis=0, concat_axis=0, tiled=True)
        got = got.reshape(expert_ranks, local_experts, CAP, model_width).transpose(1, 0, 2, 3)
        return got.reshape(local_experts, expert_ranks * CAP, model_width)

    def finish_rows(partial_value):
        share_rows = lax.psum_scatter(
            partial_value, "tensor", scatter_dimension=2, tiled=True
        ).astype(bf16)
        share_rows = share_rows.reshape(local_experts, expert_ranks, CAP, col_share).transpose(
            1, 0, 2, 3
        )
        share_rows = lax.all_to_all(
            share_rows.reshape(experts, CAP, col_share),
            "expert",
            split_axis=0,
            concat_axis=0,
            tiled=True,
        )
        whole = lax.all_gather(share_rows, "tensor", axis=2, tiled=True)
        return whole.reshape(experts * CAP, model_width)

    both_used = jnp.concatenate([gate_weight, up_weight], -1)
    rows_in = send_owners(send_rows)
    both_val = jnp.einsum("erd,edf->erf", rows_in, both_used, preferred_element_type=f32)
    gate_val = both_val[..., :hidden_units]
    up_val = both_val[..., hidden_units:]
    sigmoid_gate = jax.nn.sigmoid(gate_val)
    silu_gate = gate_val * sigmoid_gate
    inner = (silu_gate * up_val).astype(bf16)
    returned = finish_rows(
        jnp.einsum("erf,efd->erd", inner, down_weight, preferred_element_type=f32)
    )
    picked = returned[dest].reshape(tok_rows, chosen_count, model_width).astype(f32)
    output = middle + jnp.einsum("tk,tkd->td", gates, picked)
    grad_gates = jnp.einsum("td,tkd->tk", cotangent, picked)
    grad_out_rows = (
        (gates[:, :, None] * cotangent[:, None, :]).astype(bf16).reshape(pair_count, model_width)
    )
    grad_ext = jnp.concatenate([grad_out_rows, jnp.zeros((1, model_width), bf16)], 0)
    grad_send = grad_ext[owner_of].reshape(experts, CAP, model_width)
    grad_rows = send_owners(grad_send)
    grad_inner = jnp.einsum("erd,efd->erf", grad_rows, down_weight, preferred_element_type=f32)
    grad_gate_val = grad_inner * up_val * sigmoid_gate * (1.0 + gate_val * (1.0 - sigmoid_gate))
    grad_up_val = grad_inner * silu_gate
    grad_both = jnp.concatenate([grad_gate_val, grad_up_val], -1).astype(bf16)
    both_term = jnp.einsum("erd,erf->edf", rows_in, grad_both, preferred_element_type=f32)
    down_term = jnp.einsum("erf,erd->efd", inner, grad_rows, preferred_element_type=f32)
    gate_grad = both_term[..., :hidden_units]
    up_grad = both_term[..., hidden_units:]
    grad_pairs = finish_rows(
        jnp.einsum("erf,edf->erd", grad_both, both_used, preferred_element_type=f32)
    )
    grad_normed2 = jnp.sum(
        grad_pairs[dest].reshape(tok_rows, chosen_count, model_width).astype(f32), 1
    )
    grad_chosen = gates * (grad_gates - jnp.sum(grad_gates * gates, -1, keepdims=True))
    grad_logits = jnp.einsum("tke,tk->te", onehot, grad_chosen)
    loss_weight = (experts * share / total_rows)[None, :]
    grad_logits = grad_logits + router_probs * (
        loss_weight - jnp.sum(loss_weight * router_probs, -1, keepdims=True)
    )
    grad_logit_low = grad_logits.astype(bf16)
    router_grad = jnp.dot(normed2.T, grad_logit_low, preferred_element_type=f32)
    grad_normed2 = grad_normed2 + jnp.dot(
        grad_logit_low, router_weight.T, preferred_element_type=f32
    )
    gained2 = grad_normed2 * expert_gain
    expert_gain_grad = jnp.sum(grad_normed2 * middle * norm_scale2, 0)
    grad_middle = (
        cotangent
        + norm_scale2 * gained2
        - middle * norm_scale2**3 * jnp.mean(gained2 * middle, -1, keepdims=True)
    )
    grad_attn = grad_middle.astype(bf16)
    out_weight_grad = jnp.dot(attended.T, grad_attn, preferred_element_type=f32)
    grad_attended = jnp.dot(grad_attn, out_weight.T, preferred_element_type=f32).astype(bf16)
    grad_og = grad_attended.reshape(seq_count, span_rows, key_heads, groups, HD)
    delta = jnp.einsum("sqhgd,shgqd->shgq", grad_og.astype(f32), attended_raw)

    def score_grads(index, carry):
        query_acc, pair_buffer = carry
        scores, allowed, key_part, value_part = block_scores(pairs_seq, index)
        soft = jnp.where(allowed, jnp.exp(scores - log_total[..., None]), 0.0)
        grad_probs = jnp.einsum(
            "sqhgd,skhd->shgqk", grad_og, value_part, preferred_element_type=f32
        )
        grad_scores = (soft * (grad_probs - delta[..., None])).astype(bf16)
        query_acc = query_acc + jnp.einsum(
            "shgqk,skhd->sqhgd", grad_scores, key_part, preferred_element_type=f32
        )
        key_term = (
            jnp.einsum("shgqk,sqhgd->skhd", grad_scores, query_groups, preferred_element_type=f32)
            * score_scale
        )
        value_term = jnp.einsum(
            "shgqk,sqhgd->skhd", soft.astype(bf16), grad_og, preferred_element_type=f32
        )
        block_terms = jnp.concatenate(
            [
                key_term.reshape(seq_count, -1, key_width),
                value_term.reshape(seq_count, -1, key_width),
            ],
            -1,
        )
        pair_buffer = lax.dynamic_update_slice_in_dim(
            pair_buffer, block_terms, index * key_block, 1
        )
        return (query_acc, pair_buffer)

    grad_query_rot, seq_terms = lax.fori_loop(
        0,
        used_blocks,
        score_grads,
        (
            jnp.zeros((seq_count, span_rows, key_heads, groups, HD), f32),
            jnp.zeros((seq_count, seq_length, 2 * key_width), f32),
        ),
    )
    all_terms = seq_terms.reshape(seq_count, expert_ranks, span_rows, 2 * key_width).transpose(
        1, 0, 2, 3
    )
    all_terms = all_terms.reshape(total_rows, 2 * key_width)
    pair_grad = lax.psum_scatter(all_terms, "expert", scatter_dimension=0, tiled=True)
    grad_query_rot = grad_query_rot.reshape(tok_rows, query_heads, HD) * score_scale
    grad_query_lin = (
        rotate(grad_query_rot, cosines, sine_table, False)
        .reshape(tok_rows, query_width)
        .astype(bf16)
    )
    grad_key_lin = (
        rotate(
            pair_grad[:, :key_width].reshape(tok_rows, key_heads, HD), cosines, sine_table, False
        )
        .reshape(tok_rows, key_width)
        .astype(bf16)
    )
    grad_value_lin = pair_grad[:, key_width:].astype(bf16)
    query_grad = jnp.dot(normed.T, grad_query_lin, preferred_element_type=f32)
    key_grad = jnp.dot(normed.T, grad_key_lin, preferred_element_type=f32)
    value_grad = jnp.dot(normed.T, grad_value_lin, preferred_element_type=f32)
    grad_normed = head_total(
        jnp.dot(grad_query_lin, query_weight.T, preferred_element_type=f32)
        + jnp.dot(grad_key_lin, key_weight.T, preferred_element_type=f32)
        + jnp.dot(grad_value_lin, value_weight.T, preferred_element_type=f32)
    )
    gained1 = grad_normed * attention_gain
    attention_gain_grad = jnp.sum(grad_normed * residual * norm_scale, 0)
    input_grad = (
        grad_middle
        + norm_scale * gained1
        - residual * norm_scale**3 * jnp.mean(gained1 * residual, -1, keepdims=True)
    )
    (
        attention_gain_grad,
        query_grad,
        key_grad,
        value_grad,
        out_weight_grad,
        expert_gain_grad,
        router_grad,
    ) = lax.psum(
        (
            attention_gain_grad,
            query_grad,
            key_grad,
            value_grad,
            out_weight_grad,
            expert_gain_grad,
            router_grad,
        ),
        "expert",
    )
    return (
        output,
        input_grad,
        balance_loss,
        expert_load,
        attention_gain_grad,
        query_grad,
        key_grad,
        value_grad,
        out_weight_grad,
        expert_gain_grad,
        router_grad,
        gate_grad,
        up_grad,
        down_term,
    )


def solution(mesh):
    placed = (
        P("expert", None),
        P(),
        P(None, "tensor"),
        P(None, "tensor"),
        P(None, "tensor"),
        P("tensor", None),
        P(),
        P(),
        P("expert", None, "tensor"),
        P("expert", None, "tensor"),
        P("expert", "tensor", None),
        P("expert", None),
        P(),
        P("expert", None),
    )
    return jax.shard_map(
        shards,
        mesh=mesh,
        in_specs=placed,
        out_specs=(
            P("expert", None),
            P("expert", None),
            P(),
            P(),
            P(),
            P(None, "tensor"),
            P(None, "tensor"),
            P(None, "tensor"),
            P("tensor", None),
            P(),
            P(),
            P("expert", None, "tensor"),
            P("expert", None, "tensor"),
            P("expert", "tensor", None),
        ),
        check_vma=False,
    )
```

profile of v0, /device:TPU:0, one launch (start us, length us, event | category | flops | bytes accessed | tf_op | source)
XLA Modules:
  0.0 2216.3 jit_solution(5521068722448970389)
XLA Ops:
  18.2 24.7 %all-gather.4.cloned.1.call-done = bf16[3072,256]{0,1:T(8,128)(2,1)} async-done(((bf16[384,256]{0,1:T(8,128)(2,1)}), bf16[3072,256]{0,1:T(8,128)(2,1)}) %all-gather.4.cloned.1.call-update) | async-done | bytes 1572880 | tf_op jit(solution)/shard_map/all_gather | solution.py:97
  72.0 12.0 scatter_custom_fusion
  84.1 58.0 %all-reduce.8.cloned.1.call-done = f32[384,1024]{1,0:T(8,128)} async-done(((f32[384,1024]{1,0:T(8,128)}), f32[384,1024]{1,0:T(8,128)}) %all-reduce.8.cloned.1.call-update) | async-done | bytes 1572880 | tf_op jit(solution)/shard_map/psum | solution.py:36
  145.3 26.9 %gather_fusion = bf16[6144,1024]{1,0:T(8,128)(2,1)} fusion(bf16[385,1024]{1,0:T(8,128)(2,1)S(1)} %concatenate.61, s32[6144]{0:T(1024)S(1)} %get-tuple-element.405), kind=kCustom, calls=%fused_computation | custom fusion | bytes 25190400 | tf_op jit(solution)/shard_map/gather | solution.py:172
  182.1 134.4 %all-to-all-done = bf16[32,192,1024]{2,1,0:T(8,128)(2,1)} async-done(((bf16[32,192,1024]{2,1,0:T(8,128)(2,1)}), bf16[32,192,1024]{2,1,0:T(8,128)(2,1)}, u32[]{:S(2)}, u32[]{:S(2)}) %all-to-all-start) | async-done | bytes 12582944 | tf_op jit(solution)/shard_map/all_to_all | solution.py:175
  334.6 10.1 fusion.92
  344.8 411.7 %reduce-scatter.4.cloned.1.call-done = f32[4,1536,256]{2,1,0:T(8,128)} async-done(((f32[4,1536,1024]{2,1,0:T(8,128)}), f32[4,1536,256]{2,1,0:T(8,128)}) %reduce-scatter.4.cloned.1.call-update) | async-done | bytes 6291472 | tf_op jit(solution)/shard_map/reduce_scatter | solution.py:180
  759.9 41.4 %all_to_all.20 = bf16[32,192,256]{2,1,0:T(8,128)(2,1)} all-to-all(bf16[32,192,256]{2,1,0:T(8,128)(2,1)S(1)} %bitcast.312), channel_id=1, replica_groups=mesh['expert'=8,'tensor'=4] {'expert'}, dimensions={0} | all-to-all | bytes 6291456 | tf_op jit(solution)/shard_map/all_to_all | solution.py:186
  802.9 216.2 %all-gather.6.cloned.1.call-done = bf16[32,192,1024]{2,1,0:T(8,128)(2,1)} async-done(((bf16[32,192,256]{2,1,0:T(8,128)(2,1)}), bf16[32,192,1024]{2,1,0:T(8,128)(2,1)}) %all-gather.6.cloned.1.call-update) | async-done | bytes 12582928 | tf_op jit(solution)/shard_map/all_gather | solution.py:193
  1019.1 22.2 %gather_fusion.1 = bf16[3072,1024]{1,0:T(8,128)(2,1)} fusion(bf16[6144,1024]{1,0:T(8,128)(2,1)} %bitcast.298, s32[3072]{0:T(1024)S(1)} %broadcast_clamp_fusion), kind=kCustom, calls=%fused_computation.1 | custom fusion | bytes 12595200 | tf_op jit(solution)/shard_map/gather | solution.py:207
  1052.2 34.4 %gather_fusion.2 = bf16[6144,1024]{1,0:T(8,128)(2,1)} fusion(bf16[3073,1024]{1,0:T(8,128)(2,1)} %concatenate.63, s32[6144]{0:T(1024)S(1)} %get-tuple-element.404), kind=kCustom, calls=%fused_computation.2 | custom fusion | bytes 25190400 | tf_op jit(solution)/shard_map/gather | solution.py:214
  1086.6 142.9 %all_to_all.21 = bf16[32,192,1024]{2,1,0:T(8,128)(2,1)S(1)} all-to-all(bf16[32,192,1024]{2,1,0:T(8,128)(2,1)} %bitcast.306), channel_id=1, replica_groups=mesh['expert'=8,'tensor'=4] {'expert'}, dimensions={0} | all-to-all | bytes 25165824 | tf_op jit(solution)/shard_map/all_to_all | solution.py:175
  1231.4 11.0 multiply_convert_fusion.1
  1242.5 12.1 fusion.33
  1254.8 410.7 %reduce-scatter.6.cloned.1.call-done = f32[4,1536,256]{2,1,0:T(8,128)} async-done(((f32[4,1536,1024]{2,1,0:T(8,128)}), f32[4,1536,256]{2,1,0:T(8,128)}) %reduce-scatter.6.cloned.1.call-update) | async-done | bytes 6291472 | tf_op jit(solution)/shard_map/reduce_scatter | solution.py:180
  1668.8 41.4 %all_to_all.22 = bf16[32,192,256]{2,1,0:T(8,128)(2,1)} all-to-all(bf16[32,192,256]{2,1,0:T(8,128)(2,1)S(1)} %bitcast.313), channel_id=1, replica_groups=mesh['expert'=8,'tensor'=4] {'expert'}, dimensions={0} | all-to-all | bytes 6291456 | tf_op jit(solution)/shard_map/all_to_all | solution.py:186
  1710.7 11.8 psum.78
  1728.6 199.5 %all-gather.8.cloned.1.call-done = bf16[32,192,1024]{2,1,0:T(8,128)(2,1)} async-done(((bf16[32,192,256]{2,1,0:T(8,128)(2,1)}), bf16[32,192,1024]{2,1,0:T(8,128)(2,1)}) %all-gather.8.cloned.1.call-update) | async-done | bytes 12582928 | tf_op jit(solution)/shard_map/all_gather | solution.py:193
  1928.1 22.1 gather_fusion.3
  1966.6 11.1 while.39
  1990.5 61.4 %reduce-scatter.8.cloned.1.call-done = f32[384,256]{0,1:T(8,128)} async-done(((f32[3072,256]{0,1:T(8,128)}), f32[384,256]{0,1:T(8,128)}) %reduce-scatter.8.cloned.1.call-update) | async-done | bytes 393232 | tf_op jit(solution)/shard_map/reduce_scatter | solution.py:297
  2082.9 43.2 %all-reduce.10.cloned.1.call-done = f32[384,1024]{1,0:T(8,128)} async-done(((f32[384,1024]{1,0:T(8,128)}), f32[384,1024]{1,0:T(8,128)}) %all-reduce.10.cloned.1.call-update) | async-done | bytes 1572880 | tf_op jit(solution)/shard_map/psum | solution.py:36
  2128.1 13.8 all-reduce.2
  2146.7 56.0 %all-reduce.12.cloned.1.call-done = (f32[1024,256]{1,0:T(8,128)}, f32[1024,128]{1,0:T(8,128)}, f32[1024,128]{1,0:T(8,128)}, f32[256,1024]{1,0:T(8,128)}, f32[1024,32]{0,1:T(8,128)}) async-done(((f32[1024,256]{1,0:T(8,128)}, f32[1024,128]{1,0:T(8,128)}, f32[1024,128]{1,0:T(8,128)}, f32[256,1024]{1,0:T(8,128)}, f32[1024,32]{0,1:T(8,128)}), (f32[1024,256]{1,0:T(8,128)}, f32[1024,128]{1,0:T(8,128)}, ...) | async-done | bytes 3276816 | tf_op jit(solution)/shard_map/psum | solution.py:335
  (306 shorter events, 187.0 us)
Async XLA Ops:
  7.2 327.5 %copy-start = (bf16[4,128,1024]{2,1,0:T(8,128)(2,1)S(1)}, bf16[4,128,1024]{2,1,0:T(8,128)(2,1)}, u32[]{:S(2)}) copy-start(bf16[4,128,1024]{2,1,0:T(8,128)(2,1)} %param.30) | copy-start | bytes 3145732
  7.2 35.6 %all-gather.4.cloned.1.call-start = ((), (), s32[]{:S(2)}) async-start(), calls=%async_computation.7 | async-start | bytes 1769472 | tf_op jit(solution)/shard_map/all_gather | solution.py:97
  14.1 128.0 %all-reduce.8.cloned.1.call-start = ((), (), s32[]{:S(2)}) async-start(), calls=%async_computation.8 | async-start | bytes 3145728 | tf_op jit(solution)/shard_map/psum | solution.py:36
  17.4 30.7 %copy-start.26 = (s32[384,8]{1,0:T(8,128)}, s32[384,8]{1,0:T(8,128)S(1)}, u32[]{:S(2)}) copy-start(s32[384,8]{1,0:T(8,128)S(1)} %copy.84) | copy-start | bytes 36868
  72.0 73.0 %copy-start.52 = (f32[1024]{0:T(1024)S(1)}, f32[1024]{0:T(1024)}, u32[]{:S(2)}) copy-start(f32[1024]{0:T(1024)} %param.26) | copy-start | bytes 12292
  144.5 27.7 %copy-start.56 = (f32[384]{0:T(512)}, f32[384]{0:T(512)S(1)}, u32[]{:S(2)}) copy-start(f32[384]{0:T(512)S(1)} %get-tuple-element.411) | copy-start | bytes 4612
  145.2 656.6 %copy-start.13 = (bf16[384,1024]{1,0:T(8,128)(2,1)}, bf16[384,1024]{1,0:T(8,128)(2,1)S(1)}, u32[]{:S(2)}) copy-start(bf16[384,1024]{1,0:T(8,128)(2,1)S(1)} %multiply_convert_fusion.3) | copy-start | bytes 2359300
  172.1 144.4 %all-to-all-start = ((bf16[32,192,1024]{2,1,0:T(8,128)(2,1)}), bf16[32,192,1024]{2,1,0:T(8,128)(2,1)}, u32[]{:S(2)}, u32[]{:S(2)}) async-start(bf16[32,192,1024]{2,1,0:T(8,128)(2,1)} %bitcast.305), calls=%async_computation | async-start | bytes 25165824 | tf_op jit(solution)/shard_map/all_to_all | solution.py:175
  177.5 579.1 %reduce-scatter.4.cloned.1.call-start = ((), (), s32[]{:S(2)}) async-start(), calls=%async_computation.9 | async-start | bytes 31457280 | tf_op jit(solution)/shard_map/reduce_scatter | solution.py:180
  344.8 674.4 %all-gather.6.cloned.1.call-start = ((), (), s32[]{:S(2)}) async-start(), calls=%async_computation.10 | async-start | bytes 15728640 | tf_op jit(solution)/shard_map/all_gather | solution.py:193
  801.3 864.2 %reduce-scatter.6.cloned.1.call-start = ((), (), s32[]{:S(2)}) async-start(), calls=%async_computation.11 | async-start | bytes 31457280 | tf_op jit(solution)/shard_map/reduce_scatter | solution.py:180
  1019.1 22.2 %copy-start.15 = (f32[384,1024]{1,0:T(8,128)S(1)}, f32[384,1024]{1,0:T(8,128)}, u32[]{:S(2)}) copy-start(f32[384,1024]{1,0:T(8,128)} %param.33) | copy-start | bytes 4718596
  1231.4 11.0 copy-start.4
  1231.4 11.0 copy-start.21
  1231.4 11.0 copy-start.23
  1254.5 673.5 %all-gather.8.cloned.1.call-start = ((), (), s32[]{:S(2)}) async-start(), calls=%async_computation.12 | async-start | bytes 15728640 | tf_op jit(solution)/shard_map/all_gather | solution.py:193
  1710.2 341.7 %reduce-scatter.8.cloned.1.call-start = ((), (), s32[]{:S(2)}) async-start(), calls=%async_computation.13 | async-start | bytes 3538944 | tf_op jit(solution)/shard_map/reduce_scatter | solution.py:297
  1985.1 141.0 %all-reduce.10.cloned.1.call-start = ((), (), s32[]{:S(2)}) async-start(), calls=%async_computation.14 | async-start | bytes 3145728 | tf_op jit(solution)/shard_map/psum | solution.py:36
  1989.5 63.4 %copy-start.35 = (f32[384,64]{0,1:T(8,128)S(1)}, f32[384,64]{0,1:T(8,128)}, u32[]{:S(2)}) copy-start(f32[384,64]{0,1:T(8,128)} %copy-done.34) | copy-start | bytes 294916
  1990.1 63.0 %copy-start.33 = (f32[384,64]{0,1:T(8,128)S(1)}, f32[384,64]{0,1:T(8,128)}, u32[]{:S(2)}) copy-start(f32[384,64]{0,1:T(8,128)} %copy-done.32) | copy-start | bytes 294916
  1990.5 64.9 %copy-start.44 = (bf16[1024,128]{1,0:T(8,128)(2,1)S(1)}, bf16[1024,128]{1,0:T(8,128)(2,1)}, u32[]{:S(2)}) copy-start(bf16[1024,128]{1,0:T(8,128)(2,1)} %param.24) | copy-start | bytes 786436
  2056.9 9.7 copy-start.10
  2057.0 145.7 %all-reduce.12.cloned.1.call-start = ((), (), s32[]{:S(2)}) async-start(), calls=%async_computation.15 | async-start | bytes 6553600 | tf_op jit(solution)/shard_map/psum | solution.py:335
  2082.9 60.7 %copy-start.58 = (f32[384]{0:T(512)S(1)}, f32[384]{0:T(512)}, u32[]{:S(2)}) copy-start(f32[384]{0:T(512)} %get-tuple-element.408) | copy-start | bytes 4612
  (48 other events, 168.4 us)
Sparse Core Ops, SparseCore 0:
  14.2 28.5 all-gather.3
  60.8 81.2 all-reduce.7
  344.9 411.6 reduce-scatter.3
  801.4 217.6 all-gather.5
  1254.7 410.7 reduce-scatter.5
  1710.3 217.6 all-gather.7
  1985.2 66.6 reduce-scatter.7
  2057.0 69.0 all-reduce.9
  2131.7 70.8 all-reduce.11
where the time goes:
time: 2230 us; the launch traced here: 2220 us
  waiting for transfers between devices  1620 us (73%)
  blocking collectives  251 us (11%)
  local copies, waits for them, and re-layouts  181 us (8%)
  matrix products  92.9 us (4%)
  other arithmetic  51 us (2%)
    reduce_scatter x2, waiting for transfers between devices, finish_rows(): lax.psum_scatter(partial_value, 'tensor', scatter_dimension=2, tiled=True)  822 us
    all_gather x2, waiting for transfers between devices, finish_rows(): whole = lax.all_gather(share_rows, 'tensor', axis=2, tiled=True)  416 us
    all_to_all x1, blocking collectives, send_owners(): lax.all_to_all(buffer, 'expert', split_axis=0, concat_axis=0, tiled=True)  143 us
    all_to_all x1, waiting for transfers between devices, send_owners(): lax.all_to_all(buffer, 'expert', split_axis=0, concat_axis=0, tiled=True)  134 us
    psum x2, waiting for transfers between devices, head_total(): return lax.psum(partial_value, 'tensor')  101 us
    all_to_all x2, blocking collectives, finish_rows(): lax.all_to_all(share_rows.reshape(experts, CAP, col_share), 'expert', spl...  82.8 us
    reduce_scatter x1, waiting for transfers between devices, shards(): lax.psum_scatter(all_terms, 'expert', scatter_dimension=0, tiled=True)  61.4 us
    psum x1, waiting for transfers between devices, shards(): lax.psum((attention_gain_grad, query_grad, key_grad, value_grad, out_weig...  56 us
  transfers between devices with their start and end apart: 10, of which 10 were waited for; matrix products, arithmetic and copies ran while one was open for 3% of the time, Pallas kernels for 0%

commit v1 on v0

--- a/solution.py
+++ b/solution.py
@@ -6,8 +6,6 @@
 from jax.sharding import PartitionSpec as P
 
 HD = 64
-CAP = 192
-
 
 EPS = 1e-06
 THETA = 10000.0
@@ -56,7 +54,6 @@
     bf16 = jnp.bfloat16
     tok_rows, model_width = inputs.shape
     expert_ranks = lax.axis_size("expert")
-    tensor_ranks = lax.axis_size("tensor")
     expert_rank = lax.axis_index("expert")
     total_rows = tok_rows * expert_ranks
     seq_count = seq_lens.shape[0]
@@ -72,7 +69,6 @@
     local_experts = gate_weight.shape[0]
     hidden_units = gate_weight.shape[2]
     score_scale = HD ** (-0.5)
-    col_share = model_width // tensor_ranks
     local_pos = expert_rank * span_rows + jnp.arange(span_rows, dtype=jnp.int32)
     row_pos = jnp.tile(local_pos, seq_count)
     key_block = math.gcd(seq_length, 2048)
@@ -155,80 +151,76 @@
     share = counts_all / (total_rows * chosen_count)
     expert_load = experts * experts * share * (prob_all / total_rows)
     balance_loss = jnp.mean(expert_load)
-    flat_expert = routes.reshape(-1)
-    flat_hot = (flat_expert[:, None] == jnp.arange(experts, dtype=jnp.int32)[None, :]).astype(
-        jnp.int32
-    )
-    earlier = jnp.cumsum(flat_hot, 0) - flat_hot
-    slot_index = jnp.sum(earlier * flat_hot, 1)
-    dest = flat_expert * CAP + slot_index
-    pair_count = tok_rows * chosen_count
-    owner_of = (
-        jnp.full((experts * CAP,), pair_count, jnp.int32)
-        .at[dest]
-        .set(jnp.arange(pair_count, dtype=jnp.int32))
-    )
-    rows_ext = jnp.concatenate([normed2, jnp.zeros((1, model_width), bf16)], 0)
-    send_rows = rows_ext[owner_of // chosen_count].reshape(experts, CAP, model_width)
-
-    def send_owners(buffer):
-        got = lax.all_to_all(buffer, "expert", split_axis=0, concat_axis=0, tiled=True)
-        got = got.reshape(expert_ranks, local_experts, CAP, model_width).transpose(1, 0, 2, 3)
-        return got.reshape(local_experts, expert_ranks * CAP, model_width)
-
-    def finish_rows(partial_value):
-        share_rows = lax.psum_scatter(
-            partial_value, "tensor", scatter_dimension=2, tiled=True
-        ).astype(bf16)
-        share_rows = share_rows.reshape(local_experts, expert_ranks, CAP, col_share).transpose(
-            1, 0, 2, 3
-        )
-        share_rows = lax.all_to_all(
-            share_rows.reshape(experts, CAP, col_share),
+    combine = jnp.einsum("tke,tk->te", onehot, gates)
+
+    rows_all = lax.all_gather(normed2, "expert", axis=0, tiled=True)
+    cot_all = lax.all_gather(cotangent.astype(bf16), "expert", axis=0, tiled=True)
+    combine_own = lax.all_to_all(
+        combine.reshape(tok_rows, expert_ranks, local_experts),
+        "expert",
+        split_axis=1,
+        concat_axis=0,
+        tiled=True,
+    ).reshape(total_rows, local_experts)
+    width = local_experts * hidden_units
+    gate_flat = gate_weight.transpose(1, 0, 2).reshape(model_width, width)
+    up_flat = up_weight.transpose(1, 0, 2).reshape(model_width, width)
+    down_flat = down_weight.reshape(width, model_width)
+    gate_val = jnp.dot(rows_all, gate_flat, preferred_element_type=f32)
+    up_val = jnp.dot(rows_all, up_flat, preferred_element_type=f32)
+    sigmoid_gate = jax.nn.sigmoid(gate_val)
+    silu_gate = gate_val * sigmoid_gate
+    inner = silu_gate * up_val
+    weight_wide = jnp.repeat(combine_own, hidden_units, axis=1)
+    inner_low = (inner * weight_wide).astype(bf16)
+    cot_down = jnp.dot(cot_all, down_flat.T, preferred_element_type=f32)
+    gate_sums = jnp.sum((inner * cot_down).reshape(total_rows, local_experts, hidden_units), -1)
+    grad_inner = cot_down * weight_wide
+    grad_gate_val = (
+        grad_inner * up_val * sigmoid_gate * (1.0 + gate_val * (1.0 - sigmoid_gate))
+    ).astype(bf16)
+    grad_up_val = (grad_inner * silu_gate).astype(bf16)
+
+    def collect(partial_value):
+        parts = lax.all_to_all(
+            partial_value.astype(bf16).reshape(expert_ranks, tok_rows, model_width),
             "expert",
             split_axis=0,
             concat_axis=0,
             tiled=True,
         )
-        whole = lax.all_gather(share_rows, "tensor", axis=2, tiled=True)
-        return whole.reshape(experts * CAP, model_width)
-
-    both_used = jnp.concatenate([gate_weight, up_weight], -1)
-    rows_in = send_owners(send_rows)
-    both_val = jnp.einsum("erd,edf->erf", rows_in, both_used, preferred_element_type=f32)
-    gate_val = both_val[..., :hidden_units]
-    up_val = both_val[..., hidden_units:]
-    sigmoid_gate = jax.nn.sigmoid(gate_val)
-    silu_gate = gate_val * sigmoid_gate
-    inner = (silu_gate * up_val).astype(bf16)
-    returned = finish_rows(
-        jnp.einsum("erf,efd->erd", inner, down_weight, preferred_element_type=f32)
-    )
-    picked = returned[dest].reshape(tok_rows, chosen_count, model_width).astype(f32)
-    output = middle + jnp.einsum("tk,tkd->td", gates, picked)
-    grad_gates = jnp.einsum("td,tkd->tk", cotangent, picked)
-    grad_out_rows = (
-        (gates[:, :, None] * cotangent[:, None, :]).astype(bf16).reshape(pair_count, model_width)
-    )
-    grad_ext = jnp.concatenate([grad_out_rows, jnp.zeros((1, model_width), bf16)], 0)
-    grad_send = grad_ext[owner_of].reshape(experts, CAP, model_width)
-    grad_rows = send_owners(grad_send)
-    grad_inner = jnp.einsum("erd,efd->erf", grad_rows, down_weight, preferred_element_type=f32)
-    grad_gate_val = grad_inner * up_val * sigmoid_gate * (1.0 + gate_val * (1.0 - sigmoid_gate))
-    grad_up_val = grad_inner * silu_gate
-    grad_both = jnp.concatenate([grad_gate_val, grad_up_val], -1).astype(bf16)
-    both_term = jnp.einsum("erd,erf->edf", rows_in, grad_both, preferred_element_type=f32)
-    down_term = jnp.einsum("erf,erd->efd", inner, grad_rows, preferred_element_type=f32)
-    gate_grad = both_term[..., :hidden_units]
-    up_grad = both_term[..., hidden_units:]
-    grad_pairs = finish_rows(
-        jnp.einsum("erf,edf->erd", grad_both, both_used, preferred_element_type=f32)
-    )
-    grad_normed2 = jnp.sum(
-        grad_pairs[dest].reshape(tok_rows, chosen_count, model_width).astype(f32), 1
-    )
-    grad_chosen = gates * (grad_gates - jnp.sum(grad_gates * gates, -1, keepdims=True))
-    grad_logits = jnp.einsum("tke,tk->te", onehot, grad_chosen)
+        return lax.psum(jnp.sum(parts.astype(f32), 0), "tensor")
+
+    mixed = collect(jnp.dot(inner_low, down_flat, preferred_element_type=f32))
+    output = middle + mixed
+    grad_normed2 = collect(
+        jnp.dot(grad_gate_val, gate_flat.T, preferred_element_type=f32)
+        + jnp.dot(grad_up_val, up_flat.T, preferred_element_type=f32)
+    )
+    grad_gates = lax.psum(
+        lax.all_to_all(
+            gate_sums.reshape(expert_ranks, tok_rows, local_experts),
+            "expert",
+            split_axis=0,
+            concat_axis=2,
+            tiled=True,
+        ).reshape(tok_rows, experts),
+        "tensor",
+    )
+    gate_grad = (
+        jnp.dot(rows_all.T, grad_gate_val, preferred_element_type=f32)
+        .reshape(model_width, local_experts, hidden_units)
+        .transpose(1, 0, 2)
+    )
+    up_grad = (
+        jnp.dot(rows_all.T, grad_up_val, preferred_element_type=f32)
+        .reshape(model_width, local_experts, hidden_units)
+        .transpose(1, 0, 2)
+    )
+    down_term = jnp.dot(inner_low.T, cot_all, preferred_element_type=f32).reshape(
+        local_experts, hidden_units, model_width
+    )
+    grad_logits = combine * (grad_gates - jnp.sum(grad_gates * combine, -1, keepdims=True))
     loss_weight = (experts * share / total_rows)[None, :]
     grad_logits = grad_logits + router_probs * (
         loss_weight - jnp.sum(loss_weight * router_probs, -1, keepdims=True)

time: 2230 us -> 753 us (0.34)
  waiting for transfers between devices: 1620 us -> 391 us
  blocking collectives: 251 us -> 113 us
  local copies, waits for them, and re-layouts: 181 us -> 46.5 us
    reduce_scatter x2 -> x0, waiting for transfers between devices: 822 us -> none  [finish_rows(): lax.psum_scatter(partial_value, 'tensor', scatter_dimension=2, tiled=True)]
    all_gather x2, waiting for transfers between devices: 416 us -> 57.4 us  [the longest x1 33.1 us: shards(): lax.all_gather(cotangent.astype(bf16), 'expert', axis=0, tiled=True)]
    all_to_all x3 -> x0, blocking collectives: 226 us -> none  [the longest x1 143 us: send_owners(): lax.all_to_all(buffer, 'expert', split_axis=0, concat_axis=0, tiled=True)]
    all_to_all x1 -> x4, waiting for transfers between devices: 134 us -> 0.01 us  [the longest x2 0.01 us: collect(): lax.all_to_all(partial_value.astype(bf16).reshape(expert_ranks, tok_rows,...]
    psum x0 -> x2, waiting for transfers between devices: none -> 110 us  [collect(): return lax.psum(jnp.sum(parts.astype(f32), 0), 'tensor')]
    gather x4 -> x0, local copies, waits for them, and re-layouts: 106 us -> none  [the longest x1 34.4 us: shards(): grad_send = grad_ext[owner_of].reshape(experts, CAP, model_width)]
    psum x2, blocking collectives: 25.6 us -> 93.6 us  [shards(): counts_all, prob_all = lax.psum((counts, prob_sums), 'expert')]
    psum x2 -> x1, waiting for transfers between devices: 101 us -> 81.4 us  [head_total(): return lax.psum(partial_value, 'tensor')]
  transfers between devices with their start and end apart: 10 -> 12, of which waited for: 10 -> 8; matrix products, arithmetic and copies ran while one was open for 3% -> 18% of each run, Pallas kernels for 0% -> 0%
where the time goes in v1:
time: 753 us; the launch traced here: 743 us
  waiting for transfers between devices  391 us (52%)
  blocking collectives  113 us (15%)
  matrix products  104 us (14%)
  other arithmetic  53.6 us (7%)
  local copies, waits for them, and re-layouts  46.5 us (6%)
  starting transfers between devices  18.3 us (2%)
  between operations  17.1 us (2%)
    psum x2, waiting for transfers between devices, collect(): return lax.psum(jnp.sum(parts.astype(f32), 0), 'tensor')  110 us
    psum x2, blocking collectives, shards(): counts_all, prob_all = lax.psum((counts, prob_sums), 'expert')  93.6 us
    psum x1, waiting for transfers between devices, head_total(): return lax.psum(partial_value, 'tensor')  81.4 us
    reduce_scatter x1, waiting for transfers between devices, shards(): lax.psum_scatter(all_terms, 'expert', scatter_dimension=0, tiled=True)  62.9 us
    psum x1, waiting for transfers between devices, shards(): lax.psum((attention_gain_grad, query_grad, key_grad, value_grad, out_weig...  53.1 us
    all_gather x1, waiting for transfers between devices, shards(): lax.all_gather(cotangent.astype(bf16), 'expert', axis=0, tiled=True)  33.1 us
    all_gather x1, waiting for transfers between devices, shards(): flat = lax.all_gather(pair_local, 'expert', axis=0, tiled=True)  25.5 us
    all_gather x1, waiting for transfers between devices, shards(): rows_all = lax.all_gather(normed2, 'expert', axis=0, tiled=True)  24.3 us
  transfers between devices with their start and end apart: 12, of which 8 were waited for; matrix products, arithmetic and copies ran while one was open for 18% of the time, Pallas kernels for 0%

profile of v1, /device:TPU:0, one launch (start us, length us, event | category | flops | bytes accessed | tf_op | source)
XLA Modules:
  0.0 743.3 jit_solution(14740698293007910625)
XLA Ops:
  17.8 25.5 %all-gather.4.cloned.1.call-done = bf16[3072,256]{0,1:T(8,128)(2,1)} async-done(((bf16[384,256]{0,1:T(8,128)(2,1)}), bf16[3072,256]{0,1:T(8,128)(2,1)}) %all-gather.4.cloned.1.call-update) | async-done | bytes 1572880 | tf_op jit(solution)/shard_map/all_gather | solution.py:93
  57.3 81.4 %all-reduce.8.cloned.1.call-done = f32[384,1024]{1,0:T(8,128)} async-done(((f32[384,1024]{1,0:T(8,128)}), f32[384,1024]{1,0:T(8,128)}) %all-reduce.8.cloned.1.call-update) | async-done | bytes 1572880 | tf_op jit(solution)/shard_map/psum | solution.py:34
  162.7 24.3 %all-gather.6.cloned.1.call-done = bf16[3072,1024]{1,0:T(8,128)(2,1)} async-done(((bf16[384,1024]{1,0:T(8,128)(2,1)}), bf16[3072,1024]{1,0:T(8,128)(2,1)}) %all-gather.6.cloned.1.call-update) | async-done | bytes 6291472 | tf_op jit(solution)/shard_map/all_gather | solution.py:156
  187.1 9.3 %fusion.69 = f32[3072,512]{0,1:T(8,128)} fusion(bf16[3072,1024]{1,0:T(8,128)(2,1)} %all-gather.6.cloned.1.call-done, bf16[1024,512]{0,1:T(8,128)(2,1)} %bitcast.305), kind=kOutput, calls=%fused_computation.164 | convolution fusion | flops 3221225472 | bytes 13631488 | tf_op jit(solution)/shard_map/dot_general | solution.py:169
  196.4 5.4 fusion.70
  201.9 33.1 %all-gather.8.cloned.1.call-done = bf16[3072,1024]{1,0:T(8,128)(2,1)} async-done(((bf16[384,1024]{1,0:T(8,128)(2,1)}), bf16[3072,1024]{1,0:T(8,128)(2,1)}) %all-gather.8.cloned.1.call-update) | async-done | bytes 6291472 | tf_op jit(solution)/shard_map/all_gather | solution.py:157
  235.0 13.0 %multiply_convert_fusion = (bf16[3072,512]{0,1:T(8,128)(2,1)S(1)}, bf16[3072,512]{0,1:T(8,128)(2,1)S(1)}, bf16[3072,512]{0,1:T(8,128)(2,1)}, f32[3072,512]{0,1:T(8,128)}) fusion(f32[3072,4]{0,1:T(4,128)} %bitcast.16, f32[3072,512]{0,1:T(8,128)} %fusion.69, f32[3072,512]{0,1:T(8,128)} %fusion.70, bf16[3072,1024]{1,0:T(8,128)(2,1)} %all-gather.8.cloned.1.call-done, ...), kind=kOutput, calls=%fused_computation.59 | convolution fusion | flops 3247964160 | bytes 35700736 | tf_op jit(solution)/shard_map/dot_general | solution.py:176
  248.0 6.4 fusion.71
  254.4 8.2 %add_convert_fusion = bf16[3072,1024]{1,0:T(8,128)(2,1)} fusion(f32[3072,1024]{1,0:T(8,128)} %fusion.71, bf16[3072,512]{0,1:T(8,128)(2,1)S(1)} %get-tuple-element.413, bf16[1024,512]{0,1:T(8,128)(2,1)S(1)} %bitcast.304), kind=kOutput, calls=%fused_computation.53 | convolution fusion | flops 3227516928 | bytes 23068672 | tf_op jit(solution)/shard_map/dot_general | solution.py:198
  267.4 78.4 %psum.102 = f32[32]{0:T(128)} all-reduce(f32[32]{0:T(128)} %get-tuple-element.337), channel_id=1, replica_groups=mesh['expert'=8,'tensor'=4] {'expert'}, use_global_device_ids=true, to_apply=%region_21.22 | all-reduce | flops 32 | bytes 256 | tf_op jit(solution)/shard_map/psum | solution.py:150
  349.2 5.5 convert_reduce_fusion
  354.7 8.4 %bitcast_reduce_fusion = f32[3072,4]{0,1:T(4,128)} fusion(f32[3072,512]{0,1:T(8,128)} %get-tuple-element.436, f32[3072,512]{0,1:T(8,128)} %fusion.70, f32[3072,512]{0,1:T(8,128)} %fusion.69), kind=kLoop, calls=%fused_computation.58 | loop fusion | flops 10997760 | bytes 18923520 | tf_op jit(solution)/shard_map/reduce_sum | solution.py:177
  367.1 7.3 convolution_convert_fusion
  380.3 19.5 %psum.101 = f32[384,32]{0,1:T(8,128)S(1)} all-reduce(f32[384,32]{0,1:T(8,128)S(1)} %reshape.457), channel_id=1, replica_groups=mesh['expert'=8,'tensor'=4] {'tensor'}, use_global_device_ids=true, to_apply=%region_16.17 | all-reduce | flops 12288 | bytes 98304 | tf_op jit(solution)/shard_map/psum | solution.py:200
  400.0 24.9 %all-reduce.10.cloned.1.call-done = f32[384,1024]{1,0:T(8,128)} async-done(((f32[384,1024]{1,0:T(8,128)}), f32[384,1024]{1,0:T(8,128)}) %all-reduce.10.cloned.1.call-update) | async-done | bytes 1572880 | tf_op jit(solution)/shard_map/psum | solution.py:192
  434.5 12.6 %while.39 = (s32[]{:T(128)}, f32[2,192,2,2,64]{1,4,3,2,0:T(8,128)}, f32[2,1536,256]{2,1,0:T(8,128)}, s32[]{:T(128)}, bf16[2,1536,256]{1,2,0:T(8,128)(2,1)}, /*in...) while((s32[]{:T(128)}, f32[2,192,2,2,64]{1,4,3,2,0:T(8,128)}, ...), condition=%wide.region_25.26_spmd.clone, body=%wide.region_24.25_spmd.clone.sunk | while | flops 511968960 | bytes 25718508 | solution.py:276
  454.8 5.5 convert_reduce_fusion.1
  462.2 62.9 %reduce-scatter.2.cloned.1.call-done = f32[384,256]{0,1:T(8,128)} async-done(((f32[3072,256]{0,1:T(8,128)}), f32[384,256]{0,1:T(8,128)}) %reduce-scatter.2.cloned.1.call-update) | async-done | bytes 393232 | tf_op jit(solution)/shard_map/reduce_scatter | solution.py:289
  530.3 6.5 fusion.76
  538.6 8.5 %fusion.77 = f32[1024,512]{0,1:T(8,128)} fusion(bf16[3072,512]{0,1:T(8,128)(2,1)} %copy-done.12, bf16[3072,1024]{1,0:T(8,128)(2,1)} %all-gather.6.cloned.1.call-done), kind=kOutput, calls=%fused_computation.172 | convolution fusion | flops 3221225472 | bytes 11534336 | tf_op jit(solution)/shard_map/dot_general | solution.py:216
  557.6 8.6 %fusion.74 = f32[512,1024]{1,0:T(8,128)} fusion(bf16[3072,512]{0,1:T(8,128)(2,1)} %get-tuple-element.415, bf16[3072,1024]{1,0:T(8,128)(2,1)} %all-gather.8.cloned.1.call-done), kind=kOutput, calls=%fused_computation.169 | convolution fusion | flops 3221225472 | bytes 11534336 | tf_op jit(solution)/shard_map/dot_general | solution.py:220
  566.2 85.6 %all-reduce.14.cloned.1.call-done = (f32[384,1024]{1,0:T(8,128)}, f32[384,1024]{1,0:T(8,128)}) async-done(((f32[384,1024]{1,0:T(8,128)}, f32[384,1024]{1,0:T(8,128)}), (f32[384,1024]{1,0:T(8,128)}, f32[384,1024]{1,0:T(8,128)})) %all-reduce.14.cloned.1.call-update) | async-done | bytes 3145744 | tf_op jit(solution)/shard_map/psum | solution.py:192
  655.3 15.2 %all-reduce = (f32[32]{0:T(128)S(1)}, f32[1024]{0:T(1024)}, f32[1024]{0:T(1024)}) all-reduce(f32[32]{0:T(128)S(1)} %copy-done.59, f32[1024]{0:T(1024)S(1)} %get-tuple-element.333, f32[1024]{0:T(1024)S(1)} %get-tuple-element.331), channel_id=1, replica_groups=mesh['expert'=8,'tensor'=4] {'expert'}, use_global_device_ids=true, to_apply=%region_30.31 | all-reduce | flops 2080 | bytes 16640 | tf_op jit(solution)/shard_map/psum | solution.py:150
  675.3 53.1 %all-reduce.12.cloned.1.call-done = (f32[1024,256]{1,0:T(8,128)}, f32[1024,128]{1,0:T(8,128)}, f32[1024,128]{1,0:T(8,128)}, f32[256,1024]{1,0:T(8,128)}, f32[1024,32]{0,1:T(8,128)}) async-done(((f32[1024,256]{1,0:T(8,128)}, f32[1024,128]{1,0:T(8,128)}, f32[1024,128]{1,0:T(8,128)}, f32[256,1024]{1,0:T(8,128)}, f32[1024,32]{0,1:T(8,128)}), (f32[1024,256]{1,0:T(8,128)}, f32[1024,128]{1,0:T(8,128)}, ...) | async-done | bytes 3276816 | tf_op jit(solution)/shard_map/psum | solution.py:327
  (280 shorter events, 135.6 us)
Async XLA Ops:
  7.2 227.8 %copy-start = (bf16[4,128,1024]{2,1,0:T(8,128)(2,1)S(1)}, bf16[4,128,1024]{2,1,0:T(8,128)(2,1)}, u32[]{:S(2)}) copy-start(bf16[4,128,1024]{2,1,0:T(8,128)(2,1)} %param.30) | copy-start | bytes 3145732
  7.2 36.1 %all-gather.4.cloned.1.call-start = ((), (), s32[]{:S(2)}) async-start(), calls=%async_computation.5 | async-start | bytes 1769472 | tf_op jit(solution)/shard_map/all_gather | solution.py:93
  14.6 124.1 %all-reduce.8.cloned.1.call-start = ((), (), s32[]{:S(2)}) async-start(), calls=%async_computation.6 | async-start | bytes 3145728 | tf_op jit(solution)/shard_map/psum | solution.py:34
  55.1 85.4 %copy-start.39 = (s32[2]{0:T(128)}, s32[2]{0:T(128)S(1)}, u32[]{:S(2)}) copy-start(s32[2]{0:T(128)S(1)} %get-tuple-element.827) | copy-start | bytes 28
  57.2 84.0 %copy-start.43 = (f32[1024]{0:T(1024)S(1)}, f32[1024]{0:T(1024)}, u32[]{:S(2)}) copy-start(f32[1024]{0:T(1024)} %param.26) | copy-start | bytes 12292
  57.2 129.9 %all-gather.6.cloned.1.call-start = ((), (), s32[]{:S(2)}) async-start(), calls=%async_computation.7 | async-start | bytes 7077888 | tf_op jit(solution)/shard_map/all_gather | solution.py:156
  140.5 286.4 %copy-start.2 = (f32[384,1024]{1,0:T(8,128)}, f32[384,1024]{1,0:T(8,128)S(1)}, u32[]{:S(2)}) copy-start(f32[384,1024]{1,0:T(8,128)S(1)} %get-tuple-element.406) | copy-start | bytes 4718596
  142.4 92.6 %all-gather.8.cloned.1.call-start = ((), (), s32[]{:S(2)}) async-start(), calls=%async_computation.8 | async-start | bytes 7077888 | tf_op jit(solution)/shard_map/all_gather | solution.py:157
  158.6 43.3 %all-to-all-start = ((f32[384,8,4]{0,2,1:T(4,128)}), f32[384,8,4]{0,2,1:T(4,128)}, u32[]{:S(2)}, u32[]{:S(2)}) async-start(f32[384,8,4]{0,2,1:T(4,128)} %reshape.449), calls=%async_computation | async-start | bytes 98304 | tf_op jit(solution)/shard_map/all_to_all | solution.py:158
  262.5 86.6 %all-to-all-start.2 = ((bf16[8,384,1024]{2,1,0:T(8,128)(2,1)}), bf16[8,384,1024]{2,1,0:T(8,128)(2,1)}, u32[]{:S(2)}, u32[]{:S(2)}) async-start(bf16[8,384,1024]{2,1,0:T(8,128)(2,1)} %bitcast.295), calls=%async_computation.2 | async-start | bytes 12582912 | tf_op jit(solution)/shard_map/all_to_all | solution.py:185
  267.3 157.5 %all-reduce.10.cloned.1.call-start = ((), (), s32[]{:S(2)}) async-start(), calls=%async_computation.9 | async-start | bytes 3145728 | tf_op jit(solution)/shard_map/psum | solution.py:192
  363.1 11.3 %all-to-all-start.3 = ((f32[8,384,4]{1,2,0:T(4,128)}), f32[8,384,4]{1,2,0:T(4,128)}, u32[]{:S(2)}, u32[]{:S(2)}) async-start(f32[8,384,4]{1,2,0:T(4,128)} %bitcast.309), calls=%async_computation.3 | async-start | bytes 98304 | tf_op jit(solution)/shard_map/all_to_all | solution.py:201
  374.5 50.4 %copy-start.33 = (bf16[1024,32]{0,1:T(8,128)(2,1)S(1)}, bf16[1024,32]{0,1:T(8,128)(2,1)}, u32[]{:S(2)}) copy-start(bf16[1024,32]{0,1:T(8,128)(2,1)} %param.27) | copy-start | bytes 196612
  374.5 50.4 %copy-start.44 = (f32[1024]{0:T(1024)S(1)}, f32[1024]{0:T(1024)}, u32[]{:S(2)}) copy-start(f32[1024]{0:T(1024)} %param.26) | copy-start | bytes 12292
  374.5 50.4 %copy-start.49 = (f32[384]{0:T(512)S(1)}, f32[384]{0:T(512)}, u32[]{:S(2)}) copy-start(f32[384]{0:T(512)} %copy-done.48) | copy-start | bytes 4612
  374.5 80.3 %all-to-all-start.1 = ((bf16[8,384,1024]{2,1,0:T(8,128)(2,1)}), bf16[8,384,1024]{2,1,0:T(8,128)(2,1)}, u32[]{:S(2)}, u32[]{:S(2)}) async-start(bf16[8,384,1024]{2,1,0:T(8,128)(2,1)} %bitcast.294), calls=%async_computation.1 | async-start | bytes 12582912 | tf_op jit(solution)/shard_map/all_to_all | solution.py:185
  379.4 47.5 %copy-start.54 = (f32[384]{0:T(512)S(1)}, f32[384]{0:T(512)}, u32[]{:S(2)}) copy-start(f32[384]{0:T(512)} %get-tuple-element.432) | copy-start | bytes 4612
  379.5 145.7 %reduce-scatter.2.cloned.1.call-start = ((), (), s32[]{:S(2)}) async-start(), calls=%async_computation.10 | async-start | bytes 3538944 | tf_op jit(solution)/shard_map/reduce_scatter | solution.py:289
  400.0 27.0 %copy-start.35 = (bf16[384,32]{0,1:T(8,128)(2,1)}, bf16[384,32]{0,1:T(8,128)(2,1)S(1)}, u32[]{:S(2)}) copy-start(bf16[384,32]{0,1:T(8,128)(2,1)S(1)} %add_convert_fusion.1) | copy-start | bytes 73732
  454.6 197.2 %all-reduce.14.cloned.1.call-start = ((), (), s32[]{:S(2)}) async-start(), calls=%async_computation.12 | async-start | bytes 6291456 | tf_op jit(solution)/shard_map/psum | solution.py:192
  461.5 64.6 %copy-start.24 = (f32[384,64]{0,1:T(8,128)S(1)}, f32[384,64]{0,1:T(8,128)}, u32[]{:S(2)}) copy-start(f32[384,64]{0,1:T(8,128)} %copy-done.23) | copy-start | bytes 294916
  462.2 66.4 %copy-start.34 = (bf16[1024,128]{1,0:T(8,128)(2,1)S(1)}, bf16[1024,128]{1,0:T(8,128)(2,1)}, u32[]{:S(2)}) copy-start(bf16[1024,128]{1,0:T(8,128)(2,1)} %param.24) | copy-start | bytes 786436
  530.3 198.1 %all-reduce.12.cloned.1.call-start = ((), (), s32[]{:S(2)}) async-start(), calls=%async_computation.11 | async-start | bytes 6553600 | tf_op jit(solution)/shard_map/psum | solution.py:327
  557.6 94.2 %copy-start.3 = (f32[384,1024]{1,0:T(8,128)S(1)}, f32[384,1024]{1,0:T(8,128)}, u32[]{:S(2)}) copy-start(f32[384,1024]{1,0:T(8,128)} %copy-done.2) | copy-start | bytes 4718596
  (50 other events, 370.6 us)
Sparse Core Ops, SparseCore 0:
  14.7 28.5 all-gather.3
  57.3 81.2 all-reduce.7
  142.5 44.5 all-gather.5
  189.4 45.5 all-gather.7
  354.8 69.9 all-reduce.9
  454.7 70.4 reduce-scatter.1
  530.4 121.3 all-reduce.13
  657.3 70.9 all-reduce.11

commit v2 on v1

--- a/solution.py
+++ b/solution.py
@@ -1,14 +1,459 @@
+import functools
 import math
 
 import jax
 import jax.numpy as jnp
 from jax import lax
+from jax.experimental import pallas as pl
+from jax.experimental.pallas import tpu as pltpu
 from jax.sharding import PartitionSpec as P
 
 HD = 64
-
 EPS = 1e-06
 THETA = 10000.0
+MESH = pl.DeviceIdType.MESH
+f32 = jnp.float32
+bf16 = jnp.bfloat16
+
+
+def dot_nn(left, right):
+    return lax.dot_general(left, right, (((1,), (0,)), ((), ())), preferred_element_type=f32)
+
+
+def dot_nt(left, right):
+    return lax.dot_general(left, right, (((1,), (1,)), ((), ())), preferred_element_type=f32)
+
+
+def dot_tn(left, right):
+    return lax.dot_general(left, right, (((0,), (0,)), ((), ())), preferred_element_type=f32)
+
+
+def remote(src, dst, send_sem, recv_sem, device):
+    return pltpu.make_async_remote_copy(
+        src_ref=src,
+        dst_ref=dst,
+        send_sem=send_sem,
+        recv_sem=recv_sem,
+        device_id=device,
+        device_id_type=MESH,
+    )
+
+
+def expert_kernel(
+    n,
+    nz,
+    big,
+    mid_ref,
+    gain_ref,
+    router_ref,
+    routes_ref,
+    gate_ref,
+    up_ref,
+    down_ref,
+    cot_ref,
+    cot_all,
+    *rest,
+):
+    outs, rest = rest[:8], rest[8:]
+    out_ref, gmid_ref, rgrad_ref, ggrad_ref, load_ref, dgate, dup, ddown = outs
+    if big:
+        xbuf, rest = rest[0], rest[1:]
+        xstage, rest = rest[0], rest[1:]
+    else:
+        xbuf, rest = rest[0], rest[1:]
+        xstage = None
+    (
+        wbuf,
+        xn_s,
+        wg,
+        wu,
+        cbuf,
+        dg_s,
+        du_s,
+        wi_s,
+        hold,
+        osend,
+        sin,
+        fbuf,
+        fin,
+        acc,
+        zsend,
+        zin,
+        zs,
+        zr,
+        zws,
+        zwr,
+        xs,
+        xr,
+        ws,
+        wr,
+        fs,
+        fr,
+        wfs,
+        wfr,
+        csem,
+        os_,
+        or_,
+        fsem,
+        frem,
+        zgs,
+        zgr,
+        lsem,
+    ) = rest
+    e = lax.axis_index("expert")
+    z = lax.axis_index("tensor")
+    sib = e + 1 - 2 * lax.rem(e, 2)
+    half = n // 2
+    rows, width = mid_ref.shape
+    tok = rows * nz
+    experts = router_ref.shape[1]
+    local_experts, _, hid = gate_ref.shape
+    inner_w = local_experts * hid
+    fc = min(inner_w, 256)
+    slots = fbuf.shape[0]
+
+    barrier = pltpu.get_barrier_semaphore()
+    pl.semaphore_signal(barrier, inc=1, device_id=(sib, z), device_id_type=MESH)
+    for s in range(1, half):
+        pl.semaphore_signal(
+            barrier, inc=1, device_id=(lax.rem(e + 2 * s, n), z), device_id_type=MESH
+        )
+    for k in range(1, nz):
+        pl.semaphore_signal(barrier, inc=1, device_id=(e, lax.rem(z + k, nz)), device_id_type=MESH)
+
+    own_rows = pl.ds(pl.multiple_of(z * rows, 16), rows)
+    mid = mid_ref[...]
+    scale2 = lax.rsqrt(jnp.mean(mid * mid, -1, keepdims=True) + EPS)
+    xn = (mid * scale2 * gain_ref[...]).astype(bf16)
+    xn_s[...] = xn
+    logits = dot_nn(xn, router_ref[...])
+    picks = routes_ref[own_rows, :]
+    lanes = lax.broadcasted_iota(jnp.int32, (rows, experts), 1)
+    chosen = jnp.zeros((rows, experts), f32)
+    for k in range(picks.shape[1]):
+        chosen = jnp.where(picks[:, k : k + 1] == lanes, 1.0, chosen)
+    top = jnp.max(logits, -1, keepdims=True)
+    powers = jnp.exp(logits - top)
+    probs = powers / jnp.sum(powers, -1, keepdims=True)
+    low_logits = jnp.where(chosen > 0.0, logits, -1e30)
+    ctop = jnp.max(low_logits, -1, keepdims=True)
+    cpow = jnp.exp(low_logits - ctop)
+    comb = cpow / jnp.sum(cpow, -1, keepdims=True)
+    padded = jnp.concatenate([comb, jnp.zeros((rows, 128 - experts), f32)], 1)
+    if rows < 128:
+        padded = jnp.concatenate([padded, jnp.zeros((128 - rows, 128), f32)], 0)
+    piece = padded.T[:experts]
+    lane_pad = jnp.zeros((1, 128 - experts), f32)
+    cnt = jnp.concatenate([jnp.sum(chosen, 0, keepdims=True), lane_pad], 1)
+    psum = jnp.concatenate([jnp.sum(probs, 0, keepdims=True), lane_pad], 1)
+    psum_hi = psum.astype(bf16).astype(f32)
+    stats = jnp.concatenate([cnt, psum_hi, psum - psum_hi, jnp.zeros((13, 128), f32)], 0)
+    wbuf[e, z] = jnp.concatenate([piece, stats], 0).astype(bf16)
+    if big:
+        copy = pltpu.make_async_copy(xn_s, xbuf.at[e, own_rows], lsem)
+        copy.start()
+        copy.wait()
+    else:
+        xbuf[e, own_rows] = xn
+    pl.semaphore_wait(barrier, half + nz - 1)
+
+    for k in range(1, nz):
+        to = (e, lax.rem(z + k, nz))
+        piece_ref = xbuf.at[e, own_rows]
+        remote(piece_ref, piece_ref, zs.at[k - 1], zr.at[k - 1], to).start()
+        remote(wbuf.at[e, z], wbuf.at[e, z], zws.at[k - 1], zwr.at[k - 1], to).start()
+
+    def push_piece(zz):
+        piece_ref = xbuf.at[e, pl.ds(pl.multiple_of(zz * rows, 16), rows)]
+        small = wbuf.at[e, zz]
+        for s in range(1, half):
+            to = (lax.rem(e + 2 * s, n), z)
+            remote(piece_ref, piece_ref, xs.at[s], xr.at[s], to).start()
+            remote(small, small, ws.at[s], wr.at[s], to).start()
+        remote(piece_ref, piece_ref, fs.at[0], fr.at[0], (sib, z)).start()
+        remote(small, small, wfs.at[0], wfr.at[0], (sib, z)).start()
+
+    push_piece(z)
+
+    def cot_copy(index, slot):
+        start = pl.ds(pl.multiple_of(index * tok, 16), tok)
+        return pltpu.make_async_copy(cot_all.at[start], cbuf.at[slot], csem.at[slot])
+
+    cot_copy(e, 0).start()
+    for el in range(local_experts):
+        cols = slice(el * hid, (el + 1) * hid)
+        wg[:, cols] = gate_ref[el]
+        wu[:, cols] = up_ref[el]
+    dgate[...] = jnp.zeros_like(dgate)
+    dup[...] = jnp.zeros_like(dup)
+    ddown[...] = jnp.zeros_like(ddown)
+
+    for k in range(1, nz):
+        zz = lax.rem(z + nz - k, nz)
+        piece_ref = xbuf.at[e, pl.ds(pl.multiple_of(zz * rows, 16), rows)]
+        peer = (e, zz)
+        remote(piece_ref, piece_ref, zs.at[k - 1], zr.at[k - 1], peer).wait_recv()
+        remote(wbuf.at[e, zz], wbuf.at[e, zz], zws.at[k - 1], zwr.at[k - 1], peer).wait_recv()
+        push_piece(zz)
+
+    sel_row = lax.broadcasted_iota(jnp.int32, (experts, fc), 0)
+    sel_col = lax.broadcasted_iota(jnp.int32, (experts, fc), 1)
+
+    def block(index, slot, dst, dslot):
+        if big:
+            copy = pltpu.make_async_copy(xbuf.at[index], xstage, lsem)
+            copy.start()
+            copy.wait()
+            x_ref = xstage
+        else:
+            x_ref = xbuf.at[index]
+        c_ref = cbuf.at[slot]
+        sums = [jnp.zeros((experts, rows), f32) for _ in range(nz)]
+        for q in range(inner_w // fc):
+            cols = slice(q * fc, (q + 1) * fc)
+            x = x_ref[...]
+            gate_val = dot_nn(x, wg[:, cols])
+            up_val = dot_nn(x, wu[:, cols])
+            back = dot_nt(c_ref[...], down_ref[cols, :])
+            select = jnp.where(
+                sel_row == e * local_experts + (q * fc + sel_col) // hid, 1.0, 0.0
+            ).astype(bf16)
+            wide = jnp.concatenate(
+                [dot_tn(wbuf[index, zz, :experts, :], select)[:rows] for zz in range(nz)], 0
+            )
+            sig = 1.0 / (1.0 + jnp.exp(-gate_val))
+            silu = gate_val * sig
+            inner = silu * up_val
+            wi_s[:, cols] = (inner * wide).astype(bf16)
+            scaled = back * wide
+            dg_s[:, cols] = (scaled * up_val * (sig * (1.0 + gate_val * (1.0 - sig)))).astype(bf16)
+            du_s[:, cols] = (scaled * silu).astype(bf16)
+            both = (inner * back).astype(bf16)
+            for zz in range(nz):
+                sums[zz] = sums[zz] + dot_nt(select, both[zz * rows : (zz + 1) * rows])
+        for zz in range(nz):
+            gap = jnp.zeros((experts, 128 - rows), f32)
+            dst[dslot, tok : tok + experts, zz * 128 : (zz + 1) * 128] = jnp.concatenate(
+                [sums[zz], gap], 1
+            ).astype(bf16)
+        for h in range(width // 256):
+            cols = slice(h * 256, (h + 1) * 256)
+            dst[dslot, 0:tok, cols] = (
+                dot_nt(dg_s[...], wg[cols, :]) + dot_nt(du_s[...], wu[cols, :])
+            ).astype(bf16)
+            dst[dslot, tok + experts :, cols] = dot_nn(wi_s[...], down_ref[:, cols]).astype(bf16)
+        for h in range(width // 256):
+            cols = slice(h * 256, (h + 1) * 256)
+            x_part = x_ref[:, cols]
+            gate_part = dot_tn(x_part, dg_s[...])
+            up_part = dot_tn(x_part, du_s[...])
+            for el in range(local_experts):
+                dgate[el, cols, :] += gate_part[:, el * hid : (el + 1) * hid]
+                dup[el, cols, :] += up_part[:, el * hid : (el + 1) * hid]
+            ddown[:, cols] += dot_tn(wi_s[...], c_ref[:, cols])
+
+    def finish(s):
+        slot = lax.rem(s, 2)
+        remote(osend.at[slot], sin.at[slot], os_.at[slot], or_.at[slot], (sib, z)).wait_recv()
+
+        @pl.when(s == 0)
+        def _():
+            acc[...] = hold[slot].astype(f32) + sin[slot].astype(f32)
+
+        @pl.when(s > 0)
+        def _():
+            fslot = lax.rem(s - 1, slots)
+            to = (lax.rem(e - 2 * s + n, n), z)
+            out = remote(fbuf.at[fslot], fin.at[s - 1], fsem.at[fslot], frem.at[s - 1], to)
+            if half - 1 > slots:
+
+                @pl.when(s - 1 >= slots)
+                def _():
+                    out.wait_send()
+
+            fbuf[fslot] = (hold[slot].astype(f32) + sin[slot].astype(f32)).astype(bf16)
+            out.start()
+
+    def step(s, carry):
+        own = lax.rem(e - 2 * s + n, n)
+        oth = lax.rem(sib - 2 * s + n, n)
+        slot = lax.rem(s, 2)
+
+        @pl.when(s > 0)
+        def _():
+            remote(xbuf.at[own], xbuf.at[own], xs.at[s], xr.at[s], (own, z)).wait_recv()
+            remote(wbuf.at[own], wbuf.at[own], ws.at[s], wr.at[s], (own, z)).wait_recv()
+            remote(xbuf.at[own], xbuf.at[own], fs.at[s], fr.at[s], (sib, z)).start()
+            remote(wbuf.at[own], wbuf.at[own], wfs.at[s], wfr.at[s], (sib, z)).start()
+
+        cot_copy(oth, 1).start()
+        cot_copy(own, 0).wait()
+        block(own, 0, hold, slot)
+
+        @pl.when(s < half - 1)
+        def _():
+            cot_copy(lax.rem(e - 2 * s - 2 + n, n), 0).start()
+
+        @pl.when(s > 0)
+        def _():
+            finish(s - 1)
+
+        remote(xbuf.at[oth], xbuf.at[oth], fs.at[s], fr.at[s], (sib, z)).wait_recv()
+        remote(wbuf.at[oth], wbuf.at[oth], wfs.at[s], wfr.at[s], (sib, z)).wait_recv()
+        cot_copy(oth, 1).wait()
+        give = remote(osend.at[slot], sin.at[slot], os_.at[slot], or_.at[slot], (sib, z))
+
+        @pl.when(s >= 2)
+        def _():
+            give.wait_send()
+
+        block(oth, 1, osend, slot)
+        give.start()
+        return carry
+
+    lax.fori_loop(0, half, step, 0)
+    finish(jnp.int32(half - 1))
+
+    def total_stats(j, carry):
+        for zz in range(nz):
+            carry = carry + wbuf[j, zz, experts:, :].astype(f32)
+        return carry
+
+    stats = lax.fori_loop(0, n, total_stats, jnp.zeros((16, 128), f32))
+    for s in range(1, half):
+        src = lax.rem(e + 2 * s, n)
+        fslot = (s - 1) % slots
+        remote(fbuf.at[fslot], fin.at[s - 1], fsem.at[fslot], frem.at[s - 1], (src, z)).wait_recv()
+        acc[...] += fin[s - 1].astype(f32)
+
+    def take(zz):
+        part = pl.ds(pl.multiple_of(zz * rows, 16), rows)
+        lane = pl.ds(pl.multiple_of(zz * 128, 128), 128)
+        low = pl.ds(pl.multiple_of(tok + experts + zz * rows, 16), rows)
+        return acc[part, :], acc[tok : tok + experts, lane], acc[low, :]
+
+    for k in range(1, nz):
+        zz = lax.rem(z + k, nz)
+        first, second, third = take(zz)
+        zsend[k - 1, 0:rows, :] = first.astype(bf16)
+        zsend[k - 1, rows : rows + experts, 0:128] = second.astype(bf16)
+        zsend[k - 1, rows + experts :, :] = third.astype(bf16)
+        remote(zsend.at[k - 1], zin.at[k - 1], zgs.at[k - 1], zgr.at[k - 1], (e, zz)).start()
+
+    grad_rows, gate_sums, mixed = take(z)
+    for k in range(1, nz):
+        remote(zsend.at[k - 1], zin.at[k - 1], zgs.at[k - 1], zgr.at[k - 1], (e, z)).wait_recv()
+        grad_rows = grad_rows + zin[k - 1, 0:rows, :].astype(f32)
+        gate_sums = gate_sums + zin[k - 1, rows : rows + experts, 0:128].astype(f32)
+        mixed = mixed + zin[k - 1, rows + experts :, :].astype(f32)
+
+    out_ref[...] = mid_ref[...] + mixed
+    total_rows = n * tok
+    share = stats[0:1, :experts] / (total_rows * routes_ref.shape[1])
+    load_ref[...] = experts * experts * share * ((stats[1:2, :experts] + stats[2:3, :experts]) / total_rows)
+    loss_w = experts * share / total_rows
+    grow = jnp.concatenate([gate_sums, jnp.zeros((128 - experts, 128), f32)], 0).T
+    grad_gates = grow[:rows, :experts]
+    grad_logits = comb * (grad_gates - jnp.sum(grad_gates * comb, -1, keepdims=True))
+    grad_logits = grad_logits + probs * (loss_w - jnp.sum(loss_w * probs, -1, keepdims=True))
+    low_grad = grad_logits.astype(bf16)
+    rgrad_ref[...] = dot_tn(low_grad, xn_s[...])
+    grad_rows = grad_rows + dot_nt(low_grad, router_ref[...])
+    mid = mid_ref[...]
+    ggrad_ref[...] = jnp.sum(grad_rows * mid * scale2, 0, keepdims=True)
+    gained = grad_rows * gain_ref[...]
+    gmid_ref[...] = (
+        cot_ref[own_rows, :]
+        + scale2 * gained
+        - mid * (scale2 * scale2 * scale2) * jnp.mean(gained * mid, -1, keepdims=True)
+    )
+
+    for k in range(1, nz):
+        piece_ref = xbuf.at[e, own_rows]
+        peer = (e, lax.rem(z + k, nz))
+        remote(piece_ref, piece_ref, zs.at[k - 1], zr.at[k - 1], peer).wait_send()
+        remote(wbuf.at[e, z], wbuf.at[e, z], zws.at[k - 1], zwr.at[k - 1], peer).wait_send()
+        remote(zsend.at[k - 1], zin.at[k - 1], zgs.at[k - 1], zgr.at[k - 1], peer).wait_send()
+    for s in range(half):
+        peer = (lax.rem(e + 2 * s, n), z) if s else (sib, z)
+        if s:
+            remote(xbuf.at[e], xbuf.at[e], xs.at[s], xr.at[s], peer).wait_send()
+            remote(wbuf.at[e], wbuf.at[e], ws.at[s], wr.at[s], peer).wait_send()
+        remote(xbuf.at[e], xbuf.at[e], fs.at[s], fr.at[s], (sib, z)).wait_send()
+        remote(wbuf.at[e], wbuf.at[e], wfs.at[s], wfr.at[s], (sib, z)).wait_send()
+    for s in range(max(0, half - 2), half):
+        slot = s % 2
+        remote(osend.at[slot], sin.at[slot], os_.at[slot], or_.at[slot], (sib, z)).wait_send()
+    for s in range(max(1, half - slots), half):
+        fslot = (s - 1) % slots
+        remote(fbuf.at[fslot], fin.at[s - 1], fsem.at[fslot], frem.at[s - 1], (sib, z)).wait_send()
+
+
+def expert_layer(n, nz, mid, gain, router, routes, gate, up, down, cot, cot_all):
+    rows, width = mid.shape
+    tok = rows * nz
+    experts = router.shape[1]
+    local_experts, _, hid = gate.shape
+    inner_w = local_experts * hid
+    half = n // 2
+    big = n > 8
+    slots = min(half - 1, 3)
+    pay = 2 * tok + experts
+    dma = pltpu.SemaphoreType.DMA
+    vmem = pl.BlockSpec(memory_space=pltpu.VMEM)
+    hbm = pl.BlockSpec(memory_space=pl.ANY)
+    sds = jax.ShapeDtypeStruct
+    out_shape = [
+        sds((rows, width), f32),
+        sds((rows, width), f32),
+        sds((experts, width), f32),
+        sds((1, width), f32),
+        sds((1, experts), f32),
+        sds((local_experts, width, hid), f32),
+        sds((local_experts, width, hid), f32),
+        sds((inner_w, width), f32),
+    ]
+    out_specs = [vmem] * 8
+    scratch = []
+    if big:
+        out_shape.append(sds((n, tok, width), bf16))
+        out_specs.append(hbm)
+        scratch.append(pltpu.VMEM((tok, width), bf16))
+    else:
+        scratch.append(pltpu.VMEM((n, tok, width), bf16))
+    scratch += [
+        pltpu.VMEM((n, nz, experts + 16, 128), bf16),
+        pltpu.VMEM((rows, width), bf16),
+        pltpu.VMEM((width, inner_w), bf16),
+        pltpu.VMEM((width, inner_w), bf16),
+        pltpu.VMEM((2, tok, width), bf16),
+        pltpu.VMEM((tok, inner_w), bf16),
+        pltpu.VMEM((tok, inner_w), bf16),
+        pltpu.VMEM((tok, inner_w), bf16),
+        pltpu.VMEM((2, pay, width), bf16),
+        pltpu.VMEM((2, pay, width), bf16),
+        pltpu.VMEM((2, pay, width), bf16),
+        pltpu.VMEM((slots, pay, width), bf16),
+        pltpu.VMEM((half - 1, pay, width), bf16),
+        pltpu.VMEM((pay, width), f32),
+        pltpu.VMEM((nz - 1, 2 * rows + experts, width), bf16),
+        pltpu.VMEM((nz - 1, 2 * rows + experts, width), bf16),
+    ]
+    scratch += [dma((nz - 1,))] * 4
+    scratch += [dma((half,))] * 8
+    scratch += [dma((2,))] * 3
+    scratch += [dma((slots,)), dma((half - 1,)), dma((nz - 1,)), dma((nz - 1,)), dma]
+    return pl.pallas_call(
+        functools.partial(expert_kernel, n, nz, big),
+        out_shape=out_shape,
+        in_specs=[vmem] * 8 + [hbm],
+        out_specs=out_specs,
+        scratch_shapes=scratch,
+        compiler_params=pltpu.CompilerParams(
+            collective_id=1, has_side_effects=True, vmem_limit_bytes=62 << 20
+        ),
+        name="experts",
+    )(mid, gain[None], router, routes, gate, up, down.reshape(inner_w, width), cot, cot_all)[:8]
 
 
 def rope_tables(positions, head_size):
@@ -28,10 +473,6 @@
     scaled = values * sine_table[:, None, :]
     turned = jnp.concatenate([scaled[..., half_size:], -scaled[..., :half_size]], -1)
     return values * cosines[:, None, :] + turned
-
-
-def head_total(partial_value):
-    return lax.psum(partial_value, "tensor")
 
 
 def shards(
@@ -50,8 +491,6 @@
     seq_lens,
     cotangent,
 ):
-    f32 = jnp.float32
-    bf16 = jnp.bfloat16
     tok_rows, model_width = inputs.shape
     expert_ranks = lax.axis_size("expert")
     expert_rank = lax.axis_index("expert")
@@ -64,10 +503,6 @@
     query_heads = query_width // HD
     key_heads = key_width // HD
     groups = query_heads // key_heads
-    experts = router_weight.shape[1]
-    chosen_count = routes.shape[1]
-    local_experts = gate_weight.shape[0]
-    hidden_units = gate_weight.shape[2]
     score_scale = HD ** (-0.5)
     local_pos = expert_rank * span_rows + jnp.arange(span_rows, dtype=jnp.int32)
     row_pos = jnp.tile(local_pos, seq_count)
@@ -137,107 +572,47 @@
         0, used_blocks, value_sums, jnp.zeros((seq_count, key_heads, groups, span_rows, HD), f32)
     )
     attended = attended_raw.transpose(0, 3, 1, 2, 4).reshape(tok_rows, query_width).astype(bf16)
-    middle = residual + head_total(jnp.dot(attended, out_weight, preferred_element_type=f32))
-    norm_scale2 = lax.rsqrt(jnp.mean(middle * middle, -1, keepdims=True) + EPS)
-    normed2 = (middle * norm_scale2 * expert_gain).astype(bf16)
-    logits = jnp.dot(normed2, router_weight, preferred_element_type=f32)
-    router_probs = jax.nn.softmax(logits, -1)
-    onehot = (routes[:, :, None] == jnp.arange(experts, dtype=jnp.int32)[None, None, :]).astype(f32)
-    chosen = jnp.einsum("tke,te->tk", onehot, logits)
-    gates = jax.nn.softmax(chosen, -1)
-    counts = jnp.sum(onehot, (0, 1))
-    prob_sums = jnp.sum(router_probs, 0)
-    counts_all, prob_all = lax.psum((counts, prob_sums), "expert")
-    share = counts_all / (total_rows * chosen_count)
-    expert_load = experts * experts * share * (prob_all / total_rows)
+    tensor_ranks = lax.axis_size("tensor")
+    tensor_rank = lax.axis_index("tensor")
+    own_count = tok_rows // tensor_ranks
+
+    def own_part(values):
+        return lax.dynamic_slice_in_dim(values, tensor_rank * own_count, own_count, 0)
+
+    cot_all = lax.all_gather(cotangent.astype(bf16), "expert", axis=0, tiled=True)
+    middle = own_part(residual) + lax.psum_scatter(
+        jnp.dot(attended, out_weight, preferred_element_type=f32),
+        "tensor",
+        scatter_dimension=0,
+        tiled=True,
+    )
+    (
+        out_part,
+        grad_middle,
+        router_part,
+        expert_gain_part,
+        expert_load,
+        gate_grad,
+        up_grad,
+        down_term,
+    ) = expert_layer(
+        expert_ranks,
+        tensor_ranks,
+        middle,
+        expert_gain,
+        router_weight,
+        routes,
+        gate_weight,
+        up_weight,
+        down_weight,
+        cotangent,
+        cot_all,
+    )
+    expert_load = expert_load[0]
     balance_loss = jnp.mean(expert_load)
-    combine = jnp.einsum("tke,tk->te", onehot, gates)
-
-    rows_all = lax.all_gather(normed2, "expert", axis=0, tiled=True)
-    cot_all = lax.all_gather(cotangent.astype(bf16), "expert", axis=0, tiled=True)
-    combine_own = lax.all_to_all(
-        combine.reshape(tok_rows, expert_ranks, local_experts),
-        "expert",
-        split_axis=1,
-        concat_axis=0,
-        tiled=True,
-    ).reshape(total_rows, local_experts)
-    width = local_experts * hidden_units
-    gate_flat = gate_weight.transpose(1, 0, 2).reshape(model_width, width)
-    up_flat = up_weight.transpose(1, 0, 2).reshape(model_width, width)
-    down_flat = down_weight.reshape(width, model_width)
-    gate_val = jnp.dot(rows_all, gate_flat, preferred_element_type=f32)
-    up_val = jnp.dot(rows_all, up_flat, preferred_element_type=f32)
-    sigmoid_gate = jax.nn.sigmoid(gate_val)
-    silu_gate = gate_val * sigmoid_gate
-    inner = silu_gate * up_val
-    weight_wide = jnp.repeat(combine_own, hidden_units, axis=1)
-    inner_low = (inner * weight_wide).astype(bf16)
-    cot_down = jnp.dot(cot_all, down_flat.T, preferred_element_type=f32)
-    gate_sums = jnp.sum((inner * cot_down).reshape(total_rows, local_experts, hidden_units), -1)
-    grad_inner = cot_down * weight_wide
-    grad_gate_val = (
-        grad_inner * up_val * sigmoid_gate * (1.0 + gate_val * (1.0 - sigmoid_gate))
-    ).astype(bf16)
-    grad_up_val = (grad_inner * silu_gate).astype(bf16)
-
-    def collect(partial_value):
-        parts = lax.all_to_all(
-            partial_value.astype(bf16).reshape(expert_ranks, tok_rows, model_width),
-            "expert",
-            split_axis=0,
-            concat_axis=0,
-            tiled=True,
-        )
-        return lax.psum(jnp.sum(parts.astype(f32), 0), "tensor")
-
-    mixed = collect(jnp.dot(inner_low, down_flat, preferred_element_type=f32))
-    output = middle + mixed
-    grad_normed2 = collect(
-        jnp.dot(grad_gate_val, gate_flat.T, preferred_element_type=f32)
-        + jnp.dot(grad_up_val, up_flat.T, preferred_element_type=f32)
-    )
-    grad_gates = lax.psum(
-        lax.all_to_all(
-            gate_sums.reshape(expert_ranks, tok_rows, local_experts),
-            "expert",
-            split_axis=0,
-            concat_axis=2,
-            tiled=True,
-        ).reshape(tok_rows, experts),
-        "tensor",
-    )
-    gate_grad = (
-        jnp.dot(rows_all.T, grad_gate_val, preferred_element_type=f32)
-        .reshape(model_width, local_experts, hidden_units)
-        .transpose(1, 0, 2)
-    )
-    up_grad = (
-        jnp.dot(rows_all.T, grad_up_val, preferred_element_type=f32)
-        .reshape(model_width, local_experts, hidden_units)
-        .transpose(1, 0, 2)
-    )
-    down_term = jnp.dot(inner_low.T, cot_all, preferred_element_type=f32).reshape(
-        local_experts, hidden_units, model_width
-    )
-    grad_logits = combine * (grad_gates - jnp.sum(grad_gates * combine, -1, keepdims=True))
-    loss_weight = (experts * share / total_rows)[None, :]
-    grad_logits = grad_logits + router_probs * (
-        loss_weight - jnp.sum(loss_weight * router_probs, -1, keepdims=True)
-    )
-    grad_logit_low = grad_logits.astype(bf16)
-    router_grad = jnp.dot(normed2.T, grad_logit_low, preferred_element_type=f32)
-    grad_normed2 = grad_normed2 + jnp.dot(
-        grad_logit_low, router_weight.T, preferred_element_type=f32
-    )
-    gained2 = grad_normed2 * expert_gain
-    expert_gain_grad = jnp.sum(grad_normed2 * middle * norm_scale2, 0)
-    grad_middle = (
-        cotangent
-        + norm_scale2 * gained2
-        - middle * norm_scale2**3 * jnp.mean(gained2 * middle, -1, keepdims=True)
-    )
-    grad_attn = grad_middle.astype(bf16)
+    down_term = down_term.reshape(down_weight.shape)
+    output = lax.all_gather(out_part.astype(bf16), "tensor", axis=0, tiled=True).astype(f32)
+    grad_attn = lax.all_gather(grad_middle.astype(bf16), "tensor", axis=0, tiled=True)
     out_weight_grad = jnp.dot(attended.T, grad_attn, preferred_element_type=f32)
     grad_attended = jnp.dot(grad_attn, out_weight.T, preferred_element_type=f32).astype(bf16)
     grad_og = grad_attended.reshape(seq_count, span_rows, key_heads, groups, HD)
@@ -304,38 +679,31 @@
     query_grad = jnp.dot(normed.T, grad_query_lin, preferred_element_type=f32)
     key_grad = jnp.dot(normed.T, grad_key_lin, preferred_element_type=f32)
     value_grad = jnp.dot(normed.T, grad_value_lin, preferred_element_type=f32)
-    grad_normed = head_total(
+    grad_normed = lax.psum_scatter(
         jnp.dot(grad_query_lin, query_weight.T, preferred_element_type=f32)
         + jnp.dot(grad_key_lin, key_weight.T, preferred_element_type=f32)
-        + jnp.dot(grad_value_lin, value_weight.T, preferred_element_type=f32)
-    )
+        + jnp.dot(grad_value_lin, value_weight.T, preferred_element_type=f32),
+        "tensor",
+        scatter_dimension=0,
+        tiled=True,
+    )
+    own_res = own_part(residual)
+    own_scale = own_part(norm_scale)
     gained1 = grad_normed * attention_gain
-    attention_gain_grad = jnp.sum(grad_normed * residual * norm_scale, 0)
-    input_grad = (
+    attention_gain_part = jnp.sum(grad_normed * own_res * own_scale, 0)
+    input_part = (
         grad_middle
-        + norm_scale * gained1
-        - residual * norm_scale**3 * jnp.mean(gained1 * residual, -1, keepdims=True)
-    )
-    (
-        attention_gain_grad,
-        query_grad,
-        key_grad,
-        value_grad,
-        out_weight_grad,
-        expert_gain_grad,
-        router_grad,
-    ) = lax.psum(
-        (
-            attention_gain_grad,
-            query_grad,
-            key_grad,
-            value_grad,
-            out_weight_grad,
-            expert_gain_grad,
-            router_grad,
-        ),
-        "expert",
-    )
+        + own_scale * gained1
+        - own_res * own_scale**3 * jnp.mean(gained1 * own_res, -1, keepdims=True)
+    )
+    input_grad = lax.all_gather(input_part.astype(bf16), "tensor", axis=0, tiled=True).astype(f32)
+    query_grad, key_grad, value_grad, out_weight_grad = lax.psum(
+        (query_grad, key_grad, value_grad, out_weight_grad), "expert"
+    )
+    attention_gain_grad, expert_gain_grad, router_grad = lax.psum(
+        (attention_gain_part, expert_gain_part[0], router_part), ("expert", "tensor")
+    )
+    router_grad = router_grad.T
     return (
         output,
         input_grad,

time: 753 us -> 700 us (0.930); the launches traced: 743 us -> 699 us
  Pallas kernels: 0 us -> 174 us
  matrix products: 104 us -> 20.6 us
  waiting for transfers between devices: 391 us -> 318 us
  other arithmetic: 53.6 us -> 18.2 us
  starting transfers between devices: 18.3 us -> 0.29 us
  blocking collectives: 113 us -> 103 us
    pallas_call x0 -> x1, Pallas kernels: none -> 174 us  [expert_layer(): pl.pallas_call(functools.partial(expert_kernel, n, nz, big), out_shape=ou...]
    psum x4 -> x2, waiting for transfers between devices: 245 us -> 109 us  [the longest x1 95.5 us: shards(): lax.psum((attention_gain_part, expert_gain_part[0], router_part), ('exper...]
    reduce_scatter x0 -> x2, waiting for transfers between devices: none -> 80.8 us  [the longest x1 43.7 us: shards(): lax.psum_scatter(jnp.dot(attended, out_weight, preferred_element_type=f32...]
    dot_general x12 -> x0, matrix products: 78.2 us -> none  [the longest x1 13 us: shards(): cot_down = jnp.dot(cot_all, down_flat.T, preferred_element_type=f32)]
    psum x3 -> x1, blocking collectives: 113 us -> 38.9 us  [shards(): lax.psum((attention_gain_part, expert_gain_part[0], router_part), ('exper...]
    all_gather x0 -> x3, blocking collectives: none -> 64.4 us  [the longest x1 26.4 us: shards(): lax.all_gather(grad_middle.astype(bf16), 'tensor', axis=0, tiled=True)]
    reduce_sum x10 -> x1, other arithmetic: 26.3 us -> 1.26 us  [shards(): attention_gain_part = jnp.sum(grad_normed * own_res * own_scale, 0)]
    all_gather x1 -> x0, waiting for transfers between devices: 24.3 us -> none  [shards(): rows_all = lax.all_gather(normed2, 'expert', axis=0, tiled=True)]
  transfers between devices with their start and end apart: 12 -> 7, of which waited for: 8 -> 7; matrix products, arithmetic and copies ran while one was open for 18% -> 4% of each run, Pallas kernels for 0% -> 0%
where the time goes in v2:
time: 700 us; the launch traced here: 699 us
  waiting for transfers between devices  318 us (45%)
  Pallas kernels  174 us (25%)
  blocking collectives  103 us (15%)
  local copies, waits for them, and re-layouts  46.8 us (7%)
  matrix products  20.6 us (3%)
  other arithmetic  18.2 us (3%)
  between operations  16.6 us (2%)
    pallas_call x1, Pallas kernels, expert_layer(): pl.pallas_call(functools.partial(expert_kernel, n, nz, big), out_shape=ou...  174 us
    psum x1, waiting for transfers between devices, shards(): lax.psum((attention_gain_part, expert_gain_part[0], router_part), ('exper...  95.5 us
    reduce_scatter x1, waiting for transfers between devices, shards(): lax.psum_scatter(all_terms, 'expert', scatter_dimension=0, tiled=True)  58.5 us
    all_gather x1, waiting for transfers between devices, shards(): lax.all_gather(cotangent.astype(bf16), 'expert', axis=0, tiled=True)  45.2 us
    reduce_scatter x1, waiting for transfers between devices, shards(): lax.psum_scatter(jnp.dot(attended, out_weight, preferred_element_type=f32...  43.7 us
    psum x1, blocking collectives, shards(): lax.psum((attention_gain_part, expert_gain_part[0], router_part), ('exper...  38.9 us
    reduce_scatter x1, waiting for transfers between devices, shards(): lax.psum_scatter(jnp.dot(grad_query_lin, query_weight.T, preferred_elemen...  37.2 us
    all_gather x1, blocking collectives, shards(): lax.all_gather(grad_middle.astype(bf16), 'tensor', axis=0, tiled=True)  26.4 us
  transfers between devices with their start and end apart: 7, of which 7 were waited for; matrix products, arithmetic and copies ran while one was open for 4% of the time, Pallas kernels for 0%

profile of v2, /device:TPU:0, one launch (start us, length us, event | category | flops | bytes accessed | tf_op | source)
XLA Modules:
  0.0 698.7 jit_solution(14215478868854137061)
XLA Ops:
  8.9 1.7 fusion.40
  17.1 24.5 %all-gather.3.cloned.1.call-done = bf16[3072,256]{0,1:T(8,128)(2,1)} async-done(((bf16[384,256]{0,1:T(8,128)(2,1)}), bf16[3072,256]{0,1:T(8,128)(2,1)}) %all-gather.3.cloned.1.call-update) | async-done | bytes 1572880 | tf_op jit(solution)/shard_map/all_gather | solution.py:528
  41.6 1.7 copy.37
  44.6 2.6 copy.41
  47.2 3.4 while.37
  50.6 2.6 while.38
  59.5 43.7 %reduce-scatter.4.cloned.1.call-done = f32[96,1024]{1,0:T(8,128)} async-done(((f32[384,1024]{1,0:T(8,128)}), f32[96,1024]{1,0:T(8,128)}) %reduce-scatter.4.cloned.1.call-update) | async-done | bytes 393232 | tf_op jit(solution)/shard_map/reduce_scatter | solution.py:583
  103.2 1.8 dynamic-slice_add_fusion.mid_ref
  105.0 45.2 %all-gather.5.cloned.1.call-done.cot_all = bf16[3072,1024]{1,0:T(8,128)(2,1)} async-done(((bf16[384,1024]{1,0:T(8,128)(2,1)}), bf16[3072,1024]{1,0:T(8,128)(2,1)}) %all-gather.5.cloned.1.call-update) | async-done | bytes 6291472 | tf_op jit(solution)/shard_map/all_gather | solution.py:582
  150.2 174.3 %experts.1 = (f32[96,1024]{1,0:T(8,128)}, f32[96,1024]{1,0:T(8,128)}, f32[32,1024]{1,0:T(8,128)}, f32[1,1024]{1,0:T(1,128)}, f32[1,32]{1,0:T(1,128)}, /*index=5*...) custom-call(f32[96,1024]{1,0:T(8,128)} %dynamic-slice_add_fusion.mid_ref, f32[1,1024]{1,0:T(1,128)} %bitcast.243, ...), custom_call_target="tpu_custom_call" | custom-call | tf_op jit(solution)/shard_map/experts/pallas_call | solution.py:446
  325.5 26.4 %all_gather.18 = bf16[384,1024]{1,0:T(8,128)(2,1)S(1)} all-gather(bf16[96,1024]{1,0:T(8,128)(2,1)S(1)} %convert_element_type.90), channel_id=1, replica_groups=mesh['expert'=8,'tensor'=4] {'tensor'}, dimensions={0}, use_global_device_ids=true | all-gather | bytes 983040 | tf_op jit(solution)/shard_map/all_gather | solution.py:615
  353.9 1.8 broadcast_in_dim.90.clone
  356.6 11.2 %while.39 = (s32[]{:T(128)}, f32[2,192,2,2,64]{1,4,3,2,0:T(8,128)}, f32[2,1536,256]{2,1,0:T(8,128)}, s32[]{:T(128)}, bf16[2,1536,256]{1,2,0:T(8,128)(2,1)}, /*in...) while((s32[]{:T(128)}, f32[2,192,2,2,64]{1,4,3,2,0:T(8,128)}, ...), condition=%wide.region_9.10_spmd.clone, body=%wide.region_8.9_spmd.clone.sunk | while | flops 511968960 | bytes 27291428 | solution.py:651
  365.3 2.5 fusion.118
  367.8 3.9 copy.53
  371.7 3.5 copy.54
  379.2 58.5 %reduce-scatter.6.cloned.1.call-done = f32[384,256]{0,1:T(8,128)} async-done(((f32[3072,256]{0,1:T(8,128)}), f32[384,256]{0,1:T(8,128)}) %reduce-scatter.6.cloned.1.call-update) | async-done | bytes 393232 | tf_op jit(solution)/shard_map/reduce_scatter | solution.py:664
  449.0 20.0 %all_gather.17 = bf16[384,1024]{1,0:T(8,128)(2,1)S(1)} all-gather(bf16[96,1024]{1,0:T(8,128)(2,1)S(1)} %convert_element_type.88), channel_id=1, replica_groups=mesh['expert'=8,'tensor'=4] {'tensor'}, dimensions={0}, use_global_device_ids=true | all-gather | bytes 983040 | tf_op jit(solution)/shard_map/all_gather | solution.py:614
  471.6 95.5 %all-reduce.5.cloned.1.call-done = f32[1024,32]{0,1:T(8,128)} async-done(((f32[1024,32]{0,1:T(8,128)}), f32[1024,32]{0,1:T(8,128)}) %all-reduce.5.cloned.1.call-update) | async-done | bytes 131088 | tf_op jit(solution)/shard_map/psum | solution.py:703
  567.1 37.2 %reduce-scatter.8.cloned.1.call-done = f32[96,1024]{1,0:T(8,128)} async-done(((f32[384,1024]{1,0:T(8,128)}), f32[96,1024]{1,0:T(8,128)}) %reduce-scatter.8.cloned.1.call-update) | async-done | bytes 393232 | tf_op jit(solution)/shard_map/reduce_scatter | solution.py:682
  606.7 18.1 %all_gather.19 = bf16[384,1024]{1,0:T(8,128)(2,1)S(1)} all-gather(bf16[96,1024]{1,0:T(8,128)(2,1)S(1)} %subtract_convert_fusion), channel_id=1, replica_groups=mesh['expert'=8,'tensor'=4] {'tensor'}, dimensions={0}, use_global_device_ids=true | all-gather | bytes 983040 | tf_op jit(solution)/shard_map/all_gather | solution.py:699
  626.1 38.9 %all-reduce = (f32[1024]{0:T(1024)}, f32[1024]{0:T(1024)}) all-reduce(f32[1024]{0:T(1024)S(1)} %get-tuple-element.293, f32[1024]{0:T(1024)S(1)} %bitcast.244), channel_id=1, replica_groups=mesh['expert'=8,'tensor'=4] {'expert','tensor'}, use_global_device_ids=true, to_apply=%region_15.16 | all-reduce | flops 2048 | bytes 16384 | tf_op jit(solution)/shard_map/psum | solution.py:703
  665.1 13.6 %all-reduce.7.cloned.1.call-done = (f32[1024,256]{1,0:T(8,128)}, f32[1024,128]{1,0:T(8,128)}, f32[1024,128]{1,0:T(8,128)}, f32[256,1024]{1,0:T(8,128)}) async-done(((f32[1024,256]{1,0:T(8,128)}, f32[1024,128]{1,0:T(8,128)}, f32[1024,128]{1,0:T(8,128)}, f32[256,1024]{1,0:T(8,128)}), (f32[1024,256]{1,0:T(8,128)}, f32[1024,128]{1,0:T(8,128)}, f32[1024,128]{1,0:T(8,128)}, ...) | async-done | bytes 3145744 | tf_op jit(solution)/shard_map/psum | solution.py:700
  679.2 2.3 copy.118
  (206 shorter events, 64.3 us)
Async XLA Ops:
  7.2 47.0 %copy-start = (bf16[256,1024]{1,0:T(8,128)(2,1)S(1)}, bf16[256,1024]{1,0:T(8,128)(2,1)}, u32[]{:S(2)}) copy-start(bf16[256,1024]{1,0:T(8,128)(2,1)} %param.25) | copy-start | bytes 1572868
  7.2 3.4 copy-start.2
  7.2 3.4 copy-start.37
  7.2 3.4 copy-start.29
  7.2 34.4 %all-gather.3.cloned.1.call-start = ((), (), s32[]{:S(2)}) async-start(), calls=%async_computation.3 | async-start | bytes 1769472 | tf_op jit(solution)/shard_map/all_gather | solution.py:528
  12.9 90.3 %reduce-scatter.4.cloned.1.call-start = ((), (), s32[]{:S(2)}) async-start(), calls=%async_computation.4 | async-start | bytes 1966080 | tf_op jit(solution)/shard_map/reduce_scatter | solution.py:583
  44.6 2.6 copy-start.35
  47.2 3.5 copy-start.26
  55.8 94.3 %all-gather.5.cloned.1.call-start = ((), (), s32[]{:S(2)}) async-start(), calls=%async_computation.5 | async-start | bytes 7077888 | tf_op jit(solution)/shard_map/all_gather | solution.py:582
  57.1 380.6 %reduce-scatter.6.cloned.1.call-start = ((), (), s32[]{:S(2)}) async-start(), calls=%async_computation.6 | async-start | bytes 3538944 | tf_op jit(solution)/shard_map/reduce_scatter | solution.py:664
  57.3 45.9 %copy-start.7 = (f32[384,1024]{1,0:T(8,128)}, f32[384,1024]{1,0:T(8,128)S(1)}, u32[]{:S(2)}) copy-start(f32[384,1024]{1,0:T(8,128)S(1)} %convert_element_type.77) | copy-start | bytes 4718596
  356.6 4.0 copy-start.31
  375.3 191.8 %all-reduce.5.cloned.1.call-start = ((), (), s32[]{:S(2)}) async-start(), calls=%async_computation.8 | async-start | bytes 262144 | tf_op jit(solution)/shard_map/psum | solution.py:703
  378.7 60.1 %copy-start.20 = (f32[384,64]{0,1:T(8,128)S(1)}, f32[384,64]{0,1:T(8,128)}, u32[]{:S(2)}) copy-start(f32[384,64]{0,1:T(8,128)} %copy-done.19) | copy-start | bytes 294916
  379.1 59.8 %copy-start.33 = (bf16[1024,128]{1,0:T(8,128)(2,1)S(1)}, bf16[1024,128]{1,0:T(8,128)(2,1)}, u32[]{:S(2)}) copy-start(bf16[1024,128]{1,0:T(8,128)(2,1)} %param.23) | copy-start | bytes 786436
  379.1 225.2 %reduce-scatter.8.cloned.1.call-start = ((), (), s32[]{:S(2)}) async-start(), calls=%async_computation.7 | async-start | bytes 1966080 | tf_op jit(solution)/shard_map/reduce_scatter | solution.py:682
  441.3 237.4 %all-reduce.7.cloned.1.call-start = ((), (), s32[]{:S(2)}) async-start(), calls=%async_computation.9 | async-start | bytes 6291456 | tf_op jit(solution)/shard_map/psum | solution.py:700
  449.0 21.3 %copy-start.40 = (f32[1,32]{1,0:T(1,128)S(1)}, f32[1,32]{1,0:T(1,128)}, u32[]{:S(2)}) copy-start(f32[1,32]{1,0:T(1,128)} %get-tuple-element.175) | copy-start | bytes 388
  449.0 155.3 %copy-start.8 = (f32[384,1024]{1,0:T(8,128)S(1)}, f32[384,1024]{1,0:T(8,128)}, u32[]{:S(2)}) copy-start(f32[384,1024]{1,0:T(8,128)} %copy-done.7) | copy-start | bytes 4718596
  469.0 136.6 %copy-start.16 = (f32[96,1024]{1,0:T(8,128)S(1)}, f32[96,1024]{1,0:T(8,128)}, u32[]{:S(2)}) copy-start(f32[96,1024]{1,0:T(8,128)} %get-tuple-element.172) | copy-start | bytes 1179652
  606.7 19.4 %copy-start.39 = (f32[1,1024]{1,0:T(1,128)S(1)}, f32[1,1024]{1,0:T(1,128)}, u32[]{:S(2)}) copy-start(f32[1,1024]{1,0:T(1,128)} %get-tuple-element.176) | copy-start | bytes 12292
  678.6 2.8 copy-start.22
  679.2 3.1 copy-start.21
  687.1 3.7 copy-start.1
  (24 other events, 37.5 us)
Sparse Core Ops, SparseCore 0:
  13.0 28.5 all-gather.2
  55.9 47.2 reduce-scatter.3
  105.7 44.4 all-gather.4
  375.4 62.2 reduce-scatter.5
  444.0 123.0 all-reduce.4
  570.0 34.2 reduce-scatter.7
  609.5 69.1 all-reduce.6

commit v3 on v2

--- a/solution.py
+++ b/solution.py
@@ -1,5 +1,4 @@
 import functools
-import math
 
 import jax
 import jax.numpy as jnp
@@ -456,23 +455,725 @@
     )(mid, gain[None], router, routes, gate, up, down.reshape(inner_w, width), cot, cot_all)[:8]
 
 
-def rope_tables(positions, head_size):
-    half_size = head_size // 2
-    frequency = THETA ** (-2.0 * jnp.arange(half_size, dtype=jnp.float32) / head_size)
-    angles = positions.astype(jnp.float32)[:, None] * frequency[None, :]
-    cosines = jnp.cos(angles)
-    sine_table = jnp.sin(angles)
-    return (jnp.concatenate([cosines, cosines], -1), jnp.concatenate([sine_table, sine_table], -1))
-
-
-def rotate(values, cosines, sine_table, forward):
-    half_size = values.shape[-1] // 2
-    if forward:
-        turned = jnp.concatenate([-values[..., half_size:], values[..., :half_size]], -1)
-        return values * cosines[:, None, :] + turned * sine_table[:, None, :]
-    scaled = values * sine_table[:, None, :]
-    turned = jnp.concatenate([scaled[..., half_size:], -scaled[..., :half_size]], -1)
-    return values * cosines[:, None, :] + turned
+def turn(values, cos, sin, last, forward):
+    lane = lax.broadcasted_iota(jnp.int32, (values.shape[0], 128), 1)
+    first_half = lax.rem(lane, HD) < HD // 2
+    parts = []
+    for g in range(values.shape[1] // 128):
+        v = values[:, g * 128 : (g + 1) * 128]
+        if g * 128 >= last:
+            parts.append(v)
+            continue
+        turned = jnp.where(
+            first_half, -pltpu.roll(v, 128 - HD // 2, 1), pltpu.roll(v, HD // 2, 1)
+        )
+        new = v * cos + turned * sin if forward else v * cos - turned * sin
+        if (g + 1) * 128 > last:
+            new = jnp.where(lane + g * 128 < last, new, v)
+        parts.append(new)
+    return jnp.concatenate(parts, 1) if len(parts) > 1 else parts[0]
+
+
+def greet(n, nz, e, z, sib):
+    barrier = pltpu.get_barrier_semaphore()
+    pl.semaphore_signal(barrier, inc=1, device_id=(sib, z), device_id_type=MESH)
+    for s in range(1, n // 2):
+        pl.semaphore_signal(
+            barrier, inc=1, device_id=(lax.rem(e + 2 * s, n), z), device_id_type=MESH
+        )
+    for k in range(1, nz):
+        pl.semaphore_signal(barrier, inc=1, device_id=(e, lax.rem(z + k, nz)), device_id_type=MESH)
+    return barrier
+
+
+def attend_kernel(
+    n,
+    nz,
+    x_ref,
+    gain_ref,
+    wq_ref,
+    wk_ref,
+    wv_ref,
+    wo_ref,
+    cos_ref,
+    sin_ref,
+    lens_ref,
+    mid_ref,
+    q_ref,
+    kv_ref,
+    lrow_ref,
+    att_ref,
+    wqkv,
+    part,
+    m_s,
+    l_s,
+    o_s,
+    zsend,
+    zin,
+    ks,
+    kr,
+    kfs,
+    kfr,
+    zgs,
+    zgr,
+):
+    e = lax.axis_index("expert")
+    z = lax.axis_index("tensor")
+    sib = e + 1 - 2 * lax.rem(e, 2)
+    half = n // 2
+    tok, width = x_ref.shape
+    rows = tok // nz
+    qw = wq_ref.shape[1]
+    kw = wk_ref.shape[1]
+    seqs = kv_ref.shape[0]
+    span = tok // seqs
+    heads = kw // HD
+    groups = qw // kw
+    barrier = greet(n, nz, e, z, sib)
+
+    wqkv[:, 0:qw] = wq_ref[...]
+    wqkv[:, qw : qw + kw] = wk_ref[...]
+    wqkv[:, qw + kw :] = wv_ref[...]
+    x = x_ref[...].astype(f32)
+    scale1 = lax.rsqrt(jnp.mean(x * x, -1, keepdims=True) + EPS)
+    normed = (x * scale1 * gain_ref[...]).astype(bf16)
+    lin = dot_nn(normed, wqkv[...])
+    turned = turn(lin, cos_ref[...], sin_ref[...], qw + kw, True).astype(bf16)
+    q_ref[...] = turned[:, :qw]
+    for s in range(seqs):
+        kv_ref[s, pl.ds(pl.multiple_of(e * span, 16), span)] = turned[
+            s * span : (s + 1) * span, qw:
+        ]
+    pl.semaphore_wait(barrier, half + nz - 1)
+
+    def rows_of(j, s):
+        return kv_ref.at[s, pl.ds(pl.multiple_of(j * span, 16), span)]
+
+    for t in range(1, half):
+        to = (lax.rem(e + 2 * t, n), z)
+        for s in range(seqs):
+            remote(rows_of(e, s), rows_of(e, s), ks.at[t, s], kr.at[t, s], to).start()
+    for s in range(seqs):
+        remote(rows_of(e, s), rows_of(e, s), kfs.at[0, s], kfr.at[0, s], (sib, z)).start()
+
+    def forward(t, carry):
+        src = lax.rem(e - 2 * t + n, n)
+        for s in range(seqs):
+            remote(rows_of(src, s), rows_of(src, s), ks.at[t, s], kr.at[t, s], (src, z)).wait_recv()
+            remote(rows_of(src, s), rows_of(src, s), kfs.at[t, s], kfr.at[t, s], (sib, z)).start()
+        return carry
+
+    lax.fori_loop(1, half, forward, 0)
+
+    def arrive(t, carry):
+        src = lax.rem(sib - 2 * t + n, n)
+        for s in range(seqs):
+            remote(
+                rows_of(src, s), rows_of(src, s), kfs.at[t, s], kfr.at[t, s], (sib, z)
+            ).wait_recv()
+        return carry
+
+    lax.fori_loop(0, half, arrive, 0)
+
+    ck = 2 * span
+    trip = (e * span + span - 1) // ck + 1
+    stacked = groups * span
+    qpos = lax.broadcasted_iota(jnp.int32, (stacked, ck), 0)
+    qpos = e * span + lax.rem(qpos, span)
+    kiota = lax.broadcasted_iota(jnp.int32, (stacked, ck), 1)
+    for s in range(seqs):
+        for h in range(heads):
+            srows = slice(s * span, (s + 1) * span)
+            qst = jnp.concatenate(
+                [
+                    q_ref[srows, (h * groups + g) * HD : (h * groups + g + 1) * HD]
+                    for g in range(groups)
+                ],
+                0,
+            )
+            m_s[...] = jnp.full_like(m_s, -1e30)
+            l_s[...] = jnp.zeros_like(l_s)
+            o_s[...] = jnp.zeros_like(o_s)
+
+            def chunk(c, carry):
+                at = pl.ds(pl.multiple_of(c * ck, 16), ck)
+                keys = kv_ref[s, at, h * HD : (h + 1) * HD]
+                vals = kv_ref[s, at, kw + h * HD : kw + (h + 1) * HD]
+                scores = dot_nt(qst, keys) * HD ** (-0.5)
+                kpos = kiota + c * ck
+                scores = jnp.where((kpos <= qpos) & (kpos < lens_ref[s]), scores, -1e30)
+                old = m_s[:, 0:1]
+                new = jnp.maximum(old, jnp.max(scores, -1, keepdims=True))
+                weights = jnp.exp(scores - new)
+                shrink = jnp.exp(old - new)
+                m_s[...] = jnp.broadcast_to(new, m_s.shape)
+                l_s[...] = l_s[...] * shrink + jnp.sum(weights, -1, keepdims=True)
+                o_s[...] = o_s[...] * shrink + dot_nn(weights.astype(bf16), vals)
+                return carry
+
+            lax.fori_loop(0, trip, chunk, 0)
+            result = o_s[...] / l_s[:, 0:HD]
+            for g in range(groups):
+                cols = slice((h * groups + g) * HD, (h * groups + g + 1) * HD)
+                att_ref[srows, cols] = result[g * span : (g + 1) * span]
+            logs = m_s[...] + jnp.log(l_s[...])
+            lrow_ref[s * heads + h] = logs.T[0:8]
+
+    part[...] = dot_nn(att_ref[...].astype(bf16), wo_ref[...])
+    for k in range(1, nz):
+        zz = lax.rem(z + k, nz)
+        zsend[k - 1] = part[pl.ds(pl.multiple_of(zz * rows, 16), rows), :].astype(bf16)
+        remote(zsend.at[k - 1], zin.at[k - 1], zgs.at[k - 1], zgr.at[k - 1], (e, zz)).start()
+    own_rows = pl.ds(pl.multiple_of(z * rows, 16), rows)
+    mid = x_ref[own_rows, :].astype(f32) + part[own_rows, :]
+    for k in range(1, nz):
+        remote(zsend.at[k - 1], zin.at[k - 1], zgs.at[k - 1], zgr.at[k - 1], (e, z)).wait_recv()
+        mid = mid + zin[k - 1].astype(f32)
+    mid_ref[...] = mid
+    for k in range(1, nz):
+        remote(zsend.at[k - 1], zin.at[k - 1], zgs.at[k - 1], zgr.at[k - 1], (e, z)).wait_send()
+
+    def sent(t, carry):
+        for s in range(seqs):
+
+            @pl.when(t > 0)
+            def _():
+                remote(
+                    rows_of(e, s), rows_of(e, s), ks.at[t, s], kr.at[t, s], (sib, z)
+                ).wait_send()
+
+            remote(rows_of(e, s), rows_of(e, s), kfs.at[t, s], kfr.at[t, s], (sib, z)).wait_send()
+        return carry
+
+    lax.fori_loop(0, half, sent, 0)
+
+
+def attend_layer(n, nz, x, gain, wq, wk, wv, wo, cos, sin, lens):
+    tok, width = x.shape
+    rows = tok // nz
+    qw, kw = wq.shape[1], wk.shape[1]
+    seqs = lens.shape[0]
+    span = tok // seqs
+    half = n // 2
+    stacked = (qw // kw) * span
+    dma = pltpu.SemaphoreType.DMA
+    vmem = pl.BlockSpec(memory_space=pltpu.VMEM)
+    sds = jax.ShapeDtypeStruct
+    return pl.pallas_call(
+        functools.partial(attend_kernel, n, nz),
+        out_shape=[
+            sds((rows, width), f32),
+            sds((tok, qw), bf16),
+            sds((seqs, n * span, 2 * kw), bf16),
+            sds((seqs * (kw // HD), 8, stacked), f32),
+            sds((tok, qw), f32),
+        ],
+        in_specs=[vmem] * 8 + [pl.BlockSpec(memory_space=pltpu.SMEM)],
+        out_specs=[vmem] * 5,
+        scratch_shapes=[
+            pltpu.VMEM((width, qw + 2 * kw), bf16),
+            pltpu.VMEM((tok, width), f32),
+            pltpu.VMEM((stacked, 128), f32),
+            pltpu.VMEM((stacked, 128), f32),
+            pltpu.VMEM((stacked, HD), f32),
+            pltpu.VMEM((nz - 1, rows, width), bf16),
+            pltpu.VMEM((nz - 1, rows, width), bf16),
+        ]
+        + [dma((half, seqs))] * 4
+        + [dma((nz - 1,))] * 2,
+        compiler_params=pltpu.CompilerParams(
+            collective_id=2, has_side_effects=True, vmem_limit_bytes=48 << 20
+        ),
+        name="attend",
+    )(x, gain[None], wq, wk, wv, wo, cos, sin, lens)
+
+
+def return_kernel(
+    n,
+    nz,
+    gmid_ref,
+    mixed_ref,
+    rgrad_ref,
+    ggrad_ref,
+    x_ref,
+    gain_ref,
+    wq_ref,
+    wk_ref,
+    wv_ref,
+    wo_ref,
+    cos_ref,
+    sin_ref,
+    q_ref,
+    kv_ref,
+    lrow_ref,
+    att_ref,
+    lens_ref,
+    out_ref,
+    igrad_ref,
+    wsum_ref,
+    small_ref,
+    wqkv,
+    gat,
+    obuf,
+    igbuf,
+    datt,
+    dq_s,
+    acc_q,
+    dkv,
+    kvo,
+    kvi,
+    kvf,
+    kvr,
+    part,
+    zsend,
+    zin,
+    wpack,
+    wsi,
+    wsf,
+    wsr,
+    wall,
+    sz1,
+    sz2,
+    sown,
+    ssib,
+    schip,
+    zas,
+    zar,
+    zos,
+    zor,
+    zis,
+    zir,
+    zps,
+    zpr,
+    z1s,
+    z1r,
+    z2s,
+    z2r,
+    kos,
+    kor,
+    kfs,
+    kfr,
+    wos,
+    wor,
+    wfs,
+    wfr,
+    was,
+    war,
+    wbs,
+    wbr,
+    sbs,
+    sbr,
+    scs,
+    scr,
+):
+    e = lax.axis_index("expert")
+    z = lax.axis_index("tensor")
+    core = lax.rem(e, 2)
+    sib = e + 1 - 2 * core
+    half = n // 2
+    rows, width = gmid_ref.shape
+    tok = rows * nz
+    qw = wq_ref.shape[1]
+    kw = wk_ref.shape[1]
+    seqs = kv_ref.shape[0]
+    span = tok // seqs
+    heads = kw // HD
+    groups = qw // kw
+    dn = width // n
+    experts = rgrad_ref.shape[0]
+    own_rows = pl.ds(pl.multiple_of(z * rows, 16), rows)
+    barrier = greet(n, nz, e, z, sib)
+
+    gat[own_rows, :] = gmid_ref[...].astype(bf16)
+    obuf[own_rows, :] = mixed_ref[...].astype(bf16)
+    sz1[z] = jnp.concatenate(
+        [rgrad_ref[...], ggrad_ref[...], jnp.zeros((15, width), f32)], 0
+    ).astype(bf16)
+    pl.semaphore_wait(barrier, half + nz - 1)
+
+    def z_copies(buf_of, send, recv):
+        return [
+            remote(
+                buf_of(z), buf_of(z), send.at[k - 1], recv.at[k - 1], (e, lax.rem(z + k, nz))
+            )
+            for k in range(1, nz)
+        ]
+
+    def z_arrivals(buf_of, send, recv):
+        return [
+            remote(
+                buf_of(lax.rem(z + nz - k, nz)),
+                buf_of(lax.rem(z + nz - k, nz)),
+                send.at[k - 1],
+                recv.at[k - 1],
+                (e, lax.rem(z + nz - k, nz)),
+            )
+            for k in range(1, nz)
+        ]
+
+    def part_of(ref):
+        return lambda zz: ref.at[pl.ds(pl.multiple_of(zz * rows, 16), rows)]
+
+    def slot_of(ref):
+        return lambda zz: ref.at[zz]
+
+    for copy in z_copies(part_of(gat), zas, zar):
+        copy.start()
+    for copy in z_copies(slot_of(sz1), z1s, z1r):
+        copy.start()
+    for copy in z_copies(part_of(obuf), zos, zor):
+        copy.start()
+
+    wqkv[:, 0:qw] = wq_ref[...]
+    wqkv[:, qw : qw + kw] = wk_ref[...]
+    wqkv[:, qw + kw :] = wv_ref[...]
+    x = x_ref[...].astype(f32)
+    scale1 = lax.rsqrt(jnp.mean(x * x, -1, keepdims=True) + EPS)
+    normed = (x * scale1 * gain_ref[...]).astype(bf16)
+    dkv[...] = jnp.zeros_like(dkv)
+
+    for copy in z_arrivals(part_of(gat), zas, zar):
+        copy.wait_recv()
+    datt[...] = dot_nt(gat[...], wo_ref[...]).astype(bf16)
+
+    ck = 2 * span
+    trip = (e * span + span - 1) // ck + 1
+    stacked = groups * span
+    kiota = lax.broadcasted_iota(jnp.int32, (ck, stacked), 0)
+    qpos = e * span + lax.rem(lax.broadcasted_iota(jnp.int32, (ck, stacked), 1), span)
+    for s in range(seqs):
+        for h in range(heads):
+            srows = slice(s * span, (s + 1) * span)
+
+            def gather(ref):
+                return jnp.concatenate(
+                    [
+                        ref[srows, (h * groups + g) * HD : (h * groups + g + 1) * HD]
+                        for g in range(groups)
+                    ],
+                    0,
+                )
+
+            qst = gather(q_ref)
+            dst = gather(datt)
+            delta = jnp.sum(dst.astype(f32) * gather(att_ref), -1, keepdims=True)
+            drow = jnp.broadcast_to(delta, (stacked, 128)).T[0:1]
+            lrow = lrow_ref[s * heads + h, 0:1, :]
+            acc_q[...] = jnp.zeros_like(acc_q)
+
+            def chunk(c, carry):
+                at = pl.ds(pl.multiple_of(c * ck, 16), ck)
+                keys = kv_ref[s, at, h * HD : (h + 1) * HD]
+                vals = kv_ref[s, at, kw + h * HD : kw + (h + 1) * HD]
+                scores = dot_nt(keys, qst) * HD ** (-0.5)
+                kpos = kiota + c * ck
+                soft = jnp.where(
+                    (kpos <= qpos) & (kpos < lens_ref[s]), jnp.exp(scores - lrow), 0.0
+                )
+                grad_probs = dot_nt(vals, dst)
+                grad_scores = (soft * (grad_probs - drow)).astype(bf16)
+                dkv[s, at, h * HD : (h + 1) * HD] = dot_nn(grad_scores, qst) * HD ** (-0.5)
+                dkv[s, at, kw + h * HD : kw + (h + 1) * HD] = dot_nn(soft.astype(bf16), dst)
+                acc_q[...] += dot_tn(grad_scores, keys)
+                return carry
+
+            lax.fori_loop(0, trip, chunk, 0)
+            result = acc_q[...] * HD ** (-0.5)
+            for g in range(groups):
+                cols = slice((h * groups + g) * HD, (h * groups + g + 1) * HD)
+                dq_s[srows, cols] = result[g * span : (g + 1) * span]
+
+    def key_rows(j, s):
+        return dkv[s, pl.ds(pl.multiple_of(j * span, 16), span), :]
+
+    def key_send(t):
+        return remote(kvo.at[t], kvi.at[t], kos.at[t], kor.at[t], (sib, z))
+
+    def key_final(t):
+        to = (lax.rem(e - 2 * t + n, n), z)
+        return remote(kvf.at[t - 1], kvr.at[t - 1], kfs.at[t - 1], kfr.at[t - 1], to)
+
+    def key_give(i, carry):
+        t = half - 1 - i
+        oth = lax.rem(sib - 2 * t + n, n)
+        for s in range(seqs):
+            kvo[t, s] = key_rows(oth, s).astype(bf16)
+        key_send(t).start()
+        return carry
+
+    lax.fori_loop(0, half, key_give, 0)
+
+    def key_pass(i, carry):
+        t = half - 1 - i
+        key_send(t).wait_recv()
+        own = lax.rem(e - 2 * t + n, n)
+        for s in range(seqs):
+            kvf[t - 1, s] = (key_rows(own, s) + kvi[t, s].astype(f32)).astype(bf16)
+        key_final(t).start()
+        return carry
+
+    lax.fori_loop(0, half - 1, key_pass, 0)
+
+    for copy in z_arrivals(slot_of(sz1), z1s, z1r):
+        copy.wait_recv()
+    first = sz1[0].astype(f32)
+    for zz in range(1, nz):
+        first = first + sz1[zz].astype(f32)
+
+    out_grad = dot_tn(gat[...], att_ref[...].astype(bf16))
+    for j in range(n):
+        wpack[j, :, qw + 2 * kw :] = out_grad[j * dn : (j + 1) * dn].astype(bf16)
+
+    key_send(0).wait_recv()
+    own_kv = [key_rows(e, s) + kvi[0, s].astype(f32) for s in range(seqs)]
+    for t in range(1, half):
+        key_final(t).wait_recv()
+        for s in range(seqs):
+            own_kv[s] = own_kv[s] + kvr[t - 1, s].astype(f32)
+    lin = jnp.concatenate([dq_s[...], jnp.concatenate(own_kv, 0)], 1)
+    glin = turn(lin, cos_ref[...], sin_ref[...], qw + kw, False).astype(bf16)
+    part[...] = dot_nt(glin, wqkv[...])
+    for k in range(1, nz):
+        zz = lax.rem(z + k, nz)
+        zsend[k - 1] = part[pl.ds(pl.multiple_of(zz * rows, 16), rows), :].astype(bf16)
+        remote(zsend.at[k - 1], zin.at[k - 1], zps.at[k - 1], zpr.at[k - 1], (e, zz)).start()
+    again = jnp.sum(part[...] * x * scale1, 0, keepdims=True)
+    sz2[z] = jnp.concatenate([again, jnp.zeros((15, width), f32)], 0).astype(bf16)
+    for copy in z_copies(slot_of(sz2), z2s, z2r):
+        copy.start()
+
+    lin_grad = dot_tn(normed, glin)
+    for j in range(n):
+        wpack[j, :, : qw + 2 * kw] = lin_grad[j * dn : (j + 1) * dn].astype(bf16)
+
+    def weight_send(t):
+        oth = lax.rem(sib - 2 * t + n, n)
+        return remote(wpack.at[oth], wsi.at[t], wos.at[t], wor.at[t], (sib, z))
+
+    def weight_final(t):
+        to = (lax.rem(e - 2 * t + n, n), z)
+        return remote(wsf.at[t - 1], wsr.at[t - 1], wfs.at[t - 1], wfr.at[t - 1], to)
+
+    def weight_give(i, carry):
+        weight_send(half - 1 - i).start()
+        return carry
+
+    lax.fori_loop(0, half, weight_give, 0)
+
+    def weight_pass(i, carry):
+        t = half - 1 - i
+        weight_send(t).wait_recv()
+        own = lax.rem(e - 2 * t + n, n)
+        wsf[t - 1] = (wpack[own].astype(f32) + wsi[t].astype(f32)).astype(bf16)
+        weight_final(t).start()
+        return carry
+
+    lax.fori_loop(0, half - 1, weight_pass, 0)
+
+    for copy in z_arrivals(slot_of(sz2), z2s, z2r):
+        copy.wait_recv()
+    second = sz2[0].astype(f32)
+    for zz in range(1, nz):
+        second = second + sz2[zz].astype(f32)
+    sown[...] = jnp.concatenate(
+        [first[: experts + 1], second[0:1], jnp.zeros((14, width), f32)], 0
+    ).astype(bf16)
+    small_sib = remote(sown, ssib, sbs, sbr, (sib, z))
+    small_sib.start()
+
+    own_x = x_ref[own_rows, :].astype(f32)
+    own_scale = lax.rsqrt(jnp.mean(own_x * own_x, -1, keepdims=True) + EPS)
+    grad_normed = part[own_rows, :]
+    for k in range(1, nz):
+        remote(zsend.at[k - 1], zin.at[k - 1], zps.at[k - 1], zpr.at[k - 1], (e, z)).wait_recv()
+        grad_normed = grad_normed + zin[k - 1].astype(f32)
+    gained = grad_normed * gain_ref[...]
+    igrad = (
+        gmid_ref[...]
+        + own_scale * gained
+        - own_x
+        * (own_scale * own_scale * own_scale)
+        * jnp.mean(gained * own_x, -1, keepdims=True)
+    )
+    igbuf[own_rows, :] = igrad.astype(bf16)
+    for copy in z_copies(part_of(igbuf), zis, zir):
+        copy.start()
+
+    small_sib.wait_recv()
+    me = e // 2
+    schip[me] = (sown[...].astype(f32) + ssib[...].astype(f32)).astype(bf16)
+
+    def small_send(t):
+        to = (lax.rem(e + 2 * t, n), z)
+        return remote(schip.at[me], schip.at[me], scs.at[t - 1], scr.at[t - 1], to)
+
+    for t in range(1, half):
+        small_send(t).start()
+
+    weight_send(0).wait_recv()
+    total = wpack[e].astype(f32) + wsi[0].astype(f32)
+    for t in range(1, half):
+        weight_final(t).wait_recv()
+        total = total + wsr[t - 1].astype(f32)
+    wall[e] = total.astype(bf16)
+
+    def all_send(t):
+        to = (lax.rem(e + 2 * t, n), z)
+        return remote(wall.at[e], wall.at[e], was.at[t], war.at[t], to)
+
+    def all_pass(src, t):
+        return remote(wall.at[src], wall.at[src], wbs.at[t], wbr.at[t], (sib, z))
+
+    for t in range(1, half):
+        all_send(t).start()
+    all_pass(e, 0).start()
+    for copy in z_arrivals(part_of(obuf), zos, zor):
+        copy.wait_recv()
+    out_ref[...] = obuf[...].astype(f32)
+
+    def all_forward(t, carry):
+        src = lax.rem(e - 2 * t + n, n)
+        remote(wall.at[src], wall.at[src], was.at[t], war.at[t], (src, z)).wait_recv()
+        all_pass(src, t).start()
+        return carry
+
+    lax.fori_loop(1, half, all_forward, 0)
+
+    for t in range(1, half):
+        src = lax.rem(me + half - t, half)
+        remote(
+            schip.at[src], schip.at[src], scs.at[t - 1], scr.at[t - 1], (sib, z)
+        ).wait_recv()
+    small = schip[0].astype(f32)
+    for t in range(1, half):
+        small = small + schip[t].astype(f32)
+    small_ref[...] = small
+
+    for copy in z_arrivals(part_of(igbuf), zis, zir):
+        copy.wait_recv()
+    igrad_ref[...] = igbuf[...].astype(f32)
+
+    def all_arrive(t, carry):
+        src = lax.rem(sib - 2 * t + n, n)
+        all_pass(src, t).wait_recv()
+        return carry
+
+    lax.fori_loop(0, half, all_arrive, 0)
+    for j in range(n):
+        wsum_ref[j * dn : (j + 1) * dn, :] = wall[j].astype(f32)
+
+    for copy in (
+        z_copies(part_of(gat), zas, zar)
+        + z_copies(slot_of(sz1), z1s, z1r)
+        + z_copies(part_of(obuf), zos, zor)
+        + z_copies(slot_of(sz2), z2s, z2r)
+        + z_copies(part_of(igbuf), zis, zir)
+    ):
+        copy.wait_send()
+    for k in range(1, nz):
+        remote(zsend.at[k - 1], zin.at[k - 1], zps.at[k - 1], zpr.at[k - 1], (e, z)).wait_send()
+    small_sib.wait_send()
+
+    def drained(t, carry):
+        key_send(t).wait_send()
+        weight_send(t).wait_send()
+        all_pass(e, t).wait_send()
+
+        @pl.when(t > 0)
+        def _():
+            key_final(t).wait_send()
+            weight_final(t).wait_send()
+            all_send(t).wait_send()
+            small_send(t).wait_send()
+
+        return carry
+
+    lax.fori_loop(0, half, drained, 0)
+
+
+def return_layer(
+    n, nz, gmid, mixed, rgrad, ggrad, x, gain, wq, wk, wv, wo, cos, sin, q, kv, lrow, att, lens
+):
+    tok, width = x.shape
+    rows = tok // nz
+    qw, kw = wq.shape[1], wk.shape[1]
+    seqs = lens.shape[0]
+    span = tok // seqs
+    half = n // 2
+    stacked = (qw // kw) * span
+    pack = 2 * qw + 2 * kw
+    small_rows = rgrad.shape[0] + 16
+    dma = pltpu.SemaphoreType.DMA
+    vmem = pl.BlockSpec(memory_space=pltpu.VMEM)
+    sds = jax.ShapeDtypeStruct
+    zdma = dma((nz - 1,))
+    hdma = dma((half,))
+    fdma = dma((half - 1,))
+    return pl.pallas_call(
+        functools.partial(return_kernel, n, nz),
+        out_shape=[
+            sds((tok, width), f32),
+            sds((tok, width), f32),
+            sds((width, pack), f32),
+            sds((small_rows, width), f32),
+        ],
+        in_specs=[vmem] * 16 + [pl.BlockSpec(memory_space=pltpu.SMEM)],
+        out_specs=[vmem] * 4,
+        scratch_shapes=[
+            pltpu.VMEM((width, qw + 2 * kw), bf16),
+            pltpu.VMEM((tok, width), bf16),
+            pltpu.VMEM((tok, width), bf16),
+            pltpu.VMEM((tok, width), bf16),
+            pltpu.VMEM((tok, qw), bf16),
+            pltpu.VMEM((tok, qw), f32),
+            pltpu.VMEM((stacked, HD), f32),
+            pltpu.VMEM((seqs, n * span, 2 * kw), f32),
+            pltpu.VMEM((half, seqs, span, 2 * kw), bf16),
+            pltpu.VMEM((half, seqs, span, 2 * kw), bf16),
+            pltpu.VMEM((half - 1, seqs, span, 2 * kw), bf16),
+            pltpu.VMEM((half - 1, seqs, span, 2 * kw), bf16),
+            pltpu.VMEM((tok, width), f32),
+            pltpu.VMEM((nz - 1, rows, width), bf16),
+            pltpu.VMEM((nz - 1, rows, width), bf16),
+            pltpu.VMEM((n, width // n, pack), bf16),
+            pltpu.VMEM((half, width // n, pack), bf16),
+            pltpu.VMEM((half - 1, width // n, pack), bf16),
+            pltpu.VMEM((half - 1, width // n, pack), bf16),
+            pltpu.VMEM((n, width // n, pack), bf16),
+            pltpu.VMEM((nz, small_rows, width), bf16),
+            pltpu.VMEM((nz, 16, width), bf16),
+            pltpu.VMEM((small_rows, width), bf16),
+            pltpu.VMEM((small_rows, width), bf16),
+            pltpu.VMEM((half, small_rows, width), bf16),
+        ]
+        + [zdma] * 12
+        + [hdma, hdma, fdma, fdma]
+        + [hdma, hdma, fdma, fdma]
+        + [hdma] * 4
+        + [dma, dma, fdma, fdma],
+        compiler_params=pltpu.CompilerParams(
+            collective_id=3, has_side_effects=True, vmem_limit_bytes=56 << 20
+        ),
+        name="attend_back",
+    )(
+        gmid,
+        mixed,
+        rgrad,
+        ggrad,
+        x,
+        gain[None],
+        wq,
+        wk,
+        wv,
+        wo,
+        cos,
+        sin,
+        q,
+        kv,
+        lrow,
+        att,
+        lens,
+    )
 
 
 def shards(
@@ -491,100 +1192,23 @@
     seq_lens,
     cotangent,
 ):
-    tok_rows, model_width = inputs.shape
-    expert_ranks = lax.axis_size("expert")
-    expert_rank = lax.axis_index("expert")
-    total_rows = tok_rows * expert_ranks
+    n = lax.axis_size("expert")
+    nz = lax.axis_size("tensor")
+    tok_rows = inputs.shape[0]
     seq_count = seq_lens.shape[0]
-    seq_length = total_rows // seq_count
     span_rows = tok_rows // seq_count
     query_width = query_weight.shape[1]
     key_width = key_weight.shape[1]
-    query_heads = query_width // HD
-    key_heads = key_width // HD
-    groups = query_heads // key_heads
-    score_scale = HD ** (-0.5)
-    local_pos = expert_rank * span_rows + jnp.arange(span_rows, dtype=jnp.int32)
-    row_pos = jnp.tile(local_pos, seq_count)
-    key_block = math.gcd(seq_length, 2048)
-    last_pos = expert_rank * span_rows + span_rows - 1
-    used_blocks = last_pos // key_block + 1
-    residual = inputs.astype(f32)
-    norm_scale = lax.rsqrt(jnp.mean(residual * residual, -1, keepdims=True) + EPS)
-    normed = (residual * norm_scale * attention_gain).astype(bf16)
-    cosines, sine_table = rope_tables(row_pos, HD)
-    query_lin = jnp.dot(normed, query_weight, preferred_element_type=f32)
-    key_lin = jnp.dot(normed, key_weight, preferred_element_type=f32)
-    value_lin = jnp.dot(normed, value_weight, preferred_element_type=f32)
-    queries = rotate(
-        query_lin.reshape(tok_rows, query_heads, HD), cosines, sine_table, True
-    ).astype(bf16)
-    keys_rot = rotate(key_lin.reshape(tok_rows, key_heads, HD), cosines, sine_table, True).astype(
-        bf16
-    )
-    pair_local = jnp.concatenate(
-        [keys_rot.reshape(tok_rows, key_width), value_lin.astype(bf16)], -1
-    )
-    flat = lax.all_gather(pair_local, "expert", axis=0, tiled=True)
-    width_now = flat.shape[-1]
-    shaped = flat.reshape(expert_ranks, seq_count, span_rows, width_now).transpose(1, 0, 2, 3)
-    pairs_seq = shaped.reshape(seq_count, seq_length, width_now)
-    query_groups = queries.reshape(seq_count, span_rows, key_heads, groups, HD)
-
-    def block_scores(pairs_here, index):
-        start = index * key_block
-        pair_block = lax.dynamic_slice_in_dim(pairs_here, start, key_block, 1)
-        pos_block = start + jnp.arange(key_block, dtype=jnp.int32)
-        key_part = pair_block[..., :key_width].reshape(seq_count, key_block, key_heads, HD)
-        value_part = pair_block[..., key_width:].reshape(seq_count, key_block, key_heads, HD)
-        scores = (
-            jnp.einsum("sqhgd,skhd->shgqk", query_groups, key_part, preferred_element_type=f32)
-            * score_scale
-        )
-        allowed = (pos_block[None, None, :] <= local_pos[None, :, None]) & (
-            pos_block[None, None, :] < seq_lens[:, None, None]
-        )
-        return (scores, allowed[:, None, None], key_part, value_part)
-
-    def score_maxima(index, carry):
-        running_max, running_sum = carry
-        scores, allowed, _, _ = block_scores(pairs_seq, index)
-        scores = jnp.where(allowed, scores, -1e30)
-        new_max = jnp.maximum(running_max, jnp.max(scores, -1))
-        weights_now = jnp.where(allowed, jnp.exp(scores - new_max[..., None]), 0.0)
-        running_sum = running_sum * jnp.exp(running_max - new_max) + jnp.sum(weights_now, -1)
-        return (new_max, running_sum)
-
-    start_max = jnp.full((seq_count, key_heads, groups, span_rows), -1e30, f32)
-    row_max, row_sum = lax.fori_loop(
-        0, used_blocks, score_maxima, (start_max, jnp.zeros_like(start_max))
-    )
-    log_total = row_max + jnp.log(row_sum)
-
-    def value_sums(index, totals):
-        scores, allowed, _, value_part = block_scores(pairs_seq, index)
-        probs_low = jnp.where(allowed, jnp.exp(scores - log_total[..., None]), 0.0).astype(bf16)
-        return totals + jnp.einsum(
-            "shgqk,skhd->shgqd", probs_low, value_part, preferred_element_type=f32
-        )
-
-    attended_raw = lax.fori_loop(
-        0, used_blocks, value_sums, jnp.zeros((seq_count, key_heads, groups, span_rows, HD), f32)
-    )
-    attended = attended_raw.transpose(0, 3, 1, 2, 4).reshape(tok_rows, query_width).astype(bf16)
-    tensor_ranks = lax.axis_size("tensor")
-    tensor_rank = lax.axis_index("tensor")
-    own_count = tok_rows // tensor_ranks
-
-    def own_part(values):
-        return lax.dynamic_slice_in_dim(values, tensor_rank * own_count, own_count, 0)
-
+    experts = router_weight.shape[1]
+    local_pos = lax.axis_index("expert") * span_rows + jnp.arange(span_rows, dtype=jnp.int32)
+    frequency = THETA ** (-2.0 * jnp.arange(HD // 2, dtype=jnp.float32) / HD)
+    angles = local_pos.astype(f32)[:, None] * frequency[None, :]
+    cosines = jnp.tile(jnp.cos(angles), (seq_count, 4))
+    sines = jnp.tile(jnp.sin(angles), (seq_count, 4))
     cot_all = lax.all_gather(cotangent.astype(bf16), "expert", axis=0, tiled=True)
-    middle = own_part(residual) + lax.psum_scatter(
-        jnp.dot(attended, out_weight, preferred_element_type=f32),
-        "tensor",
-        scatter_dimension=0,
-        tiled=True,
+    weights = (query_weight, key_weight, value_weight, out_weight, cosines, sines)
+    middle, queries, pairs, logs, attended = attend_layer(
+        n, nz, inputs, attention_gain, *weights, seq_lens
     )
     (
         out_part,
@@ -594,10 +1218,10 @@
         expert_load,
         gate_grad,
         up_grad,
-        down_term,
+        down_grad,
     ) = expert_layer(
-        expert_ranks,
-        tensor_ranks,
+        n,
+        nz,
         middle,
         expert_gain,
         router_weight,
@@ -608,117 +1232,38 @@
         cotangent,
         cot_all,
     )
-    expert_load = expert_load[0]
-    balance_loss = jnp.mean(expert_load)
-    down_term = down_term.reshape(down_weight.shape)
-    output = lax.all_gather(out_part.astype(bf16), "tensor", axis=0, tiled=True).astype(f32)
-    grad_attn = lax.all_gather(grad_middle.astype(bf16), "tensor", axis=0, tiled=True)
-    out_weight_grad = jnp.dot(attended.T, grad_attn, preferred_element_type=f32)
-    grad_attended = jnp.dot(grad_attn, out_weight.T, preferred_element_type=f32).astype(bf16)
-    grad_og = grad_attended.reshape(seq_count, span_rows, key_heads, groups, HD)
-    delta = jnp.einsum("sqhgd,shgqd->shgq", grad_og.astype(f32), attended_raw)
-
-    def score_grads(index, carry):
-        query_acc, pair_buffer = carry
-        scores, allowed, key_part, value_part = block_scores(pairs_seq, index)
-        soft = jnp.where(allowed, jnp.exp(scores - log_total[..., None]), 0.0)
-        grad_probs = jnp.einsum(
-            "sqhgd,skhd->shgqk", grad_og, value_part, preferred_element_type=f32
-        )
-        grad_scores = (soft * (grad_probs - delta[..., None])).astype(bf16)
-        query_acc = query_acc + jnp.einsum(
-            "shgqk,skhd->sqhgd", grad_scores, key_part, preferred_element_type=f32
-        )
-        key_term = (
-            jnp.einsum("shgqk,sqhgd->skhd", grad_scores, query_groups, preferred_element_type=f32)
-            * score_scale
-        )
-        value_term = jnp.einsum(
-            "shgqk,sqhgd->skhd", soft.astype(bf16), grad_og, preferred_element_type=f32
-        )
-        block_terms = jnp.concatenate(
-            [
-                key_term.reshape(seq_count, -1, key_width),
-                value_term.reshape(seq_count, -1, key_width),
-            ],
-            -1,
-        )
-        pair_buffer = lax.dynamic_update_slice_in_dim(
-            pair_buffer, block_terms, index * key_block, 1
-        )
-        return (query_acc, pair_buffer)
-
-    grad_query_rot, seq_terms = lax.fori_loop(
-        0,
-        used_blocks,
-        score_grads,
-        (
-            jnp.zeros((seq_count, span_rows, key_heads, groups, HD), f32),
-            jnp.zeros((seq_count, seq_length, 2 * key_width), f32),
-        ),
+    output, input_grad, packed, small = return_layer(
+        n,
+        nz,
+        grad_middle,
+        out_part,
+        router_part,
+        expert_gain_part,
+        inputs,
+        attention_gain,
+        *weights,
+        queries,
+        pairs,
+        logs,
+        attended,
+        seq_lens,
     )
-    all_terms = seq_terms.reshape(seq_count, expert_ranks, span_rows, 2 * key_width).transpose(
-        1, 0, 2, 3
-    )
-    all_terms = all_terms.reshape(total_rows, 2 * key_width)
-    pair_grad = lax.psum_scatter(all_terms, "expert", scatter_dimension=0, tiled=True)
-    grad_query_rot = grad_query_rot.reshape(tok_rows, query_heads, HD) * score_scale
-    grad_query_lin = (
-        rotate(grad_query_rot, cosines, sine_table, False)
-        .reshape(tok_rows, query_width)
-        .astype(bf16)
-    )
-    grad_key_lin = (
-        rotate(
-            pair_grad[:, :key_width].reshape(tok_rows, key_heads, HD), cosines, sine_table, False
-        )
-        .reshape(tok_rows, key_width)
-        .astype(bf16)
-    )
-    grad_value_lin = pair_grad[:, key_width:].astype(bf16)
-    query_grad = jnp.dot(normed.T, grad_query_lin, preferred_element_type=f32)
-    key_grad = jnp.dot(normed.T, grad_key_lin, preferred_element_type=f32)
-    value_grad = jnp.dot(normed.T, grad_value_lin, preferred_element_type=f32)
-    grad_normed = lax.psum_scatter(
-        jnp.dot(grad_query_lin, query_weight.T, preferred_element_type=f32)
-        + jnp.dot(grad_key_lin, key_weight.T, preferred_element_type=f32)
-        + jnp.dot(grad_value_lin, value_weight.T, preferred_element_type=f32),
-        "tensor",
-        scatter_dimension=0,
-        tiled=True,
-    )
-    own_res = own_part(residual)
-    own_scale = own_part(norm_scale)
-    gained1 = grad_normed * attention_gain
-    attention_gain_part = jnp.sum(grad_normed * own_res * own_scale, 0)
-    input_part = (
-        grad_middle
-        + own_scale * gained1
-        - own_res * own_scale**3 * jnp.mean(gained1 * own_res, -1, keepdims=True)
-    )
-    input_grad = lax.all_gather(input_part.astype(bf16), "tensor", axis=0, tiled=True).astype(f32)
-    query_grad, key_grad, value_grad, out_weight_grad = lax.psum(
-        (query_grad, key_grad, value_grad, out_weight_grad), "expert"
-    )
-    attention_gain_grad, expert_gain_grad, router_grad = lax.psum(
-        (attention_gain_part, expert_gain_part[0], router_part), ("expert", "tensor")
-    )
-    router_grad = router_grad.T
+    cuts = (query_width, query_width + key_width, query_width + 2 * key_width)
     return (
         output,
         input_grad,
-        balance_loss,
-        expert_load,
-        attention_gain_grad,
-        query_grad,
-        key_grad,
-        value_grad,
-        out_weight_grad,
-        expert_gain_grad,
-        router_grad,
+        jnp.mean(expert_load),
+        expert_load[0],
+        small[experts + 1],
+        packed[:, : cuts[0]],
+        packed[:, cuts[0] : cuts[1]],
+        packed[:, cuts[1] : cuts[2]],
+        packed[:, cuts[2] :].T,
+        small[experts],
+        small[:experts].T,
         gate_grad,
         up_grad,
-        down_term,
+        down_grad.reshape(down_weight.shape),
     )
 
 

time: 700 us -> 377 us (0.54)
  waiting for transfers between devices: 318 us -> 5.62 us
  Pallas kernels: 174 us -> 326 us
  blocking collectives: 103 us -> 0 us
  local copies, waits for them, and re-layouts: 46.8 us -> 25 us
  matrix products: 20.6 us -> 0 us
  other arithmetic: 18.2 us -> 3.23 us
    pallas_call x0 -> x2, Pallas kernels: none -> 145 us  [the longest x1 104 us: return_layer(): pl.pallas_call(functools.partial(return_kernel, n, nz), out_shape=[sds((t...]
    reduce_scatter x3 -> x0, waiting for transfers between devices: 139 us -> none  [the longest x1 58.5 us: shards(): lax.psum_scatter(all_terms, 'expert', scatter_dimension=0, tiled=True)]
    psum x2 -> x0, waiting for transfers between devices: 109 us -> none  [the longest x1 95.5 us: shards(): lax.psum((attention_gain_part, expert_gain_part[0], router_part), ('exper...]
    all_gather x3 -> x0, blocking collectives: 64.4 us -> none  [the longest x1 26.4 us: shards(): lax.all_gather(grad_middle.astype(bf16), 'tensor', axis=0, tiled=True)]
    all_gather x1, waiting for transfers between devices: 45.2 us -> 5.6 us  [shards(): lax.all_gather(cotangent.astype(bf16), 'expert', axis=0, tiled=True)]
    psum x1 -> x0, blocking collectives: 38.9 us -> none  [shards(): lax.psum((attention_gain_part, expert_gain_part[0], router_part), ('exper...]
    all_gather x1 -> x0, waiting for transfers between devices: 24.5 us -> none  [shards(): flat = lax.all_gather(pair_local, 'expert', axis=0, tiled=True)]
    dot_general x19 -> x0, matrix products: 20.6 us -> none  [the longest x1 2.5 us: score_grads(): jnp.einsum('shgqk,skhd->sqhgd', grad_scores, key_part, preferred_element_...]
  transfers between devices with their start and end apart: 7 -> 1, of which waited for: 7 -> 1; matrix products, arithmetic and copies ran while one was open for 4% -> 1% of each run, Pallas kernels for 0% -> 11%
where the time goes in v3:
time: 377 us; the launch traced here: 376 us
  Pallas kernels  326 us (86%)
  local copies, waits for them, and re-layouts  25 us (7%)
  between operations  16.2 us (4%)
  waiting for transfers between devices  5.62 us (1%)
    pallas_call x1, Pallas kernels, expert_layer(): pl.pallas_call(functools.partial(expert_kernel, n, nz, big), out_shape=ou...  182 us
    pallas_call x1, Pallas kernels, return_layer(): pl.pallas_call(functools.partial(return_kernel, n, nz), out_shape=[sds((t...  104 us
    pallas_call x1, Pallas kernels, attend_layer(): pl.pallas_call(functools.partial(attend_kernel, n, nz), out_shape=[sds((r...  40 us
    unnamed x53, local copies, waits for them, and re-layouts  16.3 us
  transfers between devices with their start and end apart: 1, of which 1 were waited for; matrix products, arithmetic and copies ran while one was open for 1% of the time, Pallas kernels for 11%

profile of v3, /device:TPU:0, one launch (start us, length us, event | category | flops | bytes accessed | tf_op | source)
XLA Modules:
  0.0 376.1 jit_solution(15813252024799368213)
XLA Ops:
  7.2 2.4 convert_element_type.11
  9.7 0.8 copy.34.routes_ref
  11.6 0.8 copy.33.router_ref
  12.5 40.0 %attend.1 = (f32[96,1024]{1,0:T(8,128)S(1)}, bf16[384,256]{1,0:T(8,128)(2,1)S(1)}, bf16[2,1536,256]{2,1,0:T(8,128)(2,1)S(1)}, f32[4,8,384]{2,1,0:T(8,128)S(1)}, f32[384,256]{1,0:T(8,128)S(1)}) custom-call(bf16[384,1024]{1,0:T(8,128)(2,1)S(1)} %copy-done, f32[1,1024]{1,0:T(1,128)S(1)} %bitcast.16, bf16[1024,256]{1,0:T(8,128)(2,1)S(1)} %copy-done.1, ...), custom_call_target="tpu_custom_call" | custom-call | tf_op jit(solution)/shard_map/attend/pallas_call | solution.py:662
  52.6 1.1 copy-done.5
  53.7 0.7 copy-done.8
  54.5 0.7 copy-done.9
  55.2 0.7 copy-done.10
  55.9 0.6 copy-done.11
  56.5 5.6 %all-gather.2.cloned.1.call-done.cot_all = bf16[3072,1024]{1,0:T(8,128)(2,1)} async-done(((bf16[384,1024]{1,0:T(8,128)(2,1)}), bf16[3072,1024]{1,0:T(8,128)(2,1)}) %all-gather.2.cloned.1.call-update) | async-done | bytes 6291472 | tf_op jit(solution)/shard_map/all_gather | solution.py:1208
  62.1 181.6 %experts.1 = (f32[96,1024]{1,0:T(8,128)}, f32[96,1024]{1,0:T(8,128)}, f32[32,1024]{1,0:T(8,128)}, f32[1,1024]{1,0:T(1,128)}, f32[1,32]{1,0:T(1,128)}, /*index=5*...) custom-call(f32[96,1024]{1,0:T(8,128)} %copy-done.8, f32[1,1024]{1,0:T(1,128)} %bitcast.19, ...), custom_call_target="tpu_custom_call" | custom-call | tf_op jit(solution)/shard_map/experts/pallas_call | solution.py:445
  243.8 104.5 %attend_back.1 = (f32[384,1024]{1,0:T(8,128)}, f32[384,1024]{1,0:T(8,128)}, f32[1024,768]{1,0:T(8,128)}, f32[48,1024]{1,0:T(8,128)}) custom-call(f32[96,1024]{1,0:T(8,128)} %get-tuple-element.32.gmid_ref, f32[96,1024]{1,0:T(8,128)} %get-tuple-element.33.mixed_ref, f32[32,1024]{1,0:T(8,128)} %get-tuple-element.34.rgrad_ref, ...), custom_call_target="tpu_custom_call" | custom-call | tf_op jit(solution)/shard_map/attend_back/pallas_call | solution.py:1112
  348.2 1.4 fusion.1
  349.7 1.6 slice_bitcast_fusion.1
  351.2 2.2 fusion
  353.5 2.7 slice_bitcast_fusion
  356.7 1.3 copy.37
  358.8 1.1 copy.44
  360.0 1.1 copy.45
  362.1 1.3 copy.47
  363.5 1.0 copy-done.15
  364.5 1.3 copy.48
  365.8 1.0 copy-done.14
  366.8 1.3 copy.49
  (50 shorter events, 2.8 us)
Async XLA Ops:
  7.2 2.6 copy-start.20
  7.2 54.9 %all-gather.2.cloned.1.call-start = ((), (), s32[]{:S(2)}) async-start(), calls=%async_computation | async-start | bytes 7077888 | tf_op jit(solution)/shard_map/all_gather | solution.py:1208
  9.6 2.0 copy-start.19
  9.6 2.8 copy-start
  9.6 2.8 copy-start.1
  9.7 2.8 copy-start.2
  9.7 2.8 copy-start.6
  9.7 2.8 copy-start.7
  9.7 2.8 copy-start.12
  9.7 2.8 copy-start.13
  11.2 41.4 %copy-start.3 = (f32[384,128]{1,0:T(8,128)}, f32[384,128]{1,0:T(8,128)S(1)}, u32[]{:S(2)}) copy-start(f32[384,128]{1,0:T(8,128)S(1)} %copy.32.sin_ref) | copy-start | bytes 589828
  11.6 50.5 %copy-start.4 = (f32[384,128]{1,0:T(8,128)}, f32[384,128]{1,0:T(8,128)S(1)}, u32[]{:S(2)}) copy-start(f32[384,128]{1,0:T(8,128)S(1)} %copy.31.cos_ref) | copy-start | bytes 589828
  52.6 1.1 copy-start.5
  53.7 0.7 copy-start.8
  54.5 0.7 copy-start.9
  55.2 0.7 copy-start.10
  55.9 0.6 copy-start.11
  353.5 2.7 copy-start.21
  356.1 2.7 copy-start.18
  358.0 1.9 copy-start.17
  360.0 2.2 copy-start.16
  362.1 2.3 copy-start.15
  364.5 2.3 copy-start.14
Sparse Core Ops, SparseCore 0:
  10.5 51.6 all-gather.1

commit v4 on v3

--- a/solution.py
+++ b/solution.py
@@ -38,6 +38,37 @@
     )
 
 
+def turn(values, cos, sin, last, forward):
+    lane = lax.broadcasted_iota(jnp.int32, (values.shape[0], 128), 1)
+    first_half = lax.rem(lane, HD) < HD // 2
+    parts = []
+    for g in range(values.shape[1] // 128):
+        v = values[:, g * 128 : (g + 1) * 128]
+        if g * 128 >= last:
+            parts.append(v)
+            continue
+        turned = jnp.where(
+            first_half, -pltpu.roll(v, 128 - HD // 2, 1), pltpu.roll(v, HD // 2, 1)
+        )
+        new = v * cos + turned * sin if forward else v * cos - turned * sin
+        if (g + 1) * 128 > last:
+            new = jnp.where(lane + g * 128 < last, new, v)
+        parts.append(new)
+    return jnp.concatenate(parts, 1) if len(parts) > 1 else parts[0]
+
+
+def greet(n, nz, e, z, sib):
+    barrier = pltpu.get_barrier_semaphore()
+    pl.semaphore_signal(barrier, inc=1, device_id=(sib, z), device_id_type=MESH)
+    for s in range(1, n // 2):
+        pl.semaphore_signal(
+            barrier, inc=1, device_id=(lax.rem(e + 2 * s, n), z), device_id_type=MESH
+        )
+    for k in range(1, nz):
+        pl.semaphore_signal(barrier, inc=1, device_id=(e, lax.rem(z + k, nz)), device_id_type=MESH)
+    return barrier
+
+
 def expert_kernel(
     n,
     nz,
@@ -46,26 +77,27 @@
     gain_ref,
     router_ref,
     routes_ref,
-    gate_ref,
-    up_ref,
-    down_ref,
     cot_ref,
+    gate_hbm,
+    up_hbm,
+    down_hbm,
     cot_all,
     *rest,
 ):
     outs, rest = rest[:8], rest[8:]
-    out_ref, gmid_ref, rgrad_ref, ggrad_ref, load_ref, dgate, dup, ddown = outs
+    gmid_ref, rgrad_ref, ggrad_ref, load_ref, dgate_hbm, dup_hbm, ddown_hbm, mixed_hbm = outs
+    xbuf, rest = rest[0], rest[1:]
     if big:
-        xbuf, rest = rest[0], rest[1:]
         xstage, rest = rest[0], rest[1:]
-    else:
-        xbuf, rest = rest[0], rest[1:]
-        xstage = None
     (
         wbuf,
         xn_s,
         wg,
         wu,
+        down_ref,
+        dgate,
+        dup,
+        ddown,
         cbuf,
         dg_s,
         du_s,
@@ -73,11 +105,27 @@
         hold,
         osend,
         sin,
-        fbuf,
+        hold_o,
+        osend_o,
+        sin_o,
+        hold_g,
+        osend_g,
+        sin_g,
+        own_s,
+        own_g,
+        fsend,
         fin,
-        acc,
+        fsend_g,
+        fin_g,
         zsend,
         zin,
+        zsend_g,
+        zin_g,
+        wsem,
+        gsem,
+        csem,
+        msem,
+        lsem,
         zs,
         zr,
         zws,
@@ -90,37 +138,68 @@
         fr,
         wfs,
         wfr,
-        csem,
-        os_,
-        or_,
-        fsem,
-        frem,
+        gs,
+        gr,
+        oss,
+        osr,
+        ggs,
+        ggr,
+        ps,
+        pr,
+        pgs,
+        pgr,
         zgs,
         zgr,
-        lsem,
+        zggs,
+        zggr,
     ) = rest
     e = lax.axis_index("expert")
     z = lax.axis_index("tensor")
-    sib = e + 1 - 2 * lax.rem(e, 2)
+    core = lax.rem(e, 2)
+    other = 1 - core
+    me = e // 2
+    sib = e + 1 - 2 * core
     half = n // 2
     rows, width = mid_ref.shape
     tok = rows * nz
     experts = router_ref.shape[1]
-    local_experts, _, hid = gate_ref.shape
+    local_experts, _, hid = gate_hbm.shape
     inner_w = local_experts * hid
     fc = min(inner_w, 256)
-    slots = fbuf.shape[0]
-
-    barrier = pltpu.get_barrier_semaphore()
-    pl.semaphore_signal(barrier, inc=1, device_id=(sib, z), device_id_type=MESH)
-    for s in range(1, half):
-        pl.semaphore_signal(
-            barrier, inc=1, device_id=(lax.rem(e + 2 * s, n), z), device_id_type=MESH
-        )
-    for k in range(1, nz):
-        pl.semaphore_signal(barrier, inc=1, device_id=(e, lax.rem(z + k, nz)), device_id_type=MESH)
+    fslots = fsend.shape[0]
+
+    loads = []
+    for el in range(local_experts):
+        cols = pl.ds(el * hid, hid)
+        loads.append(pltpu.make_async_copy(gate_hbm.at[el], wg.at[:, cols], wsem.at[0, el]))
+        loads.append(pltpu.make_async_copy(up_hbm.at[el], wu.at[:, cols], wsem.at[1, el]))
+    loads.append(pltpu.make_async_copy(down_hbm, down_ref, wsem.at[2, 0]))
+    for copy in loads:
+        copy.start()
+
+    def piece_of(g):
+        return lax.rem(z + nz - g, nz)
+
+    def cot_start(g, parity, slot):
+        zz = piece_of(g)
+        for h in range(half):
+            start = (2 * h + parity) * tok + zz * rows
+            pltpu.make_async_copy(
+                cot_all.at[pl.ds(pl.multiple_of(start, 16), rows)],
+                cbuf.at[slot, pl.ds(h * rows, rows)],
+                csem.at[slot],
+            ).start()
+
+    def cot_wait(slot):
+        pltpu.make_async_copy(
+            cot_all.at[pl.ds(0, half * rows)], cbuf.at[slot], csem.at[slot]
+        ).wait()
+
+    cot_start(0, core, 0)
+    barrier = greet(n, nz, e, z, sib)
 
     own_rows = pl.ds(pl.multiple_of(z * rows, 16), rows)
+    my_rows = pl.ds(pl.multiple_of(me * rows, 16), rows)
     mid = mid_ref[...]
     scale2 = lax.rsqrt(jnp.mean(mid * mid, -1, keepdims=True) + EPS)
     xn = (mid * scale2 * gain_ref[...]).astype(bf16)
@@ -147,67 +226,62 @@
     psum = jnp.concatenate([jnp.sum(probs, 0, keepdims=True), lane_pad], 1)
     psum_hi = psum.astype(bf16).astype(f32)
     stats = jnp.concatenate([cnt, psum_hi, psum - psum_hi, jnp.zeros((13, 128), f32)], 0)
-    wbuf[e, z] = jnp.concatenate([piece, stats], 0).astype(bf16)
+    wbuf[z, core, me] = jnp.concatenate([piece, stats], 0).astype(bf16)
     if big:
-        copy = pltpu.make_async_copy(xn_s, xbuf.at[e, own_rows], lsem)
+        copy = pltpu.make_async_copy(xn_s, xbuf.at[z, core, my_rows], lsem)
         copy.start()
         copy.wait()
     else:
-        xbuf[e, own_rows] = xn
+        xbuf[z, core, my_rows] = xn
     pl.semaphore_wait(barrier, half + nz - 1)
 
+    def z_row(zz, k, to):
+        ref = xbuf.at[zz, core, my_rows]
+        return remote(ref, ref, zs.at[k - 1], zr.at[k - 1], (e, to))
+
+    def z_small(zz, k, to):
+        ref = wbuf.at[zz, core, me]
+        return remote(ref, ref, zws.at[k - 1], zwr.at[k - 1], (e, to))
+
+    def x_row(zz, h, g, s, to):
+        ref = xbuf.at[zz, core, pl.ds(pl.multiple_of(h * rows, 16), rows)]
+        return remote(ref, ref, xs.at[g, s], xr.at[g, s], (to, z))
+
+    def x_small(zz, h, g, s, to):
+        ref = wbuf.at[zz, core, h]
+        return remote(ref, ref, ws.at[g, s], wr.at[g, s], (to, z))
+
+    def push_piece(g):
+        zz = piece_of(g)
+        for s in range(1, half):
+            to = lax.rem(e + 2 * s, n)
+            x_row(zz, me, g, s, to).start()
+            x_small(zz, me, g, s, to).start()
+
+    push_piece(jnp.int32(0))
     for k in range(1, nz):
-        to = (e, lax.rem(z + k, nz))
-        piece_ref = xbuf.at[e, own_rows]
-        remote(piece_ref, piece_ref, zs.at[k - 1], zr.at[k - 1], to).start()
-        remote(wbuf.at[e, z], wbuf.at[e, z], zws.at[k - 1], zwr.at[k - 1], to).start()
-
-    def push_piece(zz):
-        piece_ref = xbuf.at[e, pl.ds(pl.multiple_of(zz * rows, 16), rows)]
-        small = wbuf.at[e, zz]
-        for s in range(1, half):
-            to = (lax.rem(e + 2 * s, n), z)
-            remote(piece_ref, piece_ref, xs.at[s], xr.at[s], to).start()
-            remote(small, small, ws.at[s], wr.at[s], to).start()
-        remote(piece_ref, piece_ref, fs.at[0], fr.at[0], (sib, z)).start()
-        remote(small, small, wfs.at[0], wfr.at[0], (sib, z)).start()
-
-    push_piece(z)
-
-    def cot_copy(index, slot):
-        start = pl.ds(pl.multiple_of(index * tok, 16), tok)
-        return pltpu.make_async_copy(cot_all.at[start], cbuf.at[slot], csem.at[slot])
-
-    cot_copy(e, 0).start()
-    for el in range(local_experts):
-        cols = slice(el * hid, (el + 1) * hid)
-        wg[:, cols] = gate_ref[el]
-        wu[:, cols] = up_ref[el]
+        z_row(z, k, lax.rem(z + k, nz)).start()
+        z_small(z, k, lax.rem(z + k, nz)).start()
+
     dgate[...] = jnp.zeros_like(dgate)
     dup[...] = jnp.zeros_like(dup)
     ddown[...] = jnp.zeros_like(ddown)
-
-    for k in range(1, nz):
-        zz = lax.rem(z + nz - k, nz)
-        piece_ref = xbuf.at[e, pl.ds(pl.multiple_of(zz * rows, 16), rows)]
-        peer = (e, zz)
-        remote(piece_ref, piece_ref, zs.at[k - 1], zr.at[k - 1], peer).wait_recv()
-        remote(wbuf.at[e, zz], wbuf.at[e, zz], zws.at[k - 1], zwr.at[k - 1], peer).wait_recv()
-        push_piece(zz)
+    for copy in loads:
+        copy.wait()
 
     sel_row = lax.broadcasted_iota(jnp.int32, (experts, fc), 0)
     sel_col = lax.broadcasted_iota(jnp.int32, (experts, fc), 1)
 
-    def block(index, slot, dst, dslot):
+    def block(zz, parity, slot, dst, dst_o, dst_g, dslot):
         if big:
-            copy = pltpu.make_async_copy(xbuf.at[index], xstage, lsem)
+            copy = pltpu.make_async_copy(xbuf.at[zz, parity], xstage, lsem)
             copy.start()
             copy.wait()
             x_ref = xstage
         else:
-            x_ref = xbuf.at[index]
+            x_ref = xbuf.at[zz, parity]
         c_ref = cbuf.at[slot]
-        sums = [jnp.zeros((experts, rows), f32) for _ in range(nz)]
+        sums = [jnp.zeros((experts, rows), f32) for _ in range(half)]
         for q in range(inner_w // fc):
             cols = slice(q * fc, (q + 1) * fc)
             x = x_ref[...]
@@ -218,7 +292,7 @@
                 sel_row == e * local_experts + (q * fc + sel_col) // hid, 1.0, 0.0
             ).astype(bf16)
             wide = jnp.concatenate(
-                [dot_tn(wbuf[index, zz, :experts, :], select)[:rows] for zz in range(nz)], 0
+                [dot_tn(wbuf[zz, parity, h, :experts, :], select)[:rows] for h in range(half)], 0
             )
             sig = 1.0 / (1.0 + jnp.exp(-gate_val))
             silu = gate_val * sig
@@ -228,19 +302,17 @@
             dg_s[:, cols] = (scaled * up_val * (sig * (1.0 + gate_val * (1.0 - sig)))).astype(bf16)
             du_s[:, cols] = (scaled * silu).astype(bf16)
             both = (inner * back).astype(bf16)
-            for zz in range(nz):
-                sums[zz] = sums[zz] + dot_nt(select, both[zz * rows : (zz + 1) * rows])
-        for zz in range(nz):
+            for h in range(half):
+                sums[h] = sums[h] + dot_nt(select, both[h * rows : (h + 1) * rows])
+        for h in range(half):
             gap = jnp.zeros((experts, 128 - rows), f32)
-            dst[dslot, tok : tok + experts, zz * 128 : (zz + 1) * 128] = jnp.concatenate(
-                [sums[zz], gap], 1
-            ).astype(bf16)
+            dst_g[dslot, h] = jnp.concatenate([sums[h], gap], 1).astype(bf16)
         for h in range(width // 256):
             cols = slice(h * 256, (h + 1) * 256)
-            dst[dslot, 0:tok, cols] = (
+            dst[dslot, :, cols] = (
                 dot_nt(dg_s[...], wg[cols, :]) + dot_nt(du_s[...], wu[cols, :])
             ).astype(bf16)
-            dst[dslot, tok + experts :, cols] = dot_nn(wi_s[...], down_ref[:, cols]).astype(bf16)
+            dst_o[dslot, :, cols] = dot_nn(wi_s[...], down_ref[:, cols]).astype(bf16)
         for h in range(width // 256):
             cols = slice(h * 256, (h + 1) * 256)
             x_part = x_ref[:, cols]
@@ -251,106 +323,181 @@
                 dup[el, cols, :] += up_part[:, el * hid : (el + 1) * hid]
             ddown[:, cols] += dot_tn(wi_s[...], c_ref[:, cols])
 
-    def finish(s):
-        slot = lax.rem(s, 2)
-        remote(osend.at[slot], sin.at[slot], os_.at[slot], or_.at[slot], (sib, z)).wait_recv()
-
-        @pl.when(s == 0)
+    def gives(slot):
+        return [
+            remote(osend.at[slot], sin.at[slot], gs.at[slot], gr.at[slot], (sib, z)),
+            remote(osend_g.at[slot], sin_g.at[slot], ggs.at[slot], ggr.at[slot], (sib, z)),
+            remote(osend_o.at[slot], sin_o.at[slot], oss.at[slot], osr.at[slot], (sib, z)),
+        ]
+
+    def finals(g, s, to):
+        at = lax.rem(g, fslots)
+        return [
+            remote(
+                fsend.at[at, s - 1], fin.at[g, s - 1], ps.at[g, s - 1], pr.at[g, s - 1], (to, z)
+            ),
+            remote(
+                fsend_g.at[at, s - 1],
+                fin_g.at[g, s - 1],
+                pgs.at[g, s - 1],
+                pgr.at[g, s - 1],
+                (to, z),
+            ),
+        ]
+
+    def lasts(k, to):
+        return [
+            remote(zsend.at[k - 1], zin.at[k - 1], zgs.at[k - 1], zgr.at[k - 1], (e, to)),
+            remote(zsend_g.at[k - 1], zin_g.at[k - 1], zggs.at[k - 1], zggr.at[k - 1], (e, to)),
+        ]
+
+    def mixed_copy(g, slot):
+        return pltpu.make_async_copy(hold_o.at[slot], mixed_hbm.at[piece_of(g)], msem.at[slot])
+
+    def plane_stage(g):
+        slot = lax.rem(g, 2)
+        for copy in gives(slot):
+            copy.wait_recv()
+        if fslots < nz:
+
+            @pl.when(g >= fslots)
+            def _():
+                for s in range(1, half):
+                    for copy in finals(g - fslots, s, sib):
+                        copy.wait_send()
+
+        spot = lax.rem(g, fslots)
+        for s in range(1, half):
+            h = lax.rem(me + half - s, half)
+            at = pl.ds(pl.multiple_of(h * rows, 16), rows)
+            fsend[spot, s - 1] = (hold[slot, at, :].astype(f32) + sin[slot, at, :].astype(f32)).astype(
+                bf16
+            )
+            fsend_g[spot, s - 1] = (hold_g[slot, h].astype(f32) + sin_g[slot, h].astype(f32)).astype(
+                bf16
+            )
+            for copy in finals(g, s, lax.rem(e - 2 * s + n, n)):
+                copy.start()
+        own_s[g] = hold[slot, my_rows, :].astype(f32) + sin[slot, my_rows, :].astype(f32)
+        own_g[g] = hold_g[slot, me].astype(f32) + sin_g[slot, me].astype(f32)
+        hold_o[slot] = (hold_o[slot].astype(f32) + sin_o[slot].astype(f32)).astype(bf16)
+        mixed_copy(g, slot).start()
+
+    def tensor_stage(g):
+        total = own_s[g]
+        total_g = own_g[g]
+        for s in range(1, half):
+            for copy in finals(g, s, sib):
+                copy.wait_recv()
+            total = total + fin[g, s - 1].astype(f32)
+            total_g = total_g + fin_g[g, s - 1].astype(f32)
+
+        @pl.when(g == 0)
         def _():
-            acc[...] = hold[slot].astype(f32) + sin[slot].astype(f32)
-
-        @pl.when(s > 0)
+            own_s[0] = total
+            own_g[0] = total_g
+
+        @pl.when(g > 0)
         def _():
-            fslot = lax.rem(s - 1, slots)
-            to = (lax.rem(e - 2 * s + n, n), z)
-            out = remote(fbuf.at[fslot], fin.at[s - 1], fsem.at[fslot], frem.at[s - 1], to)
-            if half - 1 > slots:
-
-                @pl.when(s - 1 >= slots)
-                def _():
-                    out.wait_send()
-
-            fbuf[fslot] = (hold[slot].astype(f32) + sin[slot].astype(f32)).astype(bf16)
-            out.start()
-
-    def step(s, carry):
-        own = lax.rem(e - 2 * s + n, n)
-        oth = lax.rem(sib - 2 * s + n, n)
-        slot = lax.rem(s, 2)
-
-        @pl.when(s > 0)
+            zsend[g - 1] = total.astype(bf16)
+            zsend_g[g - 1] = total_g.astype(bf16)
+            for copy in lasts(g, piece_of(g)):
+                copy.start()
+
+    def step(g, carry):
+        zz = piece_of(g)
+        slot = lax.rem(g, 2)
+
+        @pl.when(g < nz - 1)
         def _():
-            remote(xbuf.at[own], xbuf.at[own], xs.at[s], xr.at[s], (own, z)).wait_recv()
-            remote(wbuf.at[own], wbuf.at[own], ws.at[s], wr.at[s], (own, z)).wait_recv()
-            remote(xbuf.at[own], xbuf.at[own], fs.at[s], fr.at[s], (sib, z)).start()
-            remote(wbuf.at[own], wbuf.at[own], wfs.at[s], wfr.at[s], (sib, z)).start()
-
-        cot_copy(oth, 1).start()
-        cot_copy(own, 0).wait()
-        block(own, 0, hold, slot)
-
-        @pl.when(s < half - 1)
+            coming = piece_of(g + 1)
+            z_row(coming, g + 1, coming).wait_recv()
+            z_small(coming, g + 1, coming).wait_recv()
+            push_piece(g + 1)
+
+        for s in range(1, half):
+            h = lax.rem(me + half - s, half)
+            src = 2 * h + core
+            x_row(zz, h, g, s, src).wait_recv()
+            x_small(zz, h, g, s, src).wait_recv()
+        for copy in forward(zz, core, g):
+            copy.start()
+        cot_start(g, other, 1)
+        cot_wait(0)
+
+        @pl.when(g >= 2)
         def _():
-            cot_copy(lax.rem(e - 2 * s - 2 + n, n), 0).start()
-
-        @pl.when(s > 0)
+            mixed_copy(g - 2, slot).wait()
+
+        block(zz, core, 0, hold, hold_o, hold_g, slot)
+
+        @pl.when(g < nz - 1)
         def _():
-            finish(s - 1)
-
-        remote(xbuf.at[oth], xbuf.at[oth], fs.at[s], fr.at[s], (sib, z)).wait_recv()
-        remote(wbuf.at[oth], wbuf.at[oth], wfs.at[s], wfr.at[s], (sib, z)).wait_recv()
-        cot_copy(oth, 1).wait()
-        give = remote(osend.at[slot], sin.at[slot], os_.at[slot], or_.at[slot], (sib, z))
-
-        @pl.when(s >= 2)
+            cot_start(g + 1, core, 0)
+
+        @pl.when(g >= 2)
         def _():
-            give.wait_send()
-
-        block(oth, 1, osend, slot)
-        give.start()
+            tensor_stage(g - 2)
+
+        @pl.when(g >= 1)
+        def _():
+            plane_stage(g - 1)
+
+        @pl.when(g >= 2)
+        def _():
+            for copy in gives(slot):
+                copy.wait_send()
+
+        for copy in forward(zz, other, g):
+            copy.wait_recv()
+        cot_wait(1)
+        block(zz, other, 1, osend, osend_o, osend_g, slot)
+        for copy in gives(slot):
+            copy.start()
         return carry
 
-    lax.fori_loop(0, half, step, 0)
-    finish(jnp.int32(half - 1))
+    def forward(zz, parity, g):
+        ref = xbuf.at[zz, parity]
+        small = wbuf.at[zz, parity]
+        return (
+            remote(ref, ref, fs.at[g], fr.at[g], (sib, z)),
+            remote(small, small, wfs.at[g], wfr.at[g], (sib, z)),
+        )
+
+    lax.fori_loop(0, nz, step, 0)
+    grads = [
+        pltpu.make_async_copy(dgate, dgate_hbm, gsem.at[0]),
+        pltpu.make_async_copy(dup, dup_hbm, gsem.at[1]),
+        pltpu.make_async_copy(ddown, ddown_hbm, gsem.at[2]),
+    ]
+    plane_stage(jnp.int32(nz - 1))
+    for copy in grads:
+        copy.start()
+    if nz >= 2:
+        tensor_stage(jnp.int32(nz - 2))
 
     def total_stats(j, carry):
         for zz in range(nz):
-            carry = carry + wbuf[j, zz, experts:, :].astype(f32)
+            for parity in range(2):
+                carry = carry + wbuf[zz, parity, j, experts:, :].astype(f32)
         return carry
 
-    stats = lax.fori_loop(0, n, total_stats, jnp.zeros((16, 128), f32))
-    for s in range(1, half):
-        src = lax.rem(e + 2 * s, n)
-        fslot = (s - 1) % slots
-        remote(fbuf.at[fslot], fin.at[s - 1], fsem.at[fslot], frem.at[s - 1], (src, z)).wait_recv()
-        acc[...] += fin[s - 1].astype(f32)
-
-    def take(zz):
-        part = pl.ds(pl.multiple_of(zz * rows, 16), rows)
-        lane = pl.ds(pl.multiple_of(zz * 128, 128), 128)
-        low = pl.ds(pl.multiple_of(tok + experts + zz * rows, 16), rows)
-        return acc[part, :], acc[tok : tok + experts, lane], acc[low, :]
-
-    for k in range(1, nz):
-        zz = lax.rem(z + k, nz)
-        first, second, third = take(zz)
-        zsend[k - 1, 0:rows, :] = first.astype(bf16)
-        zsend[k - 1, rows : rows + experts, 0:128] = second.astype(bf16)
-        zsend[k - 1, rows + experts :, :] = third.astype(bf16)
-        remote(zsend.at[k - 1], zin.at[k - 1], zgs.at[k - 1], zgr.at[k - 1], (e, zz)).start()
-
-    grad_rows, gate_sums, mixed = take(z)
-    for k in range(1, nz):
-        remote(zsend.at[k - 1], zin.at[k - 1], zgs.at[k - 1], zgr.at[k - 1], (e, z)).wait_recv()
-        grad_rows = grad_rows + zin[k - 1, 0:rows, :].astype(f32)
-        gate_sums = gate_sums + zin[k - 1, rows : rows + experts, 0:128].astype(f32)
-        mixed = mixed + zin[k - 1, rows + experts :, :].astype(f32)
-
-    out_ref[...] = mid_ref[...] + mixed
+    stats = lax.fori_loop(0, half, total_stats, jnp.zeros((16, 128), f32))
     total_rows = n * tok
     share = stats[0:1, :experts] / (total_rows * routes_ref.shape[1])
-    load_ref[...] = experts * experts * share * ((stats[1:2, :experts] + stats[2:3, :experts]) / total_rows)
+    load_ref[...] = (
+        experts * experts * share * ((stats[1:2, :experts] + stats[2:3, :experts]) / total_rows)
+    )
     loss_w = experts * share / total_rows
+    tensor_stage(jnp.int32(nz - 1))
+
+    gate_sums = own_g[0]
+    grad_rows = own_s[0]
+    for k in range(1, nz):
+        for copy in lasts(k, z):
+            copy.wait_recv()
+        gate_sums = gate_sums + zin_g[k - 1].astype(f32)
+        grad_rows = grad_rows + zin[k - 1].astype(f32)
     grow = jnp.concatenate([gate_sums, jnp.zeros((128 - experts, 128), f32)], 0).T
     grad_gates = grow[:rows, :experts]
     grad_logits = comb * (grad_gates - jnp.sum(grad_gates * comb, -1, keepdims=True))
@@ -367,43 +514,51 @@
         - mid * (scale2 * scale2 * scale2) * jnp.mean(gained * mid, -1, keepdims=True)
     )
 
+    for copy in grads:
+        copy.wait()
     for k in range(1, nz):
-        piece_ref = xbuf.at[e, own_rows]
-        peer = (e, lax.rem(z + k, nz))
-        remote(piece_ref, piece_ref, zs.at[k - 1], zr.at[k - 1], peer).wait_send()
-        remote(wbuf.at[e, z], wbuf.at[e, z], zws.at[k - 1], zwr.at[k - 1], peer).wait_send()
-        remote(zsend.at[k - 1], zin.at[k - 1], zgs.at[k - 1], zgr.at[k - 1], peer).wait_send()
-    for s in range(half):
-        peer = (lax.rem(e + 2 * s, n), z) if s else (sib, z)
-        if s:
-            remote(xbuf.at[e], xbuf.at[e], xs.at[s], xr.at[s], peer).wait_send()
-            remote(wbuf.at[e], wbuf.at[e], ws.at[s], wr.at[s], peer).wait_send()
-        remote(xbuf.at[e], xbuf.at[e], fs.at[s], fr.at[s], (sib, z)).wait_send()
-        remote(wbuf.at[e], wbuf.at[e], wfs.at[s], wfr.at[s], (sib, z)).wait_send()
-    for s in range(max(0, half - 2), half):
-        slot = s % 2
-        remote(osend.at[slot], sin.at[slot], os_.at[slot], or_.at[slot], (sib, z)).wait_send()
-    for s in range(max(1, half - slots), half):
-        fslot = (s - 1) % slots
-        remote(fbuf.at[fslot], fin.at[s - 1], fsem.at[fslot], frem.at[s - 1], (sib, z)).wait_send()
+        z_row(z, k, z).wait_send()
+        z_small(z, k, z).wait_send()
+        for copy in lasts(k, z):
+            copy.wait_send()
+    for g in range(max(0, nz - 2), nz):
+        mixed_copy(jnp.int32(g), g % 2).wait()
+        for copy in gives(g % 2):
+            copy.wait_send()
+
+    def drained(g, carry):
+        for s in range(1, half):
+            x_row(z, me, g, s, sib).wait_send()
+            x_small(z, me, g, s, sib).wait_send()
+        for copy in forward(z, core, g):
+            copy.wait_send()
+        return carry
+
+    lax.fori_loop(0, nz, drained, 0)
+
+    def sums_sent(g, carry):
+        for s in range(1, half):
+            for copy in finals(g, s, sib):
+                copy.wait_send()
+        return carry
+
+    lax.fori_loop(nz - fslots, nz, sums_sent, 0)
 
 
 def expert_layer(n, nz, mid, gain, router, routes, gate, up, down, cot, cot_all):
     rows, width = mid.shape
-    tok = rows * nz
     experts = router.shape[1]
     local_experts, _, hid = gate.shape
     inner_w = local_experts * hid
     half = n // 2
+    batch = half * rows
     big = n > 8
-    slots = min(half - 1, 3)
-    pay = 2 * tok + experts
+    fslots = 2 if big else nz
     dma = pltpu.SemaphoreType.DMA
     vmem = pl.BlockSpec(memory_space=pltpu.VMEM)
     hbm = pl.BlockSpec(memory_space=pl.ANY)
     sds = jax.ShapeDtypeStruct
     out_shape = [
-        sds((rows, width), f32),
         sds((rows, width), f32),
         sds((experts, width), f32),
         sds((1, width), f32),
@@ -411,79 +566,73 @@
         sds((local_experts, width, hid), f32),
         sds((local_experts, width, hid), f32),
         sds((inner_w, width), f32),
+        sds((nz, batch, width), bf16),
     ]
-    out_specs = [vmem] * 8
+    out_specs = [vmem] * 4 + [hbm] * 4
     scratch = []
     if big:
-        out_shape.append(sds((n, tok, width), bf16))
+        out_shape.append(sds((nz, 2, batch, width), bf16))
         out_specs.append(hbm)
-        scratch.append(pltpu.VMEM((tok, width), bf16))
+        scratch.append(pltpu.VMEM((batch, width), bf16))
     else:
-        scratch.append(pltpu.VMEM((n, tok, width), bf16))
+        scratch.append(pltpu.VMEM((nz, 2, batch, width), bf16))
+    pair = pltpu.VMEM((2, batch, width), bf16)
+    small = pltpu.VMEM((2, half, experts, 128), bf16)
     scratch += [
-        pltpu.VMEM((n, nz, experts + 16, 128), bf16),
+        pltpu.VMEM((nz, 2, half, experts + 16, 128), bf16),
         pltpu.VMEM((rows, width), bf16),
         pltpu.VMEM((width, inner_w), bf16),
         pltpu.VMEM((width, inner_w), bf16),
-        pltpu.VMEM((2, tok, width), bf16),
-        pltpu.VMEM((tok, inner_w), bf16),
-        pltpu.VMEM((tok, inner_w), bf16),
-        pltpu.VMEM((tok, inner_w), bf16),
-        pltpu.VMEM((2, pay, width), bf16),
-        pltpu.VMEM((2, pay, width), bf16),
-        pltpu.VMEM((2, pay, width), bf16),
-        pltpu.VMEM((slots, pay, width), bf16),
-        pltpu.VMEM((half - 1, pay, width), bf16),
-        pltpu.VMEM((pay, width), f32),
-        pltpu.VMEM((nz - 1, 2 * rows + experts, width), bf16),
-        pltpu.VMEM((nz - 1, 2 * rows + experts, width), bf16),
+        pltpu.VMEM((inner_w, width), bf16),
+        pltpu.VMEM((local_experts, width, hid), f32),
+        pltpu.VMEM((local_experts, width, hid), f32),
+        pltpu.VMEM((inner_w, width), f32),
+        pair,
+        pltpu.VMEM((batch, inner_w), bf16),
+        pltpu.VMEM((batch, inner_w), bf16),
+        pltpu.VMEM((batch, inner_w), bf16),
+        pair,
+        pair,
+        pair,
+        pair,
+        pair,
+        pair,
+        small,
+        small,
+        small,
+        pltpu.VMEM((nz, rows, width), f32),
+        pltpu.VMEM((nz, experts, 128), f32),
+        pltpu.VMEM((fslots, half - 1, rows, width), bf16),
+        pltpu.VMEM((nz, half - 1, rows, width), bf16),
+        pltpu.VMEM((fslots, half - 1, experts, 128), bf16),
+        pltpu.VMEM((nz, half - 1, experts, 128), bf16),
+        pltpu.VMEM((nz - 1, rows, width), bf16),
+        pltpu.VMEM((nz - 1, rows, width), bf16),
+        pltpu.VMEM((nz - 1, experts, 128), bf16),
+        pltpu.VMEM((nz - 1, experts, 128), bf16),
+        dma((3, local_experts)),
+        dma((3,)),
+        dma((2,)),
+        dma((2,)),
+        dma,
     ]
     scratch += [dma((nz - 1,))] * 4
-    scratch += [dma((half,))] * 8
-    scratch += [dma((2,))] * 3
-    scratch += [dma((slots,)), dma((half - 1,)), dma((nz - 1,)), dma((nz - 1,)), dma]
+    scratch += [dma((nz, half))] * 4
+    scratch += [dma((nz,))] * 4
+    scratch += [dma((2,))] * 6
+    scratch += [dma((nz, half - 1))] * 4
+    scratch += [dma((nz - 1,))] * 4
     return pl.pallas_call(
         functools.partial(expert_kernel, n, nz, big),
         out_shape=out_shape,
-        in_specs=[vmem] * 8 + [hbm],
+        in_specs=[vmem] * 5 + [hbm] * 4,
         out_specs=out_specs,
         scratch_shapes=scratch,
         compiler_params=pltpu.CompilerParams(
-            collective_id=1, has_side_effects=True, vmem_limit_bytes=62 << 20
+            collective_id=1, has_side_effects=True, vmem_limit_bytes=60 << 20
         ),
         name="experts",
-    )(mid, gain[None], router, routes, gate, up, down.reshape(inner_w, width), cot, cot_all)[:8]
-
-
-def turn(values, cos, sin, last, forward):
-    lane = lax.broadcasted_iota(jnp.int32, (values.shape[0], 128), 1)
-    first_half = lax.rem(lane, HD) < HD // 2
-    parts = []
-    for g in range(values.shape[1] // 128):
-        v = values[:, g * 128 : (g + 1) * 128]
-        if g * 128 >= last:
-            parts.append(v)
-            continue
-        turned = jnp.where(
-            first_half, -pltpu.roll(v, 128 - HD // 2, 1), pltpu.roll(v, HD // 2, 1)
-        )
-        new = v * cos + turned * sin if forward else v * cos - turned * sin
-        if (g + 1) * 128 > last:
-            new = jnp.where(lane + g * 128 < last, new, v)
-        parts.append(new)
-    return jnp.concatenate(parts, 1) if len(parts) > 1 else parts[0]
-
-
-def greet(n, nz, e, z, sib):
-    barrier = pltpu.get_barrier_semaphore()
-    pl.semaphore_signal(barrier, inc=1, device_id=(sib, z), device_id_type=MESH)
-    for s in range(1, n // 2):
-        pl.semaphore_signal(
-            barrier, inc=1, device_id=(lax.rem(e + 2 * s, n), z), device_id_type=MESH
-        )
-    for k in range(1, nz):
-        pl.semaphore_signal(barrier, inc=1, device_id=(e, lax.rem(z + k, nz)), device_id_type=MESH)
-    return barrier
+    )(mid, gain[None], router, routes, cot, gate, up, down.reshape(inner_w, width), cot_all)[:8]
 
 
 def attend_kernel(
@@ -692,7 +841,7 @@
     n,
     nz,
     gmid_ref,
-    mixed_ref,
+    mid_ref,
     rgrad_ref,
     ggrad_ref,
     x_ref,
@@ -708,6 +857,7 @@
     lrow_ref,
     att_ref,
     lens_ref,
+    mixed_hbm,
     out_ref,
     igrad_ref,
     wsum_ref,
@@ -765,10 +915,19 @@
     sbr,
     scs,
     scr,
+    ofin,
+    ozs,
+    ozi,
+    ofs,
+    ofr,
+    ozsem,
+    ozrem,
+    olsem,
 ):
     e = lax.axis_index("expert")
     z = lax.axis_index("tensor")
     core = lax.rem(e, 2)
+    me = e // 2
     sib = e + 1 - 2 * core
     half = n // 2
     rows, width = gmid_ref.shape
@@ -785,7 +944,6 @@
     barrier = greet(n, nz, e, z, sib)
 
     gat[own_rows, :] = gmid_ref[...].astype(bf16)
-    obuf[own_rows, :] = mixed_ref[...].astype(bf16)
     sz1[z] = jnp.concatenate(
         [rgrad_ref[...], ggrad_ref[...], jnp.zeros((15, width), f32)], 0
     ).astype(bf16)
@@ -821,8 +979,32 @@
         copy.start()
     for copy in z_copies(slot_of(sz1), z1s, z1r):
         copy.start()
-    for copy in z_copies(part_of(obuf), zos, zor):
-        copy.start()
+    def mixed_send(t):
+        h = lax.rem(me + half - t, half)
+        return remote(
+            mixed_hbm.at[:, pl.ds(pl.multiple_of(h * rows, 16), rows), :],
+            ofin.at[t],
+            ofs.at[t - 1],
+            ofr.at[t - 1],
+            (lax.rem(e - 2 * t + n, n), z),
+        )
+
+    for t in range(1, half):
+        mixed_send(t).start()
+    mixed_own = pltpu.make_async_copy(
+        mixed_hbm.at[:, pl.ds(pl.multiple_of(me * rows, 16), rows), :], ofin.at[0], olsem
+    )
+    mixed_own.start()
+
+    def mixed_last(k):
+        to = (e, lax.rem(z + k, nz))
+        return remote(ozs.at[k - 1], ozi.at[k - 1], ozsem.at[k - 1], ozrem.at[k - 1], to)
+
+    def mixed_sum(zz):
+        total = ofin[0, zz].astype(f32)
+        for t in range(1, half):
+            total = total + ofin[t, zz].astype(f32)
+        return total
 
     wqkv[:, 0:qw] = wq_ref[...]
     wqkv[:, qw : qw + kw] = wk_ref[...]
@@ -842,6 +1024,13 @@
     kiota = lax.broadcasted_iota(jnp.int32, (ck, stacked), 0)
     qpos = e * span + lax.rem(lax.broadcasted_iota(jnp.int32, (ck, stacked), 1), span)
     for s in range(seqs):
+        if s == seqs - 1:
+            mixed_own.wait()
+            for t in range(1, half):
+                mixed_send(t).wait_recv()
+            for k in range(1, nz):
+                ozs[k - 1] = mixed_sum(lax.rem(z + k, nz)).astype(bf16)
+                mixed_last(k).start()
         for h in range(heads):
             srows = slice(s * span, (s + 1) * span)
 
@@ -923,6 +1112,12 @@
     out_grad = dot_tn(gat[...], att_ref[...].astype(bf16))
     for j in range(n):
         wpack[j, :, qw + 2 * kw :] = out_grad[j * dn : (j + 1) * dn].astype(bf16)
+
+    mixed = mid_ref[...] + mixed_sum(z)
+    for k in range(1, nz):
+        mixed_last(k).wait_recv()
+        mixed = mixed + ozi[k - 1].astype(f32)
+    obuf[own_rows, :] = mixed.astype(bf16)
 
     key_send(0).wait_recv()
     own_kv = [key_rows(e, s) + kvi[0, s].astype(f32) for s in range(seqs)]
@@ -941,6 +1136,8 @@
     sz2[z] = jnp.concatenate([again, jnp.zeros((15, width), f32)], 0).astype(bf16)
     for copy in z_copies(slot_of(sz2), z2s, z2r):
         copy.start()
+    for copy in z_copies(part_of(obuf), zos, zor):
+        copy.start()
 
     lin_grad = dot_tn(normed, glin)
     for j in range(n):
@@ -1000,7 +1197,6 @@
         copy.start()
 
     small_sib.wait_recv()
-    me = e // 2
     schip[me] = (sown[...].astype(f32) + ssib[...].astype(f32)).astype(bf16)
 
     def small_send(t):
@@ -1073,6 +1269,10 @@
     for k in range(1, nz):
         remote(zsend.at[k - 1], zin.at[k - 1], zps.at[k - 1], zpr.at[k - 1], (e, z)).wait_send()
     small_sib.wait_send()
+    for t in range(1, half):
+        mixed_send(t).wait_send()
+    for k in range(1, nz):
+        mixed_last(k).wait_send()
 
     def drained(t, carry):
         key_send(t).wait_send()
@@ -1092,7 +1292,7 @@
 
 
 def return_layer(
-    n, nz, gmid, mixed, rgrad, ggrad, x, gain, wq, wk, wv, wo, cos, sin, q, kv, lrow, att, lens
+    n, nz, gmid, mid, rgrad, ggrad, x, gain, wq, wk, wv, wo, cos, sin, q, kv, lrow, att, lens, mixed
 ):
     tok, width = x.shape
     rows = tok // nz
@@ -1117,7 +1317,8 @@
             sds((width, pack), f32),
             sds((small_rows, width), f32),
         ],
-        in_specs=[vmem] * 16 + [pl.BlockSpec(memory_space=pltpu.SMEM)],
+        in_specs=[vmem] * 16
+        + [pl.BlockSpec(memory_space=pltpu.SMEM), pl.BlockSpec(memory_space=pl.ANY)],
         out_specs=[vmem] * 4,
         scratch_shapes=[
             pltpu.VMEM((width, qw + 2 * kw), bf16),
@@ -1150,14 +1351,24 @@
         + [hdma, hdma, fdma, fdma]
         + [hdma, hdma, fdma, fdma]
         + [hdma] * 4
-        + [dma, dma, fdma, fdma],
+        + [dma, dma, fdma, fdma]
+        + [
+            pltpu.VMEM((half, nz, rows, width), bf16),
+            pltpu.VMEM((nz - 1, rows, width), bf16),
+            pltpu.VMEM((nz - 1, rows, width), bf16),
+            fdma,
+            fdma,
+            zdma,
+            zdma,
+            dma,
+        ],
         compiler_params=pltpu.CompilerParams(
             collective_id=3, has_side_effects=True, vmem_limit_bytes=56 << 20
         ),
         name="attend_back",
     )(
         gmid,
-        mixed,
+        mid,
         rgrad,
         ggrad,
         x,
@@ -1173,6 +1384,7 @@
         lrow,
         att,
         lens,
+        mixed,
     )
 
 
@@ -1211,7 +1423,6 @@
         n, nz, inputs, attention_gain, *weights, seq_lens
     )
     (
-        out_part,
         grad_middle,
         router_part,
         expert_gain_part,
@@ -1219,6 +1430,7 @@
         gate_grad,
         up_grad,
         down_grad,
+        mixed,
     ) = expert_layer(
         n,
         nz,
@@ -1236,7 +1448,7 @@
         n,
         nz,
         grad_middle,
-        out_part,
+        middle,
         router_part,
         expert_gain_part,
         inputs,
@@ -1247,6 +1459,7 @@
         logs,
         attended,
         seq_lens,
+        mixed,
     )
     cuts = (query_width, query_width + key_width, query_width + 2 * key_width)
     return (

time: 377 us -> 307 us (0.81)
  Pallas kernels: 326 us -> 254 us
    pallas_call x1, Pallas kernels: 182 us -> 99.3 us  [expert_layer(): pl.pallas_call(functools.partial(expert_kernel, n, nz, big), out_shape=ou...]
    pallas_call x1, Pallas kernels: 104 us -> 115 us  [return_layer(): pl.pallas_call(functools.partial(return_kernel, n, nz), out_shape=[sds((t...]
  transfers between devices with their start and end apart: 1 -> 1, of which waited for: 1 -> 1; matrix products, arithmetic and copies ran while one was open for 1% -> 1% of each run, Pallas kernels for 11% -> 13%
where the time goes in v4:
time: 307 us; the launch traced here: 304 us
  Pallas kernels  254 us (83%)
  local copies, waits for them, and re-layouts  25 us (8%)
  between operations  16.2 us (5%)
  waiting for transfers between devices  5.8 us (2%)
  other arithmetic  3.23 us (1%)
    pallas_call x1, Pallas kernels, return_layer(): pl.pallas_call(functools.partial(return_kernel, n, nz), out_shape=[sds((t...  115 us
    pallas_call x1, Pallas kernels, expert_layer(): pl.pallas_call(functools.partial(expert_kernel, n, nz, big), out_shape=ou...  99.3 us
    pallas_call x1, Pallas kernels, attend_layer(): pl.pallas_call(functools.partial(attend_kernel, n, nz), out_shape=[sds((r...  39.9 us
    unnamed x53, local copies, waits for them, and re-layouts  16.3 us
  transfers between devices with their start and end apart: 1, of which 1 were waited for; matrix products, arithmetic and copies ran while one was open for 1% of the time, Pallas kernels for 13%

profile of v4, /device:TPU:0, one launch (start us, length us, event | category | flops | bytes accessed | tf_op | source)
XLA Modules:
  0.0 304.2 jit_solution(13961937907635513181)
XLA Ops:
  7.2 2.4 convert_element_type.11
  9.7 0.8 copy.34.routes_ref
  11.6 0.8 copy.33.router_ref
  12.5 39.9 %attend.1 = (f32[96,1024]{1,0:T(8,128)S(1)}, bf16[384,256]{1,0:T(8,128)(2,1)S(1)}, bf16[2,1536,256]{2,1,0:T(8,128)(2,1)S(1)}, f32[4,8,384]{2,1,0:T(8,128)S(1)}, f32[384,256]{1,0:T(8,128)S(1)}) custom-call(bf16[384,1024]{1,0:T(8,128)(2,1)S(1)} %copy-done, f32[1,1024]{1,0:T(1,128)S(1)} %bitcast.16, bf16[1024,256]{1,0:T(8,128)(2,1)S(1)} %copy-done.1, ...), custom_call_target="tpu_custom_call" | custom-call | tf_op jit(solution)/shard_map/attend/pallas_call | solution.py:811
  52.4 0.7 copy-done.5
  53.2 1.1 copy-done.6
  54.3 0.7 copy-done.9
  55.1 0.7 copy-done.10
  55.7 0.6 copy-done.11
  56.4 5.8 %all-gather.2.cloned.1.call-done.cot_all = bf16[3072,1024]{1,0:T(8,128)(2,1)} async-done(((bf16[384,1024]{1,0:T(8,128)(2,1)}), bf16[3072,1024]{1,0:T(8,128)(2,1)}) %all-gather.2.cloned.1.call-update) | async-done | bytes 6291472 | tf_op jit(solution)/shard_map/all_gather | solution.py:1420
  62.1 99.3 %experts.1 = (f32[96,1024]{1,0:T(8,128)}, f32[32,1024]{1,0:T(8,128)}, f32[1,1024]{1,0:T(1,128)}, f32[1,32]{1,0:T(1,128)}, f32[4,1024,128]{2,1,0:T(8,128)}, /*ind...) custom-call(f32[96,1024]{1,0:T(8,128)} %copy-done.5, f32[1,1024]{1,0:T(1,128)} %bitcast.19, ...), custom_call_target="tpu_custom_call" | custom-call | tf_op jit(solution)/shard_map/experts/pallas_call | solution.py:625
  161.5 114.8 %attend_back.1 = (f32[384,1024]{1,0:T(8,128)}, f32[384,1024]{1,0:T(8,128)}, f32[1024,768]{1,0:T(8,128)}, f32[48,1024]{1,0:T(8,128)}) custom-call(f32[96,1024]{1,0:T(8,128)} %get-tuple-element.32.gmid_ref, f32[96,1024]{1,0:T(8,128)} %copy-done.5, f32[32,1024]{1,0:T(8,128)} %get-tuple-element.33.rgrad_ref, f32[1,1024]{1,0:T(1,128)} %get-tuple-element.34.ggrad_ref, ...), custom_call_target="tpu_custom_call" | custom-call | tf_op jit(solution)/shard_map/attend_back/pallas_call | solution.py:1312
  276.3 1.4 fusion.1
  277.8 1.6 slice_bitcast_fusion.1
  279.3 2.2 fusion
  281.6 2.7 slice_bitcast_fusion
  284.8 1.3 copy.37
  286.9 1.1 copy.44
  288.1 1.1 copy.45
  290.2 1.3 copy.47
  291.6 1.0 copy-done.15
  292.6 1.3 copy.48
  293.9 1.0 copy-done.14
  294.9 1.3 copy.49
  (50 shorter events, 2.8 us)
Async XLA Ops:
  7.2 2.6 copy-start.20
  7.2 54.9 %all-gather.2.cloned.1.call-start = ((), (), s32[]{:S(2)}) async-start(), calls=%async_computation | async-start | bytes 7077888 | tf_op jit(solution)/shard_map/all_gather | solution.py:1420
  9.6 2.0 copy-start.19
  9.6 2.8 copy-start
  9.6 2.8 copy-start.1
  9.7 2.8 copy-start.2
  9.7 2.8 copy-start.7
  9.7 2.8 copy-start.8
  9.7 2.8 copy-start.12
  9.7 2.8 copy-start.13
  11.2 41.2 %copy-start.3 = (f32[384,128]{1,0:T(8,128)}, f32[384,128]{1,0:T(8,128)S(1)}, u32[]{:S(2)}) copy-start(f32[384,128]{1,0:T(8,128)S(1)} %copy.32.sin_ref) | copy-start | bytes 589828
  11.6 149.9 %copy-start.4 = (f32[384,128]{1,0:T(8,128)}, f32[384,128]{1,0:T(8,128)S(1)}, u32[]{:S(2)}) copy-start(f32[384,128]{1,0:T(8,128)S(1)} %copy.31.cos_ref) | copy-start | bytes 589828
  52.4 0.7 copy-start.5
  53.2 1.1 copy-start.6
  54.3 0.7 copy-start.9
  55.1 0.7 copy-start.10
  55.7 0.6 copy-start.11
  281.6 2.7 copy-start.21
  284.2 2.7 copy-start.18
  286.1 1.9 copy-start.17
  288.1 2.2 copy-start.16
  290.2 2.3 copy-start.15
  292.6 2.3 copy-start.14
Sparse Core Ops, SparseCore 0:
  10.5 51.6 all-gather.1

commit v5 on v4

--- a/solution.py
+++ b/solution.py
@@ -84,8 +84,9 @@
     cot_all,
     *rest,
 ):
-    outs, rest = rest[:8], rest[8:]
-    gmid_ref, rgrad_ref, ggrad_ref, load_ref, dgate_hbm, dup_hbm, ddown_hbm, mixed_hbm = outs
+    outs, rest = rest[:9], rest[9:]
+    gmid_ref, glog_ref, ggrad_ref, load_ref = outs[:4]
+    dgate_hbm, dup_hbm, ddown_hbm, mixed_hbm, normed_hbm = outs[4:]
     xbuf, rest = rest[0], rest[1:]
     if big:
         xstage, rest = rest[0], rest[1:]
@@ -469,6 +470,7 @@
         pltpu.make_async_copy(dgate, dgate_hbm, gsem.at[0]),
         pltpu.make_async_copy(dup, dup_hbm, gsem.at[1]),
         pltpu.make_async_copy(ddown, ddown_hbm, gsem.at[2]),
+        pltpu.make_async_copy(xbuf.at[:, core, my_rows, :], normed_hbm, gsem.at[3]),
     ]
     plane_stage(jnp.int32(nz - 1))
     for copy in grads:
@@ -503,7 +505,10 @@
     grad_logits = comb * (grad_gates - jnp.sum(grad_gates * comb, -1, keepdims=True))
     grad_logits = grad_logits + probs * (loss_w - jnp.sum(loss_w * probs, -1, keepdims=True))
     low_grad = grad_logits.astype(bf16)
-    rgrad_ref[...] = dot_tn(low_grad, xn_s[...])
+    wide_grad = jnp.concatenate([grad_logits, jnp.zeros((rows, 128 - experts), f32)], 1)
+    if rows < 128:
+        wide_grad = jnp.concatenate([wide_grad, jnp.zeros((128 - rows, 128), f32)], 0)
+    glog_ref[...] = wide_grad.T[:experts].astype(bf16)
     grad_rows = grad_rows + dot_nt(low_grad, router_ref[...])
     mid = mid_ref[...]
     ggrad_ref[...] = jnp.sum(grad_rows * mid * scale2, 0, keepdims=True)
@@ -560,15 +565,16 @@
     sds = jax.ShapeDtypeStruct
     out_shape = [
         sds((rows, width), f32),
-        sds((experts, width), f32),
+        sds((experts, 128), bf16),
         sds((1, width), f32),
         sds((1, experts), f32),
         sds((local_experts, width, hid), f32),
         sds((local_experts, width, hid), f32),
         sds((inner_w, width), f32),
         sds((nz, batch, width), bf16),
+        sds((nz, rows, width), bf16),
     ]
-    out_specs = [vmem] * 4 + [hbm] * 4
+    out_specs = [vmem] * 4 + [hbm] * 5
     scratch = []
     if big:
         out_shape.append(sds((nz, 2, batch, width), bf16))
@@ -611,7 +617,7 @@
         pltpu.VMEM((nz - 1, experts, 128), bf16),
         pltpu.VMEM((nz - 1, experts, 128), bf16),
         dma((3, local_experts)),
-        dma((3,)),
+        dma((4,)),
         dma((2,)),
         dma((2,)),
         dma,
@@ -632,7 +638,7 @@
             collective_id=1, has_side_effects=True, vmem_limit_bytes=60 << 20
         ),
         name="experts",
-    )(mid, gain[None], router, routes, cot, gate, up, down.reshape(inner_w, width), cot_all)[:8]
+    )(mid, gain[None], router, routes, cot, gate, up, down.reshape(inner_w, width), cot_all)[:9]
 
 
 def attend_kernel(
@@ -842,8 +848,9 @@
     nz,
     gmid_ref,
     mid_ref,
-    rgrad_ref,
+    glog_ref,
     ggrad_ref,
+    xn_ref,
     x_ref,
     gain_ref,
     wq_ref,
@@ -858,14 +865,13 @@
     att_ref,
     lens_ref,
     mixed_hbm,
-    out_ref,
-    igrad_ref,
-    wsum_ref,
+    obuf,
+    igbuf,
+    wall,
+    wall2,
     small_ref,
     wqkv,
     gat,
-    obuf,
-    igbuf,
     datt,
     dq_s,
     acc_q,
@@ -875,18 +881,20 @@
     kvf,
     kvr,
     part,
-    zsend,
-    zin,
-    wpack,
-    wsi,
-    wsf,
-    wsr,
-    wall,
+    sums,
+    osums,
+    csend,
+    crecv,
+    osend,
+    orecv,
+    wbufs,
+    wbufs2,
     sz1,
     sz2,
     sown,
     ssib,
     schip,
+    ofin,
     zas,
     zar,
     zos,
@@ -895,6 +903,8 @@
     zir,
     zps,
     zpr,
+    zqs,
+    zqr,
     z1s,
     z1r,
     z2s,
@@ -903,25 +913,14 @@
     kor,
     kfs,
     kfr,
-    wos,
-    wor,
-    wfs,
-    wfr,
-    was,
-    war,
-    wbs,
-    wbr,
+    wsems,
+    wsems2,
     sbs,
     sbr,
     scs,
     scr,
-    ofin,
-    ozs,
-    ozi,
     ofs,
     ofr,
-    ozsem,
-    ozrem,
     olsem,
 ):
     e = lax.axis_index("expert")
@@ -939,15 +938,27 @@
     heads = kw // HD
     groups = qw // kw
     dn = width // n
-    experts = rgrad_ref.shape[0]
+    experts = glog_ref.shape[0]
     own_rows = pl.ds(pl.multiple_of(z * rows, 16), rows)
     barrier = greet(n, nz, e, z, sib)
+    w1 = PlaneSum(n, e, z, sib, wall, *wbufs, *wsems)
+    w2 = PlaneSum(n, e, z, sib, wall2, *wbufs2, *wsems2)
 
     gat[own_rows, :] = gmid_ref[...].astype(bf16)
-    sz1[z] = jnp.concatenate(
-        [rgrad_ref[...], ggrad_ref[...], jnp.zeros((15, width), f32)], 0
-    ).astype(bf16)
+    sz1[z] = glog_ref[...]
     pl.semaphore_wait(barrier, half + nz - 1)
+
+    def part_of(ref):
+        return lambda zz: ref.at[pl.ds(pl.multiple_of(zz * rows, 16), rows)]
+
+    def slot_of(ref):
+        return lambda zz: ref.at[zz]
+
+    gat_line = Line(z, nz, e, part_of(gat), zas, zar)
+    out_line = Line(z, nz, e, part_of(obuf), zos, zor)
+    igrad_line = Line(z, nz, e, part_of(igbuf), zis, zir)
+    normed_sum = LineSum(z, nz, e, csend, crecv, zps, zpr)
+    out_sum = LineSum(z, nz, e, osend, orecv, zqs, zqr)
 
     def z_copies(buf_of, send, recv):
         return [
@@ -969,16 +980,10 @@
             for k in range(1, nz)
         ]
 
-    def part_of(ref):
-        return lambda zz: ref.at[pl.ds(pl.multiple_of(zz * rows, 16), rows)]
-
-    def slot_of(ref):
-        return lambda zz: ref.at[zz]
-
-    for copy in z_copies(part_of(gat), zas, zar):
-        copy.start()
+    gat_line.start()
     for copy in z_copies(slot_of(sz1), z1s, z1r):
         copy.start()
+
     def mixed_send(t):
         h = lax.rem(me + half - t, half)
         return remote(
@@ -996,10 +1001,6 @@
     )
     mixed_own.start()
 
-    def mixed_last(k):
-        to = (e, lax.rem(z + k, nz))
-        return remote(ozs.at[k - 1], ozi.at[k - 1], ozsem.at[k - 1], ozrem.at[k - 1], to)
-
     def mixed_sum(zz):
         total = ofin[0, zz].astype(f32)
         for t in range(1, half):
@@ -1014,8 +1015,8 @@
     normed = (x * scale1 * gain_ref[...]).astype(bf16)
     dkv[...] = jnp.zeros_like(dkv)
 
-    for copy in z_arrivals(part_of(gat), zas, zar):
-        copy.wait_recv()
+    for hop in range(1, nz):
+        gat_line.hop(hop)
     datt[...] = dot_nt(gat[...], wo_ref[...]).astype(bf16)
 
     ck = 2 * span
@@ -1024,13 +1025,6 @@
     kiota = lax.broadcasted_iota(jnp.int32, (ck, stacked), 0)
     qpos = e * span + lax.rem(lax.broadcasted_iota(jnp.int32, (ck, stacked), 1), span)
     for s in range(seqs):
-        if s == seqs - 1:
-            mixed_own.wait()
-            for t in range(1, half):
-                mixed_send(t).wait_recv()
-            for k in range(1, nz):
-                ozs[k - 1] = mixed_sum(lax.rem(z + k, nz)).astype(bf16)
-                mixed_last(k).start()
         for h in range(heads):
             srows = slice(s * span, (s + 1) * span)
 
@@ -1101,23 +1095,32 @@
         key_final(t).start()
         return carry
 
+    cos, sin = cos_ref[...], sin_ref[...]
+    gq = turn(dq_s[...], cos, sin, qw, False).astype(bf16)
+    query_part = dot_tn(normed, gq)
+    out_part = dot_tn(gat[...], att_ref[...].astype(bf16))
+    for j in range(n):
+        w1.pack[j, :, :qw] = query_part[j * dn : (j + 1) * dn].astype(bf16)
+        w1.pack[j, :, qw:] = out_part[j * dn : (j + 1) * dn].astype(bf16)
     lax.fori_loop(0, half - 1, key_pass, 0)
-
+    w1.give()
+
+    mixed_own.wait()
+    for t in range(1, half):
+        mixed_send(t).wait_recv()
+    out_sum.hop(0, mixed_sum)
+    w1.spread()
     for copy in z_arrivals(slot_of(sz1), z1s, z1r):
         copy.wait_recv()
-    first = sz1[0].astype(f32)
+    rgrad = dot_nn(sz1[0][:, :rows], xn_ref[0])
     for zz in range(1, nz):
-        first = first + sz1[zz].astype(f32)
-
-    out_grad = dot_tn(gat[...], att_ref[...].astype(bf16))
-    for j in range(n):
-        wpack[j, :, qw + 2 * kw :] = out_grad[j * dn : (j + 1) * dn].astype(bf16)
-
-    mixed = mid_ref[...] + mixed_sum(z)
-    for k in range(1, nz):
-        mixed_last(k).wait_recv()
-        mixed = mixed + ozi[k - 1].astype(f32)
-    obuf[own_rows, :] = mixed.astype(bf16)
+        rgrad = rgrad + dot_nn(sz1[zz][:, :rows], xn_ref[zz])
+    sown[0:experts, :] = rgrad.astype(bf16)
+    for hop in range(1, nz - 1):
+        out_sum.hop(hop, mixed_sum)
+    out_sum.total(osums, mixed_sum)
+    obuf[own_rows, :] = (mid_ref[...] + osums[...]).astype(bf16)
+    out_line.start()
 
     key_send(0).wait_recv()
     own_kv = [key_rows(e, s) + kvi[0, s].astype(f32) for s in range(seqs)]
@@ -1125,65 +1128,33 @@
         key_final(t).wait_recv()
         for s in range(seqs):
             own_kv[s] = own_kv[s] + kvr[t - 1, s].astype(f32)
-    lin = jnp.concatenate([dq_s[...], jnp.concatenate(own_kv, 0)], 1)
-    glin = turn(lin, cos_ref[...], sin_ref[...], qw + kw, False).astype(bf16)
-    part[...] = dot_nt(glin, wqkv[...])
-    for k in range(1, nz):
-        zz = lax.rem(z + k, nz)
-        zsend[k - 1] = part[pl.ds(pl.multiple_of(zz * rows, 16), rows), :].astype(bf16)
-        remote(zsend.at[k - 1], zin.at[k - 1], zps.at[k - 1], zpr.at[k - 1], (e, zz)).start()
-    again = jnp.sum(part[...] * x * scale1, 0, keepdims=True)
-    sz2[z] = jnp.concatenate([again, jnp.zeros((15, width), f32)], 0).astype(bf16)
-    for copy in z_copies(slot_of(sz2), z2s, z2r):
-        copy.start()
-    for copy in z_copies(part_of(obuf), zos, zor):
-        copy.start()
-
-    lin_grad = dot_tn(normed, glin)
-    for j in range(n):
-        wpack[j, :, : qw + 2 * kw] = lin_grad[j * dn : (j + 1) * dn].astype(bf16)
-
-    def weight_send(t):
-        oth = lax.rem(sib - 2 * t + n, n)
-        return remote(wpack.at[oth], wsi.at[t], wos.at[t], wor.at[t], (sib, z))
-
-    def weight_final(t):
-        to = (lax.rem(e - 2 * t + n, n), z)
-        return remote(wsf.at[t - 1], wsr.at[t - 1], wfs.at[t - 1], wfr.at[t - 1], to)
-
-    def weight_give(i, carry):
-        weight_send(half - 1 - i).start()
-        return carry
-
-    lax.fori_loop(0, half, weight_give, 0)
-
-    def weight_pass(i, carry):
-        t = half - 1 - i
-        weight_send(t).wait_recv()
-        own = lax.rem(e - 2 * t + n, n)
-        wsf[t - 1] = (wpack[own].astype(f32) + wsi[t].astype(f32)).astype(bf16)
-        weight_final(t).start()
-        return carry
-
-    lax.fori_loop(0, half - 1, weight_pass, 0)
-
-    for copy in z_arrivals(slot_of(sz2), z2s, z2r):
-        copy.wait_recv()
-    second = sz2[0].astype(f32)
-    for zz in range(1, nz):
-        second = second + sz2[zz].astype(f32)
-    sown[...] = jnp.concatenate(
-        [first[: experts + 1], second[0:1], jnp.zeros((14, width), f32)], 0
-    ).astype(bf16)
-    small_sib = remote(sown, ssib, sbs, sbr, (sib, z))
-    small_sib.start()
+    gkv = turn(jnp.concatenate(own_kv, 0), cos, sin, kw, False).astype(bf16)
+    part[...] = dot_nt(gq, wqkv[:, :qw]) + dot_nt(gkv, wqkv[:, qw:])
+
+    def normed_part(zz):
+        return part[pl.ds(pl.multiple_of(zz * rows, 16), rows), :]
+
+    for hop in range(nz - 1):
+        normed_sum.hop(hop, normed_part)
+        out_line.hop(hop + 1)
+        if hop == 0:
+            again = jnp.sum(part[...] * x * scale1, 0, keepdims=True)
+            sz2[z] = jnp.concatenate([again, ggrad_ref[...], jnp.zeros((14, width), f32)], 0).astype(
+                bf16
+            )
+            for copy in z_copies(slot_of(sz2), z2s, z2r):
+                copy.start()
+            pair_part = dot_tn(normed, gkv)
+            for j in range(n):
+                w2.pack[j] = pair_part[j * dn : (j + 1) * dn].astype(bf16)
+            w2.give()
+            w1.total()
+    w2.spread()
+    normed_sum.total(sums, normed_part)
 
     own_x = x_ref[own_rows, :].astype(f32)
     own_scale = lax.rsqrt(jnp.mean(own_x * own_x, -1, keepdims=True) + EPS)
-    grad_normed = part[own_rows, :]
-    for k in range(1, nz):
-        remote(zsend.at[k - 1], zin.at[k - 1], zps.at[k - 1], zpr.at[k - 1], (e, z)).wait_recv()
-        grad_normed = grad_normed + zin[k - 1].astype(f32)
+    grad_normed = sums[...]
     gained = grad_normed * gain_ref[...]
     igrad = (
         gmid_ref[...]
@@ -1193,9 +1164,19 @@
         * jnp.mean(gained * own_x, -1, keepdims=True)
     )
     igbuf[own_rows, :] = igrad.astype(bf16)
-    for copy in z_copies(part_of(igbuf), zis, zir):
-        copy.start()
-
+    igrad_line.start()
+
+    w1.forward()
+    for copy in z_arrivals(slot_of(sz2), z2s, z2r):
+        copy.wait_recv()
+    second = sz2[0].astype(f32)
+    for zz in range(1, nz):
+        second = second + sz2[zz].astype(f32)
+    sown[experts:, :] = second.astype(bf16)
+    small_sib = remote(sown, ssib, sbs, sbr, (sib, z))
+    small_sib.start()
+    if nz > 2:
+        igrad_line.hop(1)
     small_sib.wait_recv()
     schip[me] = (sown[...].astype(f32) + ssib[...].astype(f32)).astype(bf16)
 
@@ -1206,35 +1187,12 @@
     for t in range(1, half):
         small_send(t).start()
 
-    weight_send(0).wait_recv()
-    total = wpack[e].astype(f32) + wsi[0].astype(f32)
-    for t in range(1, half):
-        weight_final(t).wait_recv()
-        total = total + wsr[t - 1].astype(f32)
-    wall[e] = total.astype(bf16)
-
-    def all_send(t):
-        to = (lax.rem(e + 2 * t, n), z)
-        return remote(wall.at[e], wall.at[e], was.at[t], war.at[t], to)
-
-    def all_pass(src, t):
-        return remote(wall.at[src], wall.at[src], wbs.at[t], wbr.at[t], (sib, z))
-
-    for t in range(1, half):
-        all_send(t).start()
-    all_pass(e, 0).start()
-    for copy in z_arrivals(part_of(obuf), zos, zor):
-        copy.wait_recv()
-    out_ref[...] = obuf[...].astype(f32)
-
-    def all_forward(t, carry):
-        src = lax.rem(e - 2 * t + n, n)
-        remote(wall.at[src], wall.at[src], was.at[t], war.at[t], (src, z)).wait_recv()
-        all_pass(src, t).start()
-        return carry
-
-    lax.fori_loop(1, half, all_forward, 0)
-
+    w2.total()
+    for hop in range(2, nz - 1):
+        igrad_line.hop(hop)
+    igrad_line.hop(nz - 1)
+
+    w2.forward()
     for t in range(1, half):
         src = lax.rem(me + half - t, half)
         remote(
@@ -1245,45 +1203,22 @@
         small = small + schip[t].astype(f32)
     small_ref[...] = small
 
-    for copy in z_arrivals(part_of(igbuf), zis, zir):
-        copy.wait_recv()
-    igrad_ref[...] = igbuf[...].astype(f32)
-
-    def all_arrive(t, carry):
-        src = lax.rem(sib - 2 * t + n, n)
-        all_pass(src, t).wait_recv()
-        return carry
-
-    lax.fori_loop(0, half, all_arrive, 0)
-    for j in range(n):
-        wsum_ref[j * dn : (j + 1) * dn, :] = wall[j].astype(f32)
-
-    for copy in (
-        z_copies(part_of(gat), zas, zar)
-        + z_copies(slot_of(sz1), z1s, z1r)
-        + z_copies(part_of(obuf), zos, zor)
-        + z_copies(slot_of(sz2), z2s, z2r)
-        + z_copies(part_of(igbuf), zis, zir)
-    ):
+    w1.arrive()
+    w2.arrive()
+    for line in (gat_line, out_line, igrad_line, normed_sum, out_sum, w1, w2):
+        line.drain()
+    for copy in z_copies(slot_of(sz1), z1s, z1r) + z_copies(slot_of(sz2), z2s, z2r):
         copy.wait_send()
-    for k in range(1, nz):
-        remote(zsend.at[k - 1], zin.at[k - 1], zps.at[k - 1], zpr.at[k - 1], (e, z)).wait_send()
     small_sib.wait_send()
     for t in range(1, half):
         mixed_send(t).wait_send()
-    for k in range(1, nz):
-        mixed_last(k).wait_send()
 
     def drained(t, carry):
         key_send(t).wait_send()
-        weight_send(t).wait_send()
-        all_pass(e, t).wait_send()
 
         @pl.when(t > 0)
         def _():
             key_final(t).wait_send()
-            weight_final(t).wait_send()
-            all_send(t).wait_send()
             small_send(t).wait_send()
 
         return carry
@@ -1291,8 +1226,202 @@
     lax.fori_loop(0, half, drained, 0)
 
 
+class PlaneSum:
+    def __init__(self, n, e, z, sib, wall, pack, near, send, recv, *sems):
+        self.n, self.e, self.z, self.sib, self.half = n, e, z, sib, n // 2
+        self.wall, self.pack, self.near, self.send, self.recv = wall, pack, near, send, recv
+        self.sems = sems
+
+    def peer(self, base, t):
+        return lax.rem(base - 2 * t + self.n, self.n)
+
+    def near_copy(self, t):
+        src = self.pack.at[self.peer(self.sib, t)]
+        return remote(
+            src, self.near.at[t], self.sems[0].at[t], self.sems[1].at[t], (self.sib, self.z)
+        )
+
+    def far_copy(self, t):
+        return remote(
+            self.send.at[t - 1],
+            self.recv.at[t - 1],
+            self.sems[2].at[t],
+            self.sems[3].at[t],
+            (self.peer(self.e, t), self.z),
+        )
+
+    def all_copy(self, src, t, to):
+        ref = self.wall.at[src]
+        return remote(ref, ref, self.sems[4].at[t], self.sems[5].at[t], (to, self.z))
+
+    def pass_copy(self, src, t):
+        ref = self.wall.at[src]
+        return remote(ref, ref, self.sems[6].at[t], self.sems[7].at[t], (self.sib, self.z))
+
+    def give(self):
+        def one(i, carry):
+            self.near_copy(self.half - 1 - i).start()
+            return carry
+
+        lax.fori_loop(0, self.half, one, 0)
+
+    def spread(self):
+        def one(i, carry):
+            t = self.half - 1 - i
+            self.near_copy(t).wait_recv()
+            own = self.pack[self.peer(self.e, t)].astype(f32)
+            self.send[t - 1] = (own + self.near[t].astype(f32)).astype(bf16)
+            self.far_copy(t).start()
+            return carry
+
+        lax.fori_loop(0, self.half - 1, one, 0)
+
+    def total(self):
+        self.near_copy(0).wait_recv()
+        total = self.pack[self.e].astype(f32) + self.near[0].astype(f32)
+        for t in range(1, self.half):
+            self.far_copy(t).wait_recv()
+            total = total + self.recv[t - 1].astype(f32)
+        self.wall[self.e] = total.astype(bf16)
+        for t in range(1, self.half):
+            self.all_copy(self.e, t, lax.rem(self.e + 2 * t, self.n)).start()
+        self.pass_copy(self.e, 0).start()
+
+    def forward(self):
+        def one(t, carry):
+            src = self.peer(self.e, t)
+            self.all_copy(src, t, src).wait_recv()
+            self.pass_copy(src, t).start()
+            return carry
+
+        lax.fori_loop(1, self.half, one, 0)
+
+    def arrive(self):
+        def one(t, carry):
+            self.pass_copy(self.peer(self.sib, t), t).wait_recv()
+            return carry
+
+        lax.fori_loop(0, self.half, one, 0)
+
+    def drain(self):
+        def one(t, carry):
+            self.near_copy(t).wait_send()
+            self.pass_copy(self.e, t).wait_send()
+
+            @pl.when(t > 0)
+            def _():
+                self.far_copy(t).wait_send()
+                self.all_copy(self.e, t, self.sib).wait_send()
+
+            return carry
+
+        lax.fori_loop(0, self.half, one, 0)
+
+
+class Line:
+    def __init__(self, z, nz, e, buf_of, send, recv):
+        self.z, self.nz, self.e = z, nz, e
+        self.buf_of, self.send, self.recv = buf_of, send, recv
+
+    def copy(self, way, piece):
+        to = self.z + 1 if way == 0 else self.z - 1
+        ref = self.buf_of(piece)
+        return remote(ref, ref, self.send.at[way, piece], self.recv.at[way, piece], (self.e, to))
+
+    def push(self, piece, ways=(0, 1)):
+        for way in ways:
+
+            @pl.when(self.z < self.nz - 1 if way == 0 else self.z > 0)
+            def _():
+                self.copy(way, piece).start()
+
+    def start(self):
+        self.push(self.z)
+
+    def hop(self, i):
+        @pl.when(self.z >= i)
+        def _():
+            self.copy(0, self.z - i).wait_recv()
+            self.push(self.z - i, (0,))
+
+        @pl.when(self.z + i <= self.nz - 1)
+        def _():
+            self.copy(1, self.z + i).wait_recv()
+            self.push(self.z + i, (1,))
+
+    def drain(self):
+        for piece in range(self.nz):
+
+            @pl.when((self.z >= piece) & (self.z < self.nz - 1))
+            def _():
+                self.copy(0, piece).wait_send()
+
+            @pl.when((self.z <= piece) & (self.z > 0))
+            def _():
+                self.copy(1, piece).wait_send()
+
+
+class LineSum:
+    def __init__(self, z, nz, e, send_buf, recv_buf, send, recv):
+        self.z, self.nz, self.e = z, nz, e
+        self.send_buf, self.recv_buf, self.send, self.recv = send_buf, recv_buf, send, recv
+
+    def copy(self, way, target):
+        to = self.z + 1 if way == 0 else self.z - 1
+        return remote(
+            self.send_buf.at[way, target],
+            self.recv_buf.at[way, target],
+            self.send.at[way, target],
+            self.recv.at[way, target],
+            (self.e, to),
+        )
+
+    def hop(self, i, own_of):
+        for way, target in ((0, self.nz - 1 - i), (1, i)):
+            passes = self.z < target if way == 0 else self.z > target
+            first = self.z == 0 if way == 0 else self.z == self.nz - 1
+            inner = self.z > 0 if way == 0 else self.z < self.nz - 1
+
+            @pl.when(passes & first)
+            def _():
+                self.send_buf[way, target] = own_of(target).astype(bf16)
+                self.copy(way, target).start()
+
+            @pl.when(passes & inner)
+            def _():
+                self.copy(way, target).wait_recv()
+                self.send_buf[way, target] = (
+                    own_of(target) + self.recv_buf[way, target].astype(f32)
+                ).astype(bf16)
+                self.copy(way, target).start()
+
+    def total(self, ref, own_of):
+        ref[...] = own_of(self.z)
+
+        @pl.when(self.z > 0)
+        def _():
+            self.copy(0, self.z).wait_recv()
+            ref[...] += self.recv_buf[0, self.z].astype(f32)
+
+        @pl.when(self.z < self.nz - 1)
+        def _():
+            self.copy(1, self.z).wait_recv()
+            ref[...] += self.recv_buf[1, self.z].astype(f32)
+
+    def drain(self):
+        for target in range(self.nz):
+
+            @pl.when(self.z < target)
+            def _():
+                self.copy(0, target).wait_send()
+
+            @pl.when(self.z > target)
+            def _():
+                self.copy(1, target).wait_send()
+
+
 def return_layer(
-    n, nz, gmid, mid, rgrad, ggrad, x, gain, wq, wk, wv, wo, cos, sin, q, kv, lrow, att, lens, mixed
+    n, nz, gmid, mid, glog, ggrad, xn, x, gain, wq, wk, wv, wo, cos, sin, q, kv, lrow, att, lens, mixed
 ):
     tok, width = x.shape
     rows = tok // nz
@@ -1301,29 +1430,38 @@
     span = tok // seqs
     half = n // 2
     stacked = (qw // kw) * span
-    pack = 2 * qw + 2 * kw
-    small_rows = rgrad.shape[0] + 16
+    experts = glog.shape[0]
+    small_rows = experts + 16
     dma = pltpu.SemaphoreType.DMA
     vmem = pl.BlockSpec(memory_space=pltpu.VMEM)
     sds = jax.ShapeDtypeStruct
     zdma = dma((nz - 1,))
+    line = dma((2, nz))
     hdma = dma((half,))
     fdma = dma((half - 1,))
+    def plane_bufs(cols):
+        return [
+            pltpu.VMEM((n, width // n, cols), bf16),
+            pltpu.VMEM((half, width // n, cols), bf16),
+            pltpu.VMEM((half - 1, width // n, cols), bf16),
+            pltpu.VMEM((half - 1, width // n, cols), bf16),
+        ]
+
+    line_buf = pltpu.VMEM((2, nz, rows, width), bf16)
     return pl.pallas_call(
         functools.partial(return_kernel, n, nz),
         out_shape=[
-            sds((tok, width), f32),
-            sds((tok, width), f32),
-            sds((width, pack), f32),
+            sds((tok, width), bf16),
+            sds((tok, width), bf16),
+            sds((n, width // n, 2 * qw), bf16),
+            sds((n, width // n, 2 * kw), bf16),
             sds((small_rows, width), f32),
         ],
-        in_specs=[vmem] * 16
+        in_specs=[vmem] * 17
         + [pl.BlockSpec(memory_space=pltpu.SMEM), pl.BlockSpec(memory_space=pl.ANY)],
-        out_specs=[vmem] * 4,
+        out_specs=[vmem] * 5,
         scratch_shapes=[
             pltpu.VMEM((width, qw + 2 * kw), bf16),
-            pltpu.VMEM((tok, width), bf16),
-            pltpu.VMEM((tok, width), bf16),
             pltpu.VMEM((tok, width), bf16),
             pltpu.VMEM((tok, qw), bf16),
             pltpu.VMEM((tok, qw), f32),
@@ -1334,43 +1472,37 @@
             pltpu.VMEM((half - 1, seqs, span, 2 * kw), bf16),
             pltpu.VMEM((half - 1, seqs, span, 2 * kw), bf16),
             pltpu.VMEM((tok, width), f32),
-            pltpu.VMEM((nz - 1, rows, width), bf16),
-            pltpu.VMEM((nz - 1, rows, width), bf16),
-            pltpu.VMEM((n, width // n, pack), bf16),
-            pltpu.VMEM((half, width // n, pack), bf16),
-            pltpu.VMEM((half - 1, width // n, pack), bf16),
-            pltpu.VMEM((half - 1, width // n, pack), bf16),
-            pltpu.VMEM((n, width // n, pack), bf16),
-            pltpu.VMEM((nz, small_rows, width), bf16),
+            pltpu.VMEM((rows, width), f32),
+            pltpu.VMEM((rows, width), f32),
+            line_buf,
+            line_buf,
+            line_buf,
+            line_buf,
+            plane_bufs(2 * qw),
+            plane_bufs(2 * kw),
+            pltpu.VMEM((nz, experts, 128), bf16),
             pltpu.VMEM((nz, 16, width), bf16),
             pltpu.VMEM((small_rows, width), bf16),
             pltpu.VMEM((small_rows, width), bf16),
             pltpu.VMEM((half, small_rows, width), bf16),
+            pltpu.VMEM((half, nz, rows, width), bf16),
         ]
-        + [zdma] * 12
+        + [line] * 10
+        + [zdma] * 4
         + [hdma, hdma, fdma, fdma]
-        + [hdma, hdma, fdma, fdma]
-        + [hdma] * 4
+        + [[hdma] * 8, [hdma] * 8]
         + [dma, dma, fdma, fdma]
-        + [
-            pltpu.VMEM((half, nz, rows, width), bf16),
-            pltpu.VMEM((nz - 1, rows, width), bf16),
-            pltpu.VMEM((nz - 1, rows, width), bf16),
-            fdma,
-            fdma,
-            zdma,
-            zdma,
-            dma,
-        ],
+        + [fdma, fdma, dma],
         compiler_params=pltpu.CompilerParams(
-            collective_id=3, has_side_effects=True, vmem_limit_bytes=56 << 20
+            collective_id=3, has_side_effects=True, vmem_limit_bytes=58 << 20
         ),
         name="attend_back",
     )(
         gmid,
         mid,
-        rgrad,
+        glog,
         ggrad,
+        xn,
         x,
         gain[None],
         wq,
@@ -1386,6 +1518,100 @@
         lens,
         mixed,
     )
+
+
+def finish_kernel(
+    out_low,
+    igrad_low,
+    wall,
+    wall2,
+    small,
+    load,
+    dgate_in,
+    dup_in,
+    ddown_in,
+    out_ref,
+    igrad_ref,
+    q_ref,
+    k_ref,
+    v_ref,
+    o_ref,
+    router_ref,
+    again_ref,
+    egain_ref,
+    loss_ref,
+    load_ref,
+    dgate,
+    dup,
+    ddown,
+    dgate_s,
+    dup_s,
+    ddown_s,
+    sems,
+):
+    pairs = ((dgate_in, dgate_s, dgate), (dup_in, dup_s, dup), (ddown_in, ddown_s, ddown))
+    reads = [pltpu.make_async_copy(p[0], p[1], sems.at[0, i]) for i, p in enumerate(pairs)]
+    writes = [pltpu.make_async_copy(p[1], p[2], sems.at[1, i]) for i, p in enumerate(pairs)]
+    for copy in reads:
+        copy.start()
+    qw, kw = q_ref.shape[1], k_ref.shape[1]
+    experts = load.shape[1]
+    out_ref[...] = out_low[...].astype(f32)
+    for read, write in zip(reads, writes):
+        read.wait()
+        write.start()
+    igrad_ref[...] = igrad_low[...].astype(f32)
+    chunks, dn, _ = wall.shape
+    flat = wall[...].reshape(chunks * dn, 2 * qw).astype(f32)
+    q_ref[...] = flat[:, :qw]
+    o_ref[...] = flat[:, qw:].T
+    flat = wall2[...].reshape(chunks * dn, 2 * kw).astype(f32)
+    k_ref[...] = flat[:, :kw]
+    v_ref[...] = flat[:, kw:]
+    router_ref[...] = small[0:experts, :].T
+    again_ref[...] = small[experts : experts + 1, :]
+    egain_ref[...] = small[experts + 1 : experts + 2, :]
+    load_ref[...] = load[...]
+    loss_ref[...] = jnp.mean(load[...], -1, keepdims=True)
+    for copy in writes:
+        copy.wait()
+
+
+def finish_layer(out_low, igrad_low, wall, wall2, small, load, dgate, dup, ddown, qw, kw):
+    tok, width = out_low.shape
+    experts = load.shape[1]
+    vmem = pl.BlockSpec(memory_space=pltpu.VMEM)
+    hbm = pl.BlockSpec(memory_space=pl.ANY)
+    sds = jax.ShapeDtypeStruct
+    return pl.pallas_call(
+        finish_kernel,
+        out_shape=[
+            sds((tok, width), f32),
+            sds((tok, width), f32),
+            sds((width, qw), f32),
+            sds((width, kw), f32),
+            sds((width, kw), f32),
+            sds((qw, width), f32),
+            sds((width, experts), f32),
+            sds((1, width), f32),
+            sds((1, width), f32),
+            sds((1, 1), f32),
+            sds((1, experts), f32),
+            sds(dgate.shape, f32),
+            sds(dup.shape, f32),
+            sds(ddown.shape, f32),
+        ],
+        in_specs=[vmem] * 6 + [hbm] * 3,
+        out_specs=[vmem] * 11 + [hbm] * 3,
+        scratch_shapes=[
+            pltpu.VMEM(dgate.shape, f32),
+            pltpu.VMEM(dup.shape, f32),
+            pltpu.VMEM(ddown.shape, f32),
+            pltpu.SemaphoreType.DMA((2, 3)),
+        ],
+        compiler_params=pltpu.CompilerParams(vmem_limit_bytes=48 << 20),
+        name="finish",
+    )(out_low, igrad_low, wall, wall2, small, load, dgate, dup, ddown)
 
 
 def shards(
@@ -1409,9 +1635,6 @@
     tok_rows = inputs.shape[0]
     seq_count = seq_lens.shape[0]
     span_rows = tok_rows // seq_count
-    query_width = query_weight.shape[1]
-    key_width = key_weight.shape[1]
-    experts = router_weight.shape[1]
     local_pos = lax.axis_index("expert") * span_rows + jnp.arange(span_rows, dtype=jnp.int32)
     frequency = THETA ** (-2.0 * jnp.arange(HD // 2, dtype=jnp.float32) / HD)
     angles = local_pos.astype(f32)[:, None] * frequency[None, :]
@@ -1424,13 +1647,14 @@
     )
     (
         grad_middle,
-        router_part,
+        logit_grads,
         expert_gain_part,
         expert_load,
         gate_grad,
         up_grad,
         down_grad,
         mixed,
+        normed2,
     ) = expert_layer(
         n,
         nz,
@@ -1444,13 +1668,14 @@
         cotangent,
         cot_all,
     )
-    output, input_grad, packed, small = return_layer(
+    out_low, igrad_low, packed, packed2, small = return_layer(
         n,
         nz,
         grad_middle,
         middle,
-        router_part,
+        logit_grads,
         expert_gain_part,
+        normed2,
         inputs,
         attention_gain,
         *weights,
@@ -1461,19 +1686,46 @@
         seq_lens,
         mixed,
     )
-    cuts = (query_width, query_width + key_width, query_width + 2 * key_width)
+    (
+        output,
+        input_grad,
+        query_grad,
+        key_grad,
+        value_grad,
+        out_weight_grad,
+        router_grad,
+        attention_gain_grad,
+        expert_gain_grad,
+        balance_loss,
+        expert_load,
+        gate_grad,
+        up_grad,
+        down_grad,
+    ) = finish_layer(
+        out_low,
+        igrad_low,
+        packed,
+        packed2,
+        small,
+        expert_load,
+        gate_grad,
+        up_grad,
+        down_grad,
+        query_weight.shape[1],
+        key_weight.shape[1],
+    )
     return (
         output,
         input_grad,
-        jnp.mean(expert_load),
+        balance_loss[0, 0],
         expert_load[0],
-        small[experts + 1],
-        packed[:, : cuts[0]],
-        packed[:, cuts[0] : cuts[1]],
-        packed[:, cuts[1] : cuts[2]],
-        packed[:, cuts[2] :].T,
-        small[experts],
-        small[:experts].T,
+        attention_gain_grad[0],
+        query_grad,
+        key_grad,
+        value_grad,
+        out_weight_grad,
+        expert_gain_grad[0],
+        router_grad,
         gate_grad,
         up_grad,
         down_grad.reshape(down_weight.shape),

time: 307 us -> 296 us (0.964)
  local copies, waits for them, and re-layouts: 25 us -> 12.7 us
  Pallas kernels: 254 us -> 260 us
    pallas_call x0 -> x1, Pallas kernels: none -> 7.22 us  [finish_layer(): pl.pallas_call(finish_kernel, out_shape=[sds((tok, width), f32), sds((tok...]
    unnamed x53 -> x49, local copies, waits for them, and re-layouts: 16.3 us -> 11.9 us
    transpose x2 -> x0, local copies, waits for them, and re-layouts: 4.22 us -> none  [the longest x1 2.65 us: shards(): packed[:, cuts[2]:]]
    slice x2 -> x0, local copies, waits for them, and re-layouts: 3.68 us -> none  [the longest x1 2.24 us: shards(): packed[:, cuts[1]:cuts[2]]]
where the time goes in v5:
time: 296 us
  Pallas kernels  260 us (88%)
  between operations  14.3 us (5%)
  local copies, waits for them, and re-layouts  12.7 us (4%)
  waiting for transfers between devices  5.8 us (2%)
    pallas_call x1, Pallas kernels, return_layer(): pl.pallas_call(functools.partial(return_kernel, n, nz), out_shape=[sds((t...  113 us
    pallas_call x1, Pallas kernels, expert_layer(): pl.pallas_call(functools.partial(expert_kernel, n, nz, big), out_shape=ou...  99.5 us
    pallas_call x1, Pallas kernels, attend_layer(): pl.pallas_call(functools.partial(attend_kernel, n, nz), out_shape=[sds((r...  39.9 us
    unnamed x49, local copies, waits for them, and re-layouts  11.9 us
    pallas_call x1, Pallas kernels, finish_layer(): pl.pallas_call(finish_kernel, out_shape=[sds((tok, width), f32), sds((tok...  7.22 us
  transfers between devices with their start and end apart: 1, of which 1 were waited for; matrix products, arithmetic and copies ran while one was open for 1% of the time, Pallas kernels for 13%

profile of v5, /device:TPU:0, one launch (start us, length us, event | category | flops | bytes accessed | tf_op | source)
XLA Modules:
  0.0 295.5 jit_solution(4342249772822948534)
XLA Ops:
  7.2 2.4 convert_element_type.11
  9.7 0.8 copy.34.routes_ref
  10.6 0.2 multiply_sine_fusion
  10.9 0.2 tile.21
  11.1 0.1 copy.32.sin_ref
  11.3 0.2 tile.9
  11.5 0.1 copy.31.cos_ref
  11.6 0.8 copy.33.router_ref
  12.5 39.9 %attend.1 = (f32[96,1024]{1,0:T(8,128)S(1)}, bf16[384,256]{1,0:T(8,128)(2,1)S(1)}, bf16[2,1536,256]{2,1,0:T(8,128)(2,1)S(1)}, f32[4,8,384]{2,1,0:T(8,128)S(1)}, f32[384,256]{1,0:T(8,128)S(1)}) custom-call(bf16[384,1024]{1,0:T(8,128)(2,1)S(1)} %copy-done, f32[1,1024]{1,0:T(1,128)S(1)} %bitcast.13, bf16[1024,256]{1,0:T(8,128)(2,1)S(1)} %copy-done.2, ...), custom_call_target="tpu_custom_call" | custom-call | tf_op jit(solution)/shard_map/attend/pallas_call | solution.py:817
  52.4 0.7 copy-done.6
  53.2 1.1 copy-done.7
  54.3 0.7 copy-done.14
  55.1 0.7 copy-done.16
  55.7 0.6 copy-done.17
  56.4 5.8 %all-gather.2.cloned.1.call-done.cot_all = bf16[3072,1024]{1,0:T(8,128)(2,1)} async-done(((bf16[384,1024]{1,0:T(8,128)(2,1)}), bf16[3072,1024]{1,0:T(8,128)(2,1)}) %all-gather.2.cloned.1.call-update) | async-done | bytes 6291472 | tf_op jit(solution)/shard_map/all_gather | solution.py:1643
  62.1 99.5 %experts.1 = (f32[96,1024]{1,0:T(8,128)}, bf16[32,128]{1,0:T(8,128)(2,1)}, f32[1,1024]{1,0:T(1,128)}, f32[1,32]{1,0:T(1,128)}, f32[4,1024,128]{2,1,0:T(8,128)}, ...) custom-call(f32[96,1024]{1,0:T(8,128)} %copy-done.6, ...), custom_call_target="tpu_custom_call" | custom-call | tf_op jit(solution)/shard_map/experts/pallas_call | solution.py:631
  161.7 113.5 %attend_back.1 = (bf16[384,1024]{1,0:T(8,128)(2,1)}, bf16[384,1024]{1,0:T(8,128)(2,1)}, bf16[8,128,512]{2,1,0:T(8,128)(2,1)}, bf16[8,128,256]{2,1,0:T(8,128)(2,1)}, f32[48,1024]{1,0:T(8,128)}) custom-call(f32[96,1024]{1,0:T(8,128)} %get-tuple-element.48.gmid_ref, f32[96,1024]{1,0:T(8,128)} %copy-done.6, bf16[32,128]{1,0:T(8,128)(2,1)} %get-tuple-element.49.glog_ref, ...), custom_call_target="tpu_custom_call" | custom-call | tf_op jit(solution)/shard_map/attend_back/pallas_call | solution.py:1451
  275.2 1.2 copy-done.8
  276.4 1.1 copy-done.11
  277.5 1.1 copy-done.12
  278.7 1.0 copy-done.13
  279.7 0.9 copy-done.15
  280.6 7.2 %finish.1 = (f32[384,1024]{1,0:T(8,128)}, f32[384,1024]{1,0:T(8,128)}, f32[1024,256]{1,0:T(8,128)}, f32[1024,128]{1,0:T(8,128)}, f32[1024,128]{1,0:T(8,128)}, /*...) custom-call(bf16[384,1024]{1,0:T(8,128)(2,1)S(1)} %copy-done.11, ...), custom_call_target="tpu_custom_call" | custom-call | tf_op jit(solution)/shard_map/finish/pallas_call | solution.py:1586
  287.9 0.8 copy.37
  (42 shorter events, 0.3 us)
Async XLA Ops:
  7.2 2.6 copy-start.22
  7.2 54.9 %all-gather.2.cloned.1.call-start = ((), (), s32[]{:S(2)}) async-start(), calls=%async_computation | async-start | bytes 7077888 | tf_op jit(solution)/shard_map/all_gather | solution.py:1643
  9.6 2.0 copy-start.21
  9.6 2.8 copy-start
  9.6 2.8 copy-start.2
  9.7 2.8 copy-start.3
  9.7 2.8 copy-start.9
  9.7 2.8 copy-start.10
  9.7 2.8 copy-start.18
  9.7 2.8 copy-start.19
  11.2 41.2 %copy-start.4 = (f32[384,128]{1,0:T(8,128)}, f32[384,128]{1,0:T(8,128)S(1)}, u32[]{:S(2)}) copy-start(f32[384,128]{1,0:T(8,128)S(1)} %copy.32.sin_ref) | copy-start | bytes 589828
  11.6 150.0 %copy-start.5 = (f32[384,128]{1,0:T(8,128)}, f32[384,128]{1,0:T(8,128)S(1)}, u32[]{:S(2)}) copy-start(f32[384,128]{1,0:T(8,128)S(1)} %copy.31.cos_ref) | copy-start | bytes 589828
  52.4 0.7 copy-start.6
  53.2 1.1 copy-start.7
  54.3 0.7 copy-start.14
  55.1 0.7 copy-start.16
  55.7 0.6 copy-start.17
  161.6 113.5 %copy-start.1 = (f32[4,1024,128]{2,1,0:T(8,128)S(1)}, f32[4,1024,128]{2,1,0:T(8,128)}, u32[]{:S(2)}) copy-start(f32[4,1024,128]{2,1,0:T(8,128)} %get-tuple-element.63.dgate_in) | copy-start | bytes 6291460
  161.7 113.5 %copy-start.20 = (f32[1,32]{1,0:T(1,128)S(1)}, f32[1,32]{1,0:T(1,128)}, u32[]{:S(2)}) copy-start(f32[1,32]{1,0:T(1,128)} %get-tuple-element.62.load) | copy-start | bytes 388
  275.2 1.2 copy-start.8
  276.4 1.1 copy-start.11
  277.5 1.1 copy-start.12
  278.7 1.0 copy-start.13
  279.7 0.9 copy-start.15
Sparse Core Ops, SparseCore 0:
  10.5 51.6 all-gather.1

commit v6 on v5

--- a/solution.py
+++ b/solution.py
@@ -153,6 +153,9 @@
         zgr,
         zggs,
         zggr,
+        zds,
+        zdr,
+        picks_s,
     ) = rest
     e = lax.axis_index("expert")
     z = lax.axis_index("tensor")
@@ -163,11 +166,16 @@
     half = n // 2
     rows, width = mid_ref.shape
     tok = rows * nz
-    experts = router_ref.shape[1]
+    experts = router_ref.shape[0]
     local_experts, _, hid = gate_hbm.shape
     inner_w = local_experts * hid
     fc = min(inner_w, 256)
     fslots = fsend.shape[0]
+    square = half == 4
+    chip_x = me + 1 - 2 * lax.rem(me, 2)
+    chip_y = lax.rem(me + 2, 4)
+    chip_d = 3 - me
+    mid_row = rows // 2
 
     loads = []
     for el in range(local_experts):
@@ -205,8 +213,11 @@
     scale2 = lax.rsqrt(jnp.mean(mid * mid, -1, keepdims=True) + EPS)
     xn = (mid * scale2 * gain_ref[...]).astype(bf16)
     xn_s[...] = xn
-    logits = dot_nn(xn, router_ref[...])
-    picks = routes_ref[own_rows, :]
+    logits = dot_nt(xn, router_ref[...])
+    choices = routes_ref[...].astype(f32)
+    top_count = choices.shape[0]
+    picks_s[...] = jnp.concatenate([choices, jnp.zeros((128 - top_count, tok), f32)], 0).T
+    picks = picks_s[own_rows, 0:top_count].astype(jnp.int32)
     lanes = lax.broadcasted_iota(jnp.int32, (rows, experts), 1)
     chosen = jnp.zeros((rows, experts), f32)
     for k in range(picks.shape[1]):
@@ -252,23 +263,52 @@
         ref = wbuf.at[zz, core, h]
         return remote(ref, ref, ws.at[g, s], wr.at[g, s], (to, z))
 
+    def x_part(zz, h, first, count, g, i, to):
+        start = pl.multiple_of(h * rows + first, 16)
+        ref = xbuf.at[zz, core, pl.ds(start, count)]
+        return remote(ref, ref, xs.at[g, i], xr.at[g, i], (2 * to + core, z))
+
     def push_piece(g):
         zz = piece_of(g)
+        if square:
+            x_part(zz, me, 0, rows, g, 0, chip_x).start()
+            x_part(zz, me, 0, rows, g, 1, chip_y).start()
         for s in range(1, half):
             to = lax.rem(e + 2 * s, n)
-            x_row(zz, me, g, s, to).start()
+            if not square:
+                x_row(zz, me, g, s, to).start()
             x_small(zz, me, g, s, to).start()
+
+    def relays():
+        low = x_part(z, chip_x, 0, mid_row, 0, 2, chip_y)
+        high = x_part(z, chip_y, mid_row, rows - mid_row, 0, 3, chip_x)
+        return low, high
+
+    def z_diag(zz, k, to):
+        ref = xbuf.at[zz, core, pl.ds(pl.multiple_of(chip_d * rows, 16), rows)]
+        return remote(ref, ref, zds.at[k - 1], zdr.at[k - 1], (e, to))
 
     push_piece(jnp.int32(0))
     for k in range(1, nz):
         z_row(z, k, lax.rem(z + k, nz)).start()
         z_small(z, k, lax.rem(z + k, nz)).start()
+
+    if square:
+        low, high = relays()
+        x_part(z, chip_x, 0, rows, 0, 0, chip_x).wait_recv()
+        low.start()
+        x_part(z, chip_y, 0, rows, 0, 1, chip_y).wait_recv()
+        high.start()
 
     dgate[...] = jnp.zeros_like(dgate)
     dup[...] = jnp.zeros_like(dup)
     ddown[...] = jnp.zeros_like(ddown)
     for copy in loads:
         copy.wait()
+    if square:
+        x_part(z, chip_d, 0, mid_row, 0, 2, chip_y).wait_recv()
+        x_part(z, chip_d, mid_row, rows - mid_row, 0, 3, chip_x).wait_recv()
+        z_diag(z, 1, lax.rem(z + 1, nz)).start()
 
     sel_row = lax.broadcasted_iota(jnp.int32, (experts, fc), 0)
     sel_col = lax.broadcasted_iota(jnp.int32, (experts, fc), 1)
@@ -333,10 +373,14 @@
 
     def finals(g, s, to):
         at = lax.rem(g, fslots)
-        return [
-            remote(
-                fsend.at[at, s - 1], fin.at[g, s - 1], ps.at[g, s - 1], pr.at[g, s - 1], (to, z)
-            ),
+        rows_copy = []
+        if not square:
+            rows_copy = [
+                remote(
+                    fsend.at[at, s - 1], fin.at[g, s - 1], ps.at[g, s - 1], pr.at[g, s - 1], (to, z)
+                )
+            ]
+        return rows_copy + [
             remote(
                 fsend_g.at[at, s - 1],
                 fin_g.at[g, s - 1],
@@ -346,6 +390,55 @@
             ),
         ]
 
+    def half_copy(g, buf, upper, i, chip):
+        first, count = (mid_row, rows - mid_row) if upper else (0, mid_row)
+        return remote(
+            fsend.at[g, buf, pl.ds(first, count)],
+            fin.at[g, buf, pl.ds(first, count)],
+            ps.at[g, i],
+            pr.at[g, i],
+            (2 * chip + core, z),
+        )
+
+    def half_copies(g):
+        return [
+            half_copy(g, 2, False, 0, chip_x),
+            half_copy(g, 2, True, 1, chip_y),
+            half_copy(g, 0, False, 2, chip_x),
+            half_copy(g, 1, True, 3, chip_y),
+            half_copy(g, 1, False, 4, chip_y),
+            half_copy(g, 0, True, 5, chip_x),
+        ]
+
+    def chip_sum(slot, chip, upper):
+        first, count = (mid_row, rows - mid_row) if upper else (0, mid_row)
+        at = pl.ds(pl.multiple_of(chip * rows + first, 16), count)
+        return hold[slot, at, :].astype(f32) + sin[slot, at, :].astype(f32)
+
+    def direct_stage(g):
+        slot = lax.rem(g, 2)
+        copies = half_copies(g)
+        fsend[g, 2, :mid_row] = chip_sum(slot, chip_d, False).astype(bf16)
+        copies[0].start()
+        fsend[g, 2, mid_row:] = chip_sum(slot, chip_d, True).astype(bf16)
+        copies[1].start()
+        fsend[g, 0, :mid_row] = chip_sum(slot, chip_x, False).astype(bf16)
+        copies[2].start()
+        fsend[g, 1, mid_row:] = chip_sum(slot, chip_y, True).astype(bf16)
+        copies[3].start()
+
+    def relay_stage(g):
+        slot = lax.rem(g, 2)
+        copies = half_copies(g)
+        copies[0].wait_recv()
+        passed = chip_sum(slot, chip_y, False) + fin[g, 2, :mid_row].astype(f32)
+        fsend[g, 1, :mid_row] = passed.astype(bf16)
+        copies[4].start()
+        copies[1].wait_recv()
+        passed = chip_sum(slot, chip_x, True) + fin[g, 2, mid_row:].astype(f32)
+        fsend[g, 0, mid_row:] = passed.astype(bf16)
+        copies[5].start()
+
     def lasts(k, to):
         return [
             remote(zsend.at[k - 1], zin.at[k - 1], zgs.at[k - 1], zgr.at[k - 1], (e, to)),
@@ -357,7 +450,7 @@
 
     def plane_stage(g):
         slot = lax.rem(g, 2)
-        for copy in gives(slot):
+        for copy in gives(slot)[:2]:
             copy.wait_recv()
         if fslots < nz:
 
@@ -368,12 +461,15 @@
                         copy.wait_send()
 
         spot = lax.rem(g, fslots)
+        if square:
+            direct_stage(g)
         for s in range(1, half):
             h = lax.rem(me + half - s, half)
             at = pl.ds(pl.multiple_of(h * rows, 16), rows)
-            fsend[spot, s - 1] = (hold[slot, at, :].astype(f32) + sin[slot, at, :].astype(f32)).astype(
-                bf16
-            )
+            if not square:
+                fsend[spot, s - 1] = (
+                    hold[slot, at, :].astype(f32) + sin[slot, at, :].astype(f32)
+                ).astype(bf16)
             fsend_g[spot, s - 1] = (hold_g[slot, h].astype(f32) + sin_g[slot, h].astype(f32)).astype(
                 bf16
             )
@@ -381,6 +477,10 @@
                 copy.start()
         own_s[g] = hold[slot, my_rows, :].astype(f32) + sin[slot, my_rows, :].astype(f32)
         own_g[g] = hold_g[slot, me].astype(f32) + sin_g[slot, me].astype(f32)
+
+    def mixed_stage(g):
+        slot = lax.rem(g, 2)
+        gives(slot)[2].wait_recv()
         hold_o[slot] = (hold_o[slot].astype(f32) + sin_o[slot].astype(f32)).astype(bf16)
         mixed_copy(g, slot).start()
 
@@ -390,8 +490,14 @@
         for s in range(1, half):
             for copy in finals(g, s, sib):
                 copy.wait_recv()
-            total = total + fin[g, s - 1].astype(f32)
+            if not square:
+                total = total + fin[g, s - 1].astype(f32)
             total_g = total_g + fin_g[g, s - 1].astype(f32)
+
+        if square:
+            for copy in half_copies(g)[2:]:
+                copy.wait_recv()
+            total = total + fin[g, 0].astype(f32) + fin[g, 1].astype(f32)
 
         @pl.when(g == 0)
         def _():
@@ -416,10 +522,19 @@
             z_small(coming, g + 1, coming).wait_recv()
             push_piece(g + 1)
 
+        if square:
+
+            @pl.when(g > 0)
+            def _():
+                x_part(zz, chip_x, 0, rows, g, 0, chip_x).wait_recv()
+                x_part(zz, chip_y, 0, rows, g, 1, chip_y).wait_recv()
+                z_diag(zz, g, zz).wait_recv()
+
         for s in range(1, half):
             h = lax.rem(me + half - s, half)
             src = 2 * h + core
-            x_row(zz, h, g, s, src).wait_recv()
+            if not square:
+                x_row(zz, h, g, s, src).wait_recv()
             x_small(zz, h, g, s, src).wait_recv()
         for copy in forward(zz, core, g):
             copy.start()
@@ -431,6 +546,13 @@
             mixed_copy(g - 2, slot).wait()
 
         block(zz, core, 0, hold, hold_o, hold_g, slot)
+        if square:
+            for k in range(2, nz):
+
+                @pl.when(g == k - 2)
+                def _():
+                    z_diag(z, k, lax.rem(z + k, nz)).start()
+
 
         @pl.when(g < nz - 1)
         def _():
@@ -443,6 +565,7 @@
         @pl.when(g >= 1)
         def _():
             plane_stage(g - 1)
+            mixed_stage(g - 1)
 
         @pl.when(g >= 2)
         def _():
@@ -455,6 +578,12 @@
         block(zz, other, 1, osend, osend_o, osend_g, slot)
         for copy in gives(slot):
             copy.start()
+        if square:
+
+            @pl.when(g >= 1)
+            def _():
+                relay_stage(g - 1)
+
         return carry
 
     def forward(zz, parity, g):
@@ -477,6 +606,8 @@
         copy.start()
     if nz >= 2:
         tensor_stage(jnp.int32(nz - 2))
+    if square:
+        relay_stage(jnp.int32(nz - 1))
 
     def total_stats(j, carry):
         for zz in range(nz):
@@ -486,11 +617,12 @@
 
     stats = lax.fori_loop(0, half, total_stats, jnp.zeros((16, 128), f32))
     total_rows = n * tok
-    share = stats[0:1, :experts] / (total_rows * routes_ref.shape[1])
+    share = stats[0:1, :experts] / (total_rows * top_count)
     load_ref[...] = (
         experts * experts * share * ((stats[1:2, :experts] + stats[2:3, :experts]) / total_rows)
     )
     loss_w = experts * share / total_rows
+    mixed_stage(jnp.int32(nz - 1))
     tensor_stage(jnp.int32(nz - 1))
 
     gate_sums = own_g[0]
@@ -509,7 +641,7 @@
     if rows < 128:
         wide_grad = jnp.concatenate([wide_grad, jnp.zeros((128 - rows, 128), f32)], 0)
     glog_ref[...] = wide_grad.T[:experts].astype(bf16)
-    grad_rows = grad_rows + dot_nt(low_grad, router_ref[...])
+    grad_rows = grad_rows + dot_nn(low_grad, router_ref[...])
     mid = mid_ref[...]
     ggrad_ref[...] = jnp.sum(grad_rows * mid * scale2, 0, keepdims=True)
     gained = grad_rows * gain_ref[...]
@@ -521,6 +653,11 @@
 
     for copy in grads:
         copy.wait()
+    if square:
+        for copy in relays():
+            copy.wait_send()
+        for k in range(1, nz):
+            z_diag(z, k, z).wait_send()
     for k in range(1, nz):
         z_row(z, k, z).wait_send()
         z_small(z, k, z).wait_send()
@@ -532,8 +669,14 @@
             copy.wait_send()
 
     def drained(g, carry):
+        if square:
+            x_part(z, me, 0, rows, g, 0, chip_x).wait_send()
+            x_part(z, me, 0, rows, g, 1, chip_y).wait_send()
+            for copy in half_copies(g):
+                copy.wait_send()
         for s in range(1, half):
-            x_row(z, me, g, s, sib).wait_send()
+            if not square:
+                x_row(z, me, g, s, sib).wait_send()
             x_small(z, me, g, s, sib).wait_send()
         for copy in forward(z, core, g):
             copy.wait_send()
@@ -626,8 +769,9 @@
     scratch += [dma((nz, half))] * 4
     scratch += [dma((nz,))] * 4
     scratch += [dma((2,))] * 6
-    scratch += [dma((nz, half - 1))] * 4
-    scratch += [dma((nz - 1,))] * 4
+    scratch += [dma((nz, 6 if half == 4 else half - 1))] * 2
+    scratch += [dma((nz, half - 1))] * 2
+    scratch += [dma((nz - 1,))] * 6 + [pltpu.VMEM((nz * rows, 128), f32)]
     return pl.pallas_call(
         functools.partial(expert_kernel, n, nz, big),
         out_shape=out_shape,
@@ -638,7 +782,7 @@
             collective_id=1, has_side_effects=True, vmem_limit_bytes=60 << 20
         ),
         name="experts",
-    )(mid, gain[None], router, routes, cot, gate, up, down.reshape(inner_w, width), cot_all)[:9]
+    )(mid, gain[None], router.T, routes.T, cot, gate, up, down.reshape(inner_w, width), cot_all)[:9]
 
 
 def attend_kernel(
@@ -660,6 +804,7 @@
     att_ref,
     wqkv,
     part,
+    qst_s,
     m_s,
     l_s,
     o_s,
@@ -731,48 +876,64 @@
     lax.fori_loop(0, half, arrive, 0)
 
     ck = 2 * span
-    trip = (e * span + span - 1) // ck + 1
+    last = (e * span + span - 1) // ck
     stacked = groups * span
     qpos = lax.broadcasted_iota(jnp.int32, (stacked, ck), 0)
     qpos = e * span + lax.rem(qpos, span)
     kiota = lax.broadcasted_iota(jnp.int32, (stacked, ck), 1)
+    klane = lax.broadcasted_iota(jnp.int32, (1, ck), 1)
+    m_s[...] = jnp.full_like(m_s, -1e30)
+    l_s[...] = jnp.zeros_like(l_s)
+    o_s[...] = jnp.zeros_like(o_s)
     for s in range(seqs):
         for h in range(heads):
-            srows = slice(s * span, (s + 1) * span)
-            qst = jnp.concatenate(
+            qst_s[s * heads + h] = jnp.concatenate(
                 [
-                    q_ref[srows, (h * groups + g) * HD : (h * groups + g + 1) * HD]
+                    q_ref[
+                        s * span : (s + 1) * span,
+                        (h * groups + g) * HD : (h * groups + g + 1) * HD,
+                    ]
                     for g in range(groups)
                 ],
                 0,
-            )
-            m_s[...] = jnp.full_like(m_s, -1e30)
-            l_s[...] = jnp.zeros_like(l_s)
-            o_s[...] = jnp.zeros_like(o_s)
-
-            def chunk(c, carry):
-                at = pl.ds(pl.multiple_of(c * ck, 16), ck)
+            ) * jnp.array(HD ** (-0.5), bf16)
+
+    def chunk(c, diagonal):
+        at = pl.ds(pl.multiple_of(c * ck, 16), ck)
+        for s in range(seqs):
+            for h in range(heads):
+                i = s * heads + h
                 keys = kv_ref[s, at, h * HD : (h + 1) * HD]
                 vals = kv_ref[s, at, kw + h * HD : kw + (h + 1) * HD]
-                scores = dot_nt(qst, keys) * HD ** (-0.5)
-                kpos = kiota + c * ck
-                scores = jnp.where((kpos <= qpos) & (kpos < lens_ref[s]), scores, -1e30)
-                old = m_s[:, 0:1]
+                scores = dot_nt(qst_s[i], keys)
+                if diagonal:
+                    kpos = kiota + c * ck
+                    scores = jnp.where((kpos <= qpos) & (kpos < lens_ref[s]), scores, -1e30)
+                else:
+                    scores = scores + jnp.where(klane + c * ck < lens_ref[s], 0.0, -1e30)
+                old = m_s[i, :, 0:1]
                 new = jnp.maximum(old, jnp.max(scores, -1, keepdims=True))
                 weights = jnp.exp(scores - new)
                 shrink = jnp.exp(old - new)
-                m_s[...] = jnp.broadcast_to(new, m_s.shape)
-                l_s[...] = l_s[...] * shrink + jnp.sum(weights, -1, keepdims=True)
-                o_s[...] = o_s[...] * shrink + dot_nn(weights.astype(bf16), vals)
-                return carry
-
-            lax.fori_loop(0, trip, chunk, 0)
-            result = o_s[...] / l_s[:, 0:HD]
+                m_s[i] = jnp.broadcast_to(new, (stacked, 128))
+                l_s[i] = l_s[i] * shrink + jnp.sum(weights, -1, keepdims=True)
+                o_s[i] = o_s[i] * shrink + dot_nn(weights.astype(bf16), vals)
+
+    def whole_chunk(c, carry):
+        chunk(c, False)
+        return carry
+
+    lax.fori_loop(0, last, whole_chunk, 0)
+    chunk(last, True)
+    for s in range(seqs):
+        for h in range(heads):
+            i = s * heads + h
+            result = o_s[i] / l_s[i, :, 0:HD]
             for g in range(groups):
                 cols = slice((h * groups + g) * HD, (h * groups + g + 1) * HD)
-                att_ref[srows, cols] = result[g * span : (g + 1) * span]
-            logs = m_s[...] + jnp.log(l_s[...])
-            lrow_ref[s * heads + h] = logs.T[0:8]
+                att_ref[s * span : (s + 1) * span, cols] = result[g * span : (g + 1) * span]
+            logs = m_s[i] + jnp.log(l_s[i])
+            lrow_ref[i] = logs.T[0:8]
 
     part[...] = dot_nn(att_ref[...].astype(bf16), wo_ref[...])
     for k in range(1, nz):
@@ -811,6 +972,7 @@
     span = tok // seqs
     half = n // 2
     stacked = (qw // kw) * span
+    pairs = seqs * (kw // HD)
     dma = pltpu.SemaphoreType.DMA
     vmem = pl.BlockSpec(memory_space=pltpu.VMEM)
     sds = jax.ShapeDtypeStruct
@@ -828,16 +990,17 @@
         scratch_shapes=[
             pltpu.VMEM((width, qw + 2 * kw), bf16),
             pltpu.VMEM((tok, width), f32),
-            pltpu.VMEM((stacked, 128), f32),
-            pltpu.VMEM((stacked, 128), f32),
-            pltpu.VMEM((stacked, HD), f32),
+            pltpu.VMEM((pairs, stacked, HD), bf16),
+            pltpu.VMEM((pairs, stacked, 128), f32),
+            pltpu.VMEM((pairs, stacked, 128), f32),
+            pltpu.VMEM((pairs, stacked, HD), f32),
             pltpu.VMEM((nz - 1, rows, width), bf16),
             pltpu.VMEM((nz - 1, rows, width), bf16),
         ]
         + [dma((half, seqs))] * 4
         + [dma((nz - 1,))] * 2,
         compiler_params=pltpu.CompilerParams(
-            collective_id=2, has_side_effects=True, vmem_limit_bytes=48 << 20
+            collective_id=2, has_side_effects=True, vmem_limit_bytes=60 << 20
         ),
         name="attend",
     )(x, gain[None], wq, wk, wv, wo, cos, sin, lens)
@@ -874,6 +1037,8 @@
     gat,
     datt,
     dq_s,
+    qst_s,
+    dst_s,
     acc_q,
     dkv,
     kvo,
@@ -882,7 +1047,6 @@
     kvr,
     part,
     sums,
-    osums,
     csend,
     crecv,
     osend,
@@ -958,7 +1122,6 @@
     out_line = Line(z, nz, e, part_of(obuf), zos, zor)
     igrad_line = Line(z, nz, e, part_of(igbuf), zis, zir)
     normed_sum = LineSum(z, nz, e, csend, crecv, zps, zpr)
-    out_sum = LineSum(z, nz, e, osend, orecv, zqs, zqr)
 
     def z_copies(buf_of, send, recv):
         return [
@@ -1020,51 +1183,67 @@
     datt[...] = dot_nt(gat[...], wo_ref[...]).astype(bf16)
 
     ck = 2 * span
-    trip = (e * span + span - 1) // ck + 1
+    last = (e * span + span - 1) // ck
     stacked = groups * span
     kiota = lax.broadcasted_iota(jnp.int32, (ck, stacked), 0)
+    krow = lax.broadcasted_iota(jnp.int32, (ck, 1), 0)
     qpos = e * span + lax.rem(lax.broadcasted_iota(jnp.int32, (ck, stacked), 1), span)
+    drows = []
     for s in range(seqs):
         for h in range(heads):
-            srows = slice(s * span, (s + 1) * span)
 
             def gather(ref):
                 return jnp.concatenate(
                     [
-                        ref[srows, (h * groups + g) * HD : (h * groups + g + 1) * HD]
+                        ref[
+                            s * span : (s + 1) * span,
+                            (h * groups + g) * HD : (h * groups + g + 1) * HD,
+                        ]
                         for g in range(groups)
                     ],
                     0,
                 )
 
-            qst = gather(q_ref)
+            i = s * heads + h
+            qst_s[i] = gather(q_ref) * jnp.array(HD ** (-0.5), bf16)
             dst = gather(datt)
+            dst_s[i] = dst
             delta = jnp.sum(dst.astype(f32) * gather(att_ref), -1, keepdims=True)
-            drow = jnp.broadcast_to(delta, (stacked, 128)).T[0:1]
-            lrow = lrow_ref[s * heads + h, 0:1, :]
-            acc_q[...] = jnp.zeros_like(acc_q)
-
-            def chunk(c, carry):
-                at = pl.ds(pl.multiple_of(c * ck, 16), ck)
+            drows.append(jnp.broadcast_to(delta, (stacked, 128)).T[0:1])
+    acc_q[...] = jnp.zeros_like(acc_q)
+
+    def chunk(c, diagonal):
+        at = pl.ds(pl.multiple_of(c * ck, 16), ck)
+        for s in range(seqs):
+            for h in range(heads):
+                i = s * heads + h
                 keys = kv_ref[s, at, h * HD : (h + 1) * HD]
                 vals = kv_ref[s, at, kw + h * HD : kw + (h + 1) * HD]
-                scores = dot_nt(keys, qst) * HD ** (-0.5)
-                kpos = kiota + c * ck
-                soft = jnp.where(
-                    (kpos <= qpos) & (kpos < lens_ref[s]), jnp.exp(scores - lrow), 0.0
-                )
-                grad_probs = dot_nt(vals, dst)
-                grad_scores = (soft * (grad_probs - drow)).astype(bf16)
-                dkv[s, at, h * HD : (h + 1) * HD] = dot_nn(grad_scores, qst) * HD ** (-0.5)
-                dkv[s, at, kw + h * HD : kw + (h + 1) * HD] = dot_nn(soft.astype(bf16), dst)
-                acc_q[...] += dot_tn(grad_scores, keys)
-                return carry
-
-            lax.fori_loop(0, trip, chunk, 0)
-            result = acc_q[...] * HD ** (-0.5)
+                scores = dot_nt(keys, qst_s[i]) - lrow_ref[i, 0:1, :]
+                if diagonal:
+                    kpos = kiota + c * ck
+                    allowed = (kpos <= qpos) & (kpos < lens_ref[s])
+                    soft = jnp.where(allowed, jnp.exp(scores), 0.0)
+                else:
+                    soft = jnp.exp(scores + jnp.where(krow + c * ck < lens_ref[s], 0.0, -1e30))
+                grad_probs = dot_nt(vals, dst_s[i])
+                grad_scores = (soft * (grad_probs - drows[i])).astype(bf16)
+                dkv[s, at, h * HD : (h + 1) * HD] = dot_nn(grad_scores, qst_s[i])
+                dkv[s, at, kw + h * HD : kw + (h + 1) * HD] = dot_nn(soft.astype(bf16), dst_s[i])
+                acc_q[i] += dot_tn(grad_scores, keys)
+
+    def whole_chunk(c, carry):
+        chunk(c, False)
+        return carry
+
+    lax.fori_loop(0, last, whole_chunk, 0)
+    chunk(last, True)
+    for s in range(seqs):
+        for h in range(heads):
+            result = acc_q[s * heads + h] * HD ** (-0.5)
             for g in range(groups):
                 cols = slice((h * groups + g) * HD, (h * groups + g + 1) * HD)
-                dq_s[srows, cols] = result[g * span : (g + 1) * span]
+                dq_s[s * span : (s + 1) * span, cols] = result[g * span : (g + 1) * span]
 
     def key_rows(j, s):
         return dkv[s, pl.ds(pl.multiple_of(j * span, 16), span), :]
@@ -1105,10 +1284,17 @@
     lax.fori_loop(0, half - 1, key_pass, 0)
     w1.give()
 
+    def mixed_last(k, to):
+        return remote(osend.at[k - 1], orecv.at[k - 1], zqs.at[k - 1], zqr.at[k - 1], (e, to))
+
     mixed_own.wait()
     for t in range(1, half):
         mixed_send(t).wait_recv()
-    out_sum.hop(0, mixed_sum)
+    for k in range(1, nz):
+        zz = lax.rem(z + k, nz)
+        osend[k - 1] = mixed_sum(zz).astype(bf16)
+        mixed_last(k, zz).start()
+    own_mixed = mid_ref[...] + mixed_sum(z)
     w1.spread()
     for copy in z_arrivals(slot_of(sz1), z1s, z1r):
         copy.wait_recv()
@@ -1116,11 +1302,6 @@
     for zz in range(1, nz):
         rgrad = rgrad + dot_nn(sz1[zz][:, :rows], xn_ref[zz])
     sown[0:experts, :] = rgrad.astype(bf16)
-    for hop in range(1, nz - 1):
-        out_sum.hop(hop, mixed_sum)
-    out_sum.total(osums, mixed_sum)
-    obuf[own_rows, :] = (mid_ref[...] + osums[...]).astype(bf16)
-    out_line.start()
 
     key_send(0).wait_recv()
     own_kv = [key_rows(e, s) + kvi[0, s].astype(f32) for s in range(seqs)]
@@ -1136,8 +1317,14 @@
 
     for hop in range(nz - 1):
         normed_sum.hop(hop, normed_part)
-        out_line.hop(hop + 1)
+        if hop > 0:
+            out_line.hop(hop)
         if hop == 0:
+            for k in range(1, nz):
+                mixed_last(k, z).wait_recv()
+                own_mixed = own_mixed + orecv[k - 1].astype(f32)
+            obuf[own_rows, :] = own_mixed.astype(bf16)
+            out_line.start()
             again = jnp.sum(part[...] * x * scale1, 0, keepdims=True)
             sz2[z] = jnp.concatenate([again, ggrad_ref[...], jnp.zeros((14, width), f32)], 0).astype(
                 bf16
@@ -1165,6 +1352,7 @@
     )
     igbuf[own_rows, :] = igrad.astype(bf16)
     igrad_line.start()
+    out_line.hop(nz - 1)
 
     w1.forward()
     for copy in z_arrivals(slot_of(sz2), z2s, z2r):
@@ -1205,7 +1393,9 @@
 
     w1.arrive()
     w2.arrive()
-    for line in (gat_line, out_line, igrad_line, normed_sum, out_sum, w1, w2):
+    for k in range(1, nz):
+        mixed_last(k, z).wait_send()
+    for line in (gat_line, out_line, igrad_line, normed_sum, w1, w2):
         line.drain()
     for copy in z_copies(slot_of(sz1), z1s, z1r) + z_copies(slot_of(sz2), z2s, z2r):
         copy.wait_send()
@@ -1430,6 +1620,7 @@
     span = tok // seqs
     half = n // 2
     stacked = (qw // kw) * span
+    pairs = seqs * (kw // HD)
     experts = glog.shape[0]
     small_rows = experts + 16
     dma = pltpu.SemaphoreType.DMA
@@ -1465,7 +1656,9 @@
             pltpu.VMEM((tok, width), bf16),
             pltpu.VMEM((tok, qw), bf16),
             pltpu.VMEM((tok, qw), f32),
-            pltpu.VMEM((stacked, HD), f32),
+            pltpu.VMEM((pairs, stacked, HD), bf16),
+            pltpu.VMEM((pairs, stacked, HD), bf16),
+            pltpu.VMEM((pairs, stacked, HD), f32),
             pltpu.VMEM((seqs, n * span, 2 * kw), f32),
             pltpu.VMEM((half, seqs, span, 2 * kw), bf16),
             pltpu.VMEM((half, seqs, span, 2 * kw), bf16),
@@ -1473,11 +1666,10 @@
             pltpu.VMEM((half - 1, seqs, span, 2 * kw), bf16),
             pltpu.VMEM((tok, width), f32),
             pltpu.VMEM((rows, width), f32),
-            pltpu.VMEM((rows, width), f32),
             line_buf,
             line_buf,
-            line_buf,
-            line_buf,
+            pltpu.VMEM((nz - 1, rows, width), bf16),
+            pltpu.VMEM((nz - 1, rows, width), bf16),
             plane_bufs(2 * qw),
             plane_bufs(2 * kw),
             pltpu.VMEM((nz, experts, 128), bf16),
@@ -1487,8 +1679,8 @@
             pltpu.VMEM((half, small_rows, width), bf16),
             pltpu.VMEM((half, nz, rows, width), bf16),
         ]
-        + [line] * 10
-        + [zdma] * 4
+        + [line] * 8
+        + [zdma] * 6
         + [hdma, hdma, fdma, fdma]
         + [[hdma] * 8, [hdma] * 8]
         + [dma, dma, fdma, fdma]
@@ -1609,7 +1801,7 @@
             pltpu.VMEM(ddown.shape, f32),
             pltpu.SemaphoreType.DMA((2, 3)),
         ],
-        compiler_params=pltpu.CompilerParams(vmem_limit_bytes=48 << 20),
+        compiler_params=pltpu.CompilerParams(vmem_limit_bytes=60 << 20),
         name="finish",
     )(out_low, igrad_low, wall, wall2, small, load, dgate, dup, ddown)
 

time: 296 us -> 280 us (0.946)
  Pallas kernels: 260 us -> 251 us
  local copies, waits for them, and re-layouts: 12.7 us -> 4.05 us
    unnamed x49 -> x1, local copies, waits for them, and re-layouts: 11.9 us -> 1.87 us
    pallas_call x1, Pallas kernels: 99.5 us -> 89.7 us  [expert_layer(): pl.pallas_call(functools.partial(expert_kernel, n, nz, big), out_shape=ou...]
    pallas_call x1, Pallas kernels: 113 us -> 109 us  [return_layer(): pl.pallas_call(functools.partial(return_kernel, n, nz), out_shape=[sds((t...]
  transfers between devices with their start and end apart: 1 -> 1, of which waited for: 1 -> 1; matrix products, arithmetic and copies ran while one was open for 1% -> 1% of each run, Pallas kernels for 13% -> 15%
where the time goes in v6:
time: 280 us
  Pallas kernels  251 us (90%)
  between operations  14.1 us (5%)
  waiting for transfers between devices  7.69 us (3%)
  local copies, waits for them, and re-layouts  4.05 us (1%)
    pallas_call x1, Pallas kernels, return_layer(): pl.pallas_call(functools.partial(return_kernel, n, nz), out_shape=[sds((t...  109 us
    pallas_call x1, Pallas kernels, expert_layer(): pl.pallas_call(functools.partial(expert_kernel, n, nz, big), out_shape=ou...  89.7 us
    pallas_call x1, Pallas kernels, attend_layer(): pl.pallas_call(functools.partial(attend_kernel, n, nz), out_shape=[sds((r...  42.7 us
    pallas_call x1, Pallas kernels, finish_layer(): pl.pallas_call(finish_kernel, out_shape=[sds((tok, width), f32), sds((tok...  9.59 us
    all_gather x1, waiting for transfers between devices, shards(): lax.all_gather(cotangent.astype(bf16), 'expert', axis=0, tiled=True)  7.67 us
  transfers between devices with their start and end apart: 1, of which 1 were waited for; matrix products, arithmetic and copies ran while one was open for 1% of the time, Pallas kernels for 15%

profile of v6, /device:TPU:0, one launch (start us, length us, event | category | flops | bytes accessed | tf_op | source)
XLA Modules:
  0.0 279.8 jit_solution(10641653112710295579)
XLA Ops:
  7.2 0.0 all-gather.2.cloned.1.call-start
  7.2 2.4 convert_element_type.11
  9.6 0.0 all-gather.2.cloned.1.call-update
  9.7 0.2 multiply_sine_fusion
  9.9 0.1 tile.20
  10.0 0.2 tile.21
  10.2 0.8 copy.30.sin_ref
  11.0 0.1 tile.8
  11.1 0.2 tile.9
  11.3 0.8 copy.29.cos_ref
  12.1 42.7 %attend.1 = (f32[96,1024]{1,0:T(8,128)}, bf16[384,256]{1,0:T(8,128)(2,1)}, bf16[2,1536,256]{2,1,0:T(8,128)(2,1)}, f32[4,8,384]{2,1,0:T(8,128)}, f32[384,256]{1,0:T(8,128)}) custom-call(bf16[384,1024]{1,0:T(8,128)(2,1)} %x_ref.3, f32[1,1024]{1,0:T(1,128)} %bitcast.16, bf16[1024,256]{1,0:T(8,128)(2,1)} %wq_ref.3, bf16[1024,128]{1,0:T(8,128)(2,1)} %wk_ref.3, ...), custom_call_target="tpu_custom_call" | custom-call | tf_op jit(solution)/shard_map/attend/pallas_call | solution.py:979
  54.8 7.7 %all-gather.2.cloned.1.call-done.cot_all = bf16[3072,1024]{1,0:T(8,128)(2,1)} async-done(((bf16[384,1024]{1,0:T(8,128)(2,1)}), bf16[3072,1024]{1,0:T(8,128)(2,1)}) %all-gather.2.cloned.1.call-update) | async-done | bytes 6291472 | tf_op jit(solution)/shard_map/all_gather | solution.py:1835
  62.5 89.7 %experts.1 = (f32[96,1024]{1,0:T(8,128)}, bf16[32,128]{1,0:T(8,128)(2,1)}, f32[1,1024]{1,0:T(1,128)}, f32[1,32]{1,0:T(1,128)}, f32[4,1024,128]{2,1,0:T(8,128)}, ...) custom-call(f32[96,1024]{1,0:T(8,128)} %get-tuple-element.47.mid_ref, ...), custom_call_target="tpu_custom_call" | custom-call | tf_op jit(solution)/shard_map/experts/pallas_call | solution.py:775
  152.2 109.2 %attend_back.1 = (bf16[384,1024]{1,0:T(8,128)(2,1)}, bf16[384,1024]{1,0:T(8,128)(2,1)}, bf16[8,128,512]{2,1,0:T(8,128)(2,1)}, bf16[8,128,256]{2,1,0:T(8,128)(2,1)}, f32[48,1024]{1,0:T(8,128)}) custom-call(f32[96,1024]{1,0:T(8,128)} %get-tuple-element.48.gmid_ref, f32[96,1024]{1,0:T(8,128)} %get-tuple-element.47.mid_ref, ...), custom_call_target="tpu_custom_call" | custom-call | tf_op jit(solution)/shard_map/attend_back/pallas_call | solution.py:1642
  261.4 9.6 %finish.1 = (f32[384,1024]{1,0:T(8,128)}, f32[384,1024]{1,0:T(8,128)}, f32[1024,256]{1,0:T(8,128)}, f32[1024,128]{1,0:T(8,128)}, f32[1024,128]{1,0:T(8,128)}, /*...) custom-call(bf16[384,1024]{1,0:T(8,128)(2,1)} %get-tuple-element.57., ...), custom_call_target="tpu_custom_call" | custom-call | tf_op jit(solution)/shard_map/finish/pallas_call | solution.py:1778
  271.0 1.9 copy.33
  (2 shorter events, 0.0 us)
Async XLA Ops:
  7.2 55.3 %all-gather.2.cloned.1.call-start = ((), (), s32[]{:S(2)}) async-start(), calls=%async_computation | async-start | bytes 7077888 | tf_op jit(solution)/shard_map/all_gather | solution.py:1835
Sparse Core Ops, SparseCore 0:
  10.5 51.9 all-gather.1

commit v7 on v6

--- a/solution.py
+++ b/solution.py
@@ -803,23 +803,28 @@
     lrow_ref,
     att_ref,
     wqkv,
-    part,
+    wfull,
     qst_s,
     m_s,
     l_s,
     o_s,
-    zsend,
-    zin,
+    att_low,
+    acol,
     ks,
     kr,
     kfs,
     kfr,
     zgs,
     zgr,
+    gos,
+    gor,
+    gps,
+    gpr,
 ):
     e = lax.axis_index("expert")
     z = lax.axis_index("tensor")
-    sib = e + 1 - 2 * lax.rem(e, 2)
+    core = lax.rem(e, 2)
+    sib = e + 1 - 2 * core
     half = n // 2
     tok, width = x_ref.shape
     rows = tok // nz
@@ -849,12 +854,33 @@
     def rows_of(j, s):
         return kv_ref.at[s, pl.ds(pl.multiple_of(j * span, 16), span)]
 
+    half_rows = qw // 2
+    my_half = pl.ds(pl.multiple_of(core * half_rows, 16), half_rows)
+
+    def weight_send(k):
+        to = (e, lax.rem(z + k, nz))
+        return remote(
+            wo_ref.at[my_half], wfull.at[z, my_half], gos.at[k - 1], gor.at[k - 1], to
+        )
+
+    def weight_copy(zz, k, to):
+        ref = wfull.at[zz, my_half]
+        return remote(ref, ref, gos.at[k - 1], gor.at[k - 1], (e, to))
+
+    def weight_pass(zz, which, k):
+        at = pl.ds(pl.multiple_of(which * half_rows, 16), half_rows)
+        ref = wfull.at[zz, at]
+        return remote(ref, ref, gps.at[k - 1], gpr.at[k - 1], (sib, z))
+
     for t in range(1, half):
         to = (lax.rem(e + 2 * t, n), z)
         for s in range(seqs):
             remote(rows_of(e, s), rows_of(e, s), ks.at[t, s], kr.at[t, s], to).start()
     for s in range(seqs):
         remote(rows_of(e, s), rows_of(e, s), kfs.at[0, s], kfr.at[0, s], (sib, z)).start()
+    for k in range(1, nz):
+        weight_send(k).start()
+    wfull[z] = wo_ref[...]
 
     def forward(t, carry):
         src = lax.rem(e - 2 * t + n, n)
@@ -935,19 +961,31 @@
             logs = m_s[i] + jnp.log(l_s[i])
             lrow_ref[i] = logs.T[0:8]
 
-    part[...] = dot_nn(att_ref[...].astype(bf16), wo_ref[...])
+    att_low[...] = att_ref[...].astype(bf16)
+    own_rows = pl.ds(pl.multiple_of(z * rows, 16), rows)
+
+    def row_copy(k, to):
+        src = att_low.at[pl.ds(pl.multiple_of(to * rows, 16), rows)]
+        return remote(src, acol.at[z], zgs.at[k - 1], zgr.at[k - 1], (e, to))
+
     for k in range(1, nz):
-        zz = lax.rem(z + k, nz)
-        zsend[k - 1] = part[pl.ds(pl.multiple_of(zz * rows, 16), rows), :].astype(bf16)
-        remote(zsend.at[k - 1], zin.at[k - 1], zgs.at[k - 1], zgr.at[k - 1], (e, zz)).start()
-    own_rows = pl.ds(pl.multiple_of(z * rows, 16), rows)
-    mid = x_ref[own_rows, :].astype(f32) + part[own_rows, :]
+        row_copy(k, lax.rem(z + k, nz)).start()
+    acol[z] = att_low[own_rows, :]
     for k in range(1, nz):
-        remote(zsend.at[k - 1], zin.at[k - 1], zgs.at[k - 1], zgr.at[k - 1], (e, z)).wait_recv()
-        mid = mid + zin[k - 1].astype(f32)
+        zz = lax.rem(z + nz - k, nz)
+        weight_copy(zz, k, zz).wait_recv()
+        weight_pass(zz, core, k).start()
+    for k in range(1, nz):
+        row_copy(k, lax.rem(z + nz - k, nz)).wait_recv()
+        weight_pass(lax.rem(z + nz - k, nz), 1 - core, k).wait_recv()
+    mid = x_ref[own_rows, :].astype(f32)
+    for zz in range(nz):
+        mid = mid + dot_nn(acol[zz], wfull[zz])
     mid_ref[...] = mid
     for k in range(1, nz):
-        remote(zsend.at[k - 1], zin.at[k - 1], zgs.at[k - 1], zgr.at[k - 1], (e, z)).wait_send()
+        row_copy(k, lax.rem(z + k, nz)).wait_send()
+        weight_send(k).wait_send()
+        weight_pass(lax.rem(z + nz - k, nz), core, k).wait_send()
 
     def sent(t, carry):
         for s in range(seqs):
@@ -989,16 +1027,16 @@
         out_specs=[vmem] * 5,
         scratch_shapes=[
             pltpu.VMEM((width, qw + 2 * kw), bf16),
-            pltpu.VMEM((tok, width), f32),
+            pltpu.VMEM((nz, qw, width), bf16),
             pltpu.VMEM((pairs, stacked, HD), bf16),
             pltpu.VMEM((pairs, stacked, 128), f32),
             pltpu.VMEM((pairs, stacked, 128), f32),
             pltpu.VMEM((pairs, stacked, HD), f32),
-            pltpu.VMEM((nz - 1, rows, width), bf16),
-            pltpu.VMEM((nz - 1, rows, width), bf16),
+            pltpu.VMEM((tok, qw), bf16),
+            pltpu.VMEM((nz, rows, qw), bf16),
         ]
         + [dma((half, seqs))] * 4
-        + [dma((nz - 1,))] * 2,
+        + [dma((nz - 1,))] * 6,
         compiler_params=pltpu.CompilerParams(
             collective_id=2, has_side_effects=True, vmem_limit_bytes=60 << 20
         ),
@@ -1760,7 +1798,7 @@
     flat = wall2[...].reshape(chunks * dn, 2 * kw).astype(f32)
     k_ref[...] = flat[:, :kw]
     v_ref[...] = flat[:, kw:]
-    router_ref[...] = small[0:experts, :].T
+    router_ref[...] = small[0:experts, :]
     again_ref[...] = small[experts : experts + 1, :]
     egain_ref[...] = small[experts + 1 : experts + 2, :]
     load_ref[...] = load[...]
@@ -1784,7 +1822,7 @@
             sds((width, kw), f32),
             sds((width, kw), f32),
             sds((qw, width), f32),
-            sds((width, experts), f32),
+            sds((experts, width), f32),
             sds((1, width), f32),
             sds((1, width), f32),
             sds((1, 1), f32),
@@ -1827,11 +1865,12 @@
     tok_rows = inputs.shape[0]
     seq_count = seq_lens.shape[0]
     span_rows = tok_rows // seq_count
-    local_pos = lax.axis_index("expert") * span_rows + jnp.arange(span_rows, dtype=jnp.int32)
-    frequency = THETA ** (-2.0 * jnp.arange(HD // 2, dtype=jnp.float32) / HD)
-    angles = local_pos.astype(f32)[:, None] * frequency[None, :]
-    cosines = jnp.tile(jnp.cos(angles), (seq_count, 4))
-    sines = jnp.tile(jnp.sin(angles), (seq_count, 4))
+    row = lax.broadcasted_iota(jnp.int32, (tok_rows, 128), 0) % span_rows
+    lane = lax.broadcasted_iota(jnp.int32, (tok_rows, 128), 1) % (HD // 2)
+    frequency = THETA ** (-2.0 * lane.astype(f32) / HD)
+    angles = (lax.axis_index("expert") * span_rows + row).astype(f32) * frequency
+    cosines = jnp.cos(angles)
+    sines = jnp.sin(angles)
     cot_all = lax.all_gather(cotangent.astype(bf16), "expert", axis=0, tiled=True)
     weights = (query_weight, key_weight, value_weight, out_weight, cosines, sines)
     middle, queries, pairs, logs, attended = attend_layer(
@@ -1917,7 +1956,7 @@
         value_grad,
         out_weight_grad,
         expert_gain_grad[0],
-        router_grad,
+        router_grad.T,
         gate_grad,
         up_grad,
         down_grad.reshape(down_weight.shape),

time: 280 us -> 274 us (0.979)
  Pallas kernels: 251 us -> 242 us
  waiting for transfers between devices: 7.69 us -> 13.1 us
  local copies, waits for them, and re-layouts: 4.05 us -> 0 us
    all_gather x1, waiting for transfers between devices: 7.67 us -> 13.1 us  [shards(): lax.all_gather(cotangent.astype(bf16), 'expert', axis=0, tiled=True)]
    pallas_call x1, Pallas kernels: 42.7 us -> 37.5 us  [attend_layer(): pl.pallas_call(functools.partial(attend_kernel, n, nz), out_shape=[sds((r...]
    pallas_call x1, Pallas kernels: 89.7 us -> 86.3 us  [expert_layer(): pl.pallas_call(functools.partial(expert_kernel, n, nz, big), out_shape=ou...]
  transfers between devices with their start and end apart: 1 -> 1, of which waited for: 1 -> 1; matrix products, arithmetic and copies ran while one was open for 1% -> 1% of each run, Pallas kernels for 15% -> 14%
where the time goes in v7:
time: 274 us
  Pallas kernels  242 us (88%)
  between operations  14.1 us (5%)
  waiting for transfers between devices  13.1 us (5%)
  other arithmetic  4.51 us (2%)
    pallas_call x1, Pallas kernels, return_layer(): pl.pallas_call(functools.partial(return_kernel, n, nz), out_shape=[sds((t...  109 us
    pallas_call x1, Pallas kernels, expert_layer(): pl.pallas_call(functools.partial(expert_kernel, n, nz, big), out_shape=ou...  86.3 us
    pallas_call x1, Pallas kernels, attend_layer(): pl.pallas_call(functools.partial(attend_kernel, n, nz), out_shape=[sds((r...  37.5 us
    all_gather x1, waiting for transfers between devices, shards(): lax.all_gather(cotangent.astype(bf16), 'expert', axis=0, tiled=True)  13.1 us
    pallas_call x1, Pallas kernels, finish_layer(): pl.pallas_call(finish_kernel, out_shape=[sds((tok, width), f32), sds((tok...  9.46 us
  transfers between devices with their start and end apart: 1, of which 1 were waited for; matrix products, arithmetic and copies ran while one was open for 1% of the time, Pallas kernels for 14%

profile of v7, /device:TPU:0, one launch (start us, length us, event | category | flops | bytes accessed | tf_op | source)
XLA Modules:
  0.0 273.6 jit_solution(14980423979075499309)
XLA Ops:
  7.2 0.0 all-gather.2.cloned.1.call-start
  7.2 2.4 convert_element_type.11
  9.6 0.0 all-gather.2.cloned.1.call-update
  9.7 2.1 fusion
  11.8 37.5 %attend.1 = (f32[96,1024]{1,0:T(8,128)}, bf16[384,256]{1,0:T(8,128)(2,1)}, bf16[2,1536,256]{2,1,0:T(8,128)(2,1)}, f32[4,8,384]{2,1,0:T(8,128)}, f32[384,256]{1,0:T(8,128)}) custom-call(bf16[384,1024]{1,0:T(8,128)(2,1)} %x_ref.3, f32[1,1024]{1,0:T(1,128)} %bitcast.13, bf16[1024,256]{1,0:T(8,128)(2,1)} %wq_ref.3, bf16[1024,128]{1,0:T(8,128)(2,1)} %wk_ref.3, ...), custom_call_target="tpu_custom_call" | custom-call | tf_op jit(solution)/shard_map/attend/pallas_call | solution.py:1017
  49.2 13.1 %all-gather.2.cloned.1.call-done.cot_all = bf16[3072,1024]{1,0:T(8,128)(2,1)} async-done(((bf16[384,1024]{1,0:T(8,128)(2,1)}), bf16[3072,1024]{1,0:T(8,128)(2,1)}) %all-gather.2.cloned.1.call-update) | async-done | bytes 6291472 | tf_op jit(solution)/shard_map/all_gather | solution.py:1874
  62.3 86.3 %experts.1 = (f32[96,1024]{1,0:T(8,128)}, bf16[32,128]{1,0:T(8,128)(2,1)}, f32[1,1024]{1,0:T(1,128)}, f32[1,32]{1,0:T(1,128)}, f32[4,1024,128]{2,1,0:T(8,128)}, ...) custom-call(f32[96,1024]{1,0:T(8,128)} %get-tuple-element.47.mid_ref, ...), custom_call_target="tpu_custom_call" | custom-call | tf_op jit(solution)/shard_map/experts/pallas_call | solution.py:775
  148.7 108.6 %attend_back.1 = (bf16[384,1024]{1,0:T(8,128)(2,1)}, bf16[384,1024]{1,0:T(8,128)(2,1)}, bf16[8,128,512]{2,1,0:T(8,128)(2,1)}, bf16[8,128,256]{2,1,0:T(8,128)(2,1)}, f32[48,1024]{1,0:T(8,128)}) custom-call(f32[96,1024]{1,0:T(8,128)} %get-tuple-element.48.gmid_ref, f32[96,1024]{1,0:T(8,128)} %get-tuple-element.47.mid_ref, ...), custom_call_target="tpu_custom_call" | custom-call | tf_op jit(solution)/shard_map/attend_back/pallas_call | solution.py:1680
  257.3 9.5 %finish.1 = (f32[384,1024]{1,0:T(8,128)}, f32[384,1024]{1,0:T(8,128)}, f32[1024,256]{1,0:T(8,128)}, f32[1024,128]{1,0:T(8,128)}, f32[1024,128]{1,0:T(8,128)}, /*...) custom-call(bf16[384,1024]{1,0:T(8,128)(2,1)} %get-tuple-element.57., ...), custom_call_target="tpu_custom_call" | custom-call | tf_op jit(solution)/shard_map/finish/pallas_call | solution.py:1816
  (4 shorter events, 0.0 us)
Async XLA Ops:
  7.2 55.2 %all-gather.2.cloned.1.call-start = ((), (), s32[]{:S(2)}) async-start(), calls=%async_computation | async-start | bytes 7077888 | tf_op jit(solution)/shard_map/all_gather | solution.py:1874
Sparse Core Ops, SparseCore 0:
  10.5 51.8 all-gather.1

commit v8 on v7

--- a/solution.py
+++ b/solution.py
@@ -1124,6 +1124,7 @@
     ofs,
     ofr,
     olsem,
+    obase,
 ):
     e = lax.axis_index("expert")
     z = lax.axis_index("tensor")
@@ -1185,26 +1186,65 @@
     for copy in z_copies(slot_of(sz1), z1s, z1r):
         copy.start()
 
-    def mixed_send(t):
-        h = lax.rem(me + half - t, half)
-        return remote(
-            mixed_hbm.at[:, pl.ds(pl.multiple_of(h * rows, 16), rows), :],
-            ofin.at[t],
-            ofs.at[t - 1],
-            ofr.at[t - 1],
-            (lax.rem(e - 2 * t + n, n), z),
-        )
-
-    for t in range(1, half):
-        mixed_send(t).start()
-    mixed_own = pltpu.make_async_copy(
-        mixed_hbm.at[:, pl.ds(pl.multiple_of(me * rows, 16), rows), :], ofin.at[0], olsem
-    )
-    mixed_own.start()
+    square = half == 4
+    chip_x = me + 1 - 2 * lax.rem(me, 2)
+    chip_y = lax.rem(me + 2, 4)
+    chip_d = 3 - me
+    low, high = pl.ds(0, nz // 2), pl.ds(nz // 2, nz - nz // 2)
+
+    def mixed_at(chip, which=slice(None)):
+        return mixed_hbm.at[which, pl.ds(pl.multiple_of(chip * rows, 16), rows), :]
+
+    def mixed_copy(src, dst, i, chip):
+        return remote(src, dst, ofs.at[i], ofr.at[i], (2 * chip + core, z))
+
+    def mixed_sends():
+        if not square:
+            return [
+                mixed_copy(
+                    mixed_at(lax.rem(me + half - t, half)),
+                    ofin.at[t],
+                    t - 1,
+                    lax.rem(me + half - t, half),
+                )
+                for t in range(1, half)
+            ]
+        return [
+            mixed_copy(mixed_at(chip_d, low), ofin.at[3, low], 0, chip_x),
+            mixed_copy(mixed_at(chip_d, high), ofin.at[3, high], 1, chip_y),
+            mixed_copy(mixed_at(chip_x, low), ofin.at[1, low], 2, chip_x),
+            mixed_copy(mixed_at(chip_y, high), ofin.at[2, high], 3, chip_y),
+        ]
+
+    def mixed_relays():
+        return [
+            mixed_copy(obase.at[low], ofin.at[2, low], 4, chip_y),
+            mixed_copy(obase.at[high], ofin.at[1, high], 5, chip_x),
+        ]
+
+    for copy in mixed_sends():
+        copy.start()
+    mixed_own = [pltpu.make_async_copy(mixed_at(me), ofin.at[0], olsem.at[0])]
+    if square:
+        mixed_own += [
+            pltpu.make_async_copy(mixed_at(chip_y, low), obase.at[low], olsem.at[1]),
+            pltpu.make_async_copy(mixed_at(chip_x, high), obase.at[high], olsem.at[2]),
+        ]
+    for copy in mixed_own:
+        copy.start()
+
+    def mixed_relay():
+        waits = mixed_sends()
+        for copy, part, i in zip(mixed_relays(), (low, high), (0, 1)):
+            waits[i].wait_recv()
+            obase[part] = (obase[part].astype(f32) + ofin[3, part].astype(f32)).astype(bf16)
+            copy.start()
+
+    mixed_count = 3 if square else half
 
     def mixed_sum(zz):
         total = ofin[0, zz].astype(f32)
-        for t in range(1, half):
+        for t in range(1, mixed_count):
             total = total + ofin[t, zz].astype(f32)
         return total
 
@@ -1249,6 +1289,10 @@
             delta = jnp.sum(dst.astype(f32) * gather(att_ref), -1, keepdims=True)
             drows.append(jnp.broadcast_to(delta, (stacked, 128)).T[0:1])
     acc_q[...] = jnp.zeros_like(acc_q)
+    for copy in mixed_own:
+        copy.wait()
+    if square:
+        mixed_relay()
 
     def chunk(c, diagonal):
         at = pl.ds(pl.multiple_of(c * ck, 16), ck)
@@ -1325,9 +1369,8 @@
     def mixed_last(k, to):
         return remote(osend.at[k - 1], orecv.at[k - 1], zqs.at[k - 1], zqr.at[k - 1], (e, to))
 
-    mixed_own.wait()
-    for t in range(1, half):
-        mixed_send(t).wait_recv()
+    for copy in mixed_sends()[2:] + mixed_relays() if square else mixed_sends():
+        copy.wait_recv()
     for k in range(1, nz):
         zz = lax.rem(z + k, nz)
         osend[k - 1] = mixed_sum(zz).astype(bf16)
@@ -1438,8 +1481,8 @@
     for copy in z_copies(slot_of(sz1), z1s, z1r) + z_copies(slot_of(sz2), z2s, z2r):
         copy.wait_send()
     small_sib.wait_send()
-    for t in range(1, half):
-        mixed_send(t).wait_send()
+    for copy in mixed_sends() + (mixed_relays() if square else []):
+        copy.wait_send()
 
     def drained(t, carry):
         key_send(t).wait_send()
@@ -1722,7 +1765,8 @@
         + [hdma, hdma, fdma, fdma]
         + [[hdma] * 8, [hdma] * 8]
         + [dma, dma, fdma, fdma]
-        + [fdma, fdma, dma],
+        + [dma((6 if half == 4 else half - 1,))] * 2
+        + [dma((3,)), pltpu.VMEM((nz, rows, width), bf16)],
         compiler_params=pltpu.CompilerParams(
             collective_id=3, has_side_effects=True, vmem_limit_bytes=58 << 20
         ),

time: 274 us -> 264 us (0.964)
  Pallas kernels: 242 us -> 232 us
    pallas_call x1, Pallas kernels: 109 us -> 99 us  [return_layer(): pl.pallas_call(functools.partial(return_kernel, n, nz), out_shape=[sds((t...]
where the time goes in v8:
time: 264 us
  Pallas kernels  232 us (88%)
  between operations  14.1 us (5%)
  waiting for transfers between devices  13.1 us (5%)
  other arithmetic  4.51 us (2%)
    pallas_call x1, Pallas kernels, return_layer(): pl.pallas_call(functools.partial(return_kernel, n, nz), out_shape=[sds((t...  99 us
    pallas_call x1, Pallas kernels, expert_layer(): pl.pallas_call(functools.partial(expert_kernel, n, nz, big), out_shape=ou...  86.3 us
    pallas_call x1, Pallas kernels, attend_layer(): pl.pallas_call(functools.partial(attend_kernel, n, nz), out_shape=[sds((r...  37.5 us
    all_gather x1, waiting for transfers between devices, shards(): lax.all_gather(cotangent.astype(bf16), 'expert', axis=0, tiled=True)  13.1 us
    pallas_call x1, Pallas kernels, finish_layer(): pl.pallas_call(finish_kernel, out_shape=[sds((tok, width), f32), sds((tok...  9.46 us
  transfers between devices with their start and end apart: 1, of which 1 were waited for; matrix products, arithmetic and copies ran while one was open for 1% of the time, Pallas kernels for 14%

profile of v8, /device:TPU:0, one launch (start us, length us, event | category | flops | bytes accessed | tf_op | source)
XLA Modules:
  0.0 264.0 jit_solution(5245244643029428115)
XLA Ops:
  7.2 0.0 all-gather.2.cloned.1.call-start
  7.2 2.4 convert_element_type.11
  9.6 0.0 all-gather.2.cloned.1.call-update
  9.7 2.1 fusion
  11.8 37.5 %attend.1 = (f32[96,1024]{1,0:T(8,128)}, bf16[384,256]{1,0:T(8,128)(2,1)}, bf16[2,1536,256]{2,1,0:T(8,128)(2,1)}, f32[4,8,384]{2,1,0:T(8,128)}, f32[384,256]{1,0:T(8,128)}) custom-call(bf16[384,1024]{1,0:T(8,128)(2,1)} %x_ref.3, f32[1,1024]{1,0:T(1,128)} %bitcast.13, bf16[1024,256]{1,0:T(8,128)(2,1)} %wq_ref.3, bf16[1024,128]{1,0:T(8,128)(2,1)} %wk_ref.3, ...), custom_call_target="tpu_custom_call" | custom-call | tf_op jit(solution)/shard_map/attend/pallas_call | solution.py:1017
  49.2 13.1 %all-gather.2.cloned.1.call-done.cot_all = bf16[3072,1024]{1,0:T(8,128)(2,1)} async-done(((bf16[384,1024]{1,0:T(8,128)(2,1)}), bf16[3072,1024]{1,0:T(8,128)(2,1)}) %all-gather.2.cloned.1.call-update) | async-done | bytes 6291472 | tf_op jit(solution)/shard_map/all_gather | solution.py:1918
  62.3 86.3 %experts.1 = (f32[96,1024]{1,0:T(8,128)}, bf16[32,128]{1,0:T(8,128)(2,1)}, f32[1,1024]{1,0:T(1,128)}, f32[1,32]{1,0:T(1,128)}, f32[4,1024,128]{2,1,0:T(8,128)}, ...) custom-call(f32[96,1024]{1,0:T(8,128)} %get-tuple-element.47.mid_ref, ...), custom_call_target="tpu_custom_call" | custom-call | tf_op jit(solution)/shard_map/experts/pallas_call | solution.py:775
  148.7 99.0 %attend_back.1 = (bf16[384,1024]{1,0:T(8,128)(2,1)}, bf16[384,1024]{1,0:T(8,128)(2,1)}, bf16[8,128,512]{2,1,0:T(8,128)(2,1)}, bf16[8,128,256]{2,1,0:T(8,128)(2,1)}, f32[48,1024]{1,0:T(8,128)}) custom-call(f32[96,1024]{1,0:T(8,128)} %get-tuple-element.48.gmid_ref, f32[96,1024]{1,0:T(8,128)} %get-tuple-element.47.mid_ref, ...), custom_call_target="tpu_custom_call" | custom-call | tf_op jit(solution)/shard_map/attend_back/pallas_call | solution.py:1723
  247.7 9.5 %finish.1 = (f32[384,1024]{1,0:T(8,128)}, f32[384,1024]{1,0:T(8,128)}, f32[1024,256]{1,0:T(8,128)}, f32[1024,128]{1,0:T(8,128)}, f32[1024,128]{1,0:T(8,128)}, /*...) custom-call(bf16[384,1024]{1,0:T(8,128)(2,1)} %get-tuple-element.57., ...), custom_call_target="tpu_custom_call" | custom-call | tf_op jit(solution)/shard_map/finish/pallas_call | solution.py:1860
  (4 shorter events, 0.0 us)
Async XLA Ops:
  7.2 55.2 %all-gather.2.cloned.1.call-start = ((), (), s32[]{:S(2)}) async-start(), calls=%async_computation | async-start | bytes 7077888 | tf_op jit(solution)/shard_map/all_gather | solution.py:1918
Sparse Core Ops, SparseCore 0:
  10.5 51.8 all-gather.1

commit v9 on v8

--- a/solution.py
+++ b/solution.py
@@ -153,8 +153,6 @@
         zgr,
         zggs,
         zggr,
-        zds,
-        zdr,
         picks_s,
     ) = rest
     e = lax.axis_index("expert")
@@ -279,36 +277,39 @@
                 x_row(zz, me, g, s, to).start()
             x_small(zz, me, g, s, to).start()
 
-    def relays():
-        low = x_part(z, chip_x, 0, mid_row, 0, 2, chip_y)
-        high = x_part(z, chip_y, mid_row, rows - mid_row, 0, 3, chip_x)
-        return low, high
-
-    def z_diag(zz, k, to):
-        ref = xbuf.at[zz, core, pl.ds(pl.multiple_of(chip_d * rows, 16), rows)]
-        return remote(ref, ref, zds.at[k - 1], zdr.at[k - 1], (e, to))
+    def relays(g):
+        zz = piece_of(g)
+        return (
+            x_part(zz, chip_x, 0, mid_row, g, 2, chip_y),
+            x_part(zz, chip_y, mid_row, rows - mid_row, g, 3, chip_x),
+        )
+
+    def relay_pieces(g):
+        zz = piece_of(g)
+        low, high = relays(g)
+        x_part(zz, chip_x, 0, rows, g, 0, chip_x).wait_recv()
+        low.start()
+        x_part(zz, chip_y, 0, rows, g, 1, chip_y).wait_recv()
+        high.start()
 
     push_piece(jnp.int32(0))
-    for k in range(1, nz):
+    def z_push(k):
         z_row(z, k, lax.rem(z + k, nz)).start()
         z_small(z, k, lax.rem(z + k, nz)).start()
 
+    for k in range(1, min(nz, 2) if square else nz):
+        z_push(k)
+
     if square:
-        low, high = relays()
-        x_part(z, chip_x, 0, rows, 0, 0, chip_x).wait_recv()
-        low.start()
-        x_part(z, chip_y, 0, rows, 0, 1, chip_y).wait_recv()
-        high.start()
+        relay_pieces(jnp.int32(0))
+        if nz > 2:
+            z_push(2)
 
     dgate[...] = jnp.zeros_like(dgate)
     dup[...] = jnp.zeros_like(dup)
     ddown[...] = jnp.zeros_like(ddown)
     for copy in loads:
         copy.wait()
-    if square:
-        x_part(z, chip_d, 0, mid_row, 0, 2, chip_y).wait_recv()
-        x_part(z, chip_d, mid_row, rows - mid_row, 0, 3, chip_x).wait_recv()
-        z_diag(z, 1, lax.rem(z + 1, nz)).start()
 
     sel_row = lax.broadcasted_iota(jnp.int32, (experts, fc), 0)
     sel_col = lax.broadcasted_iota(jnp.int32, (experts, fc), 1)
@@ -523,12 +524,8 @@
             push_piece(g + 1)
 
         if square:
-
-            @pl.when(g > 0)
-            def _():
-                x_part(zz, chip_x, 0, rows, g, 0, chip_x).wait_recv()
-                x_part(zz, chip_y, 0, rows, g, 1, chip_y).wait_recv()
-                z_diag(zz, g, zz).wait_recv()
+            x_part(zz, chip_d, 0, mid_row, g, 2, chip_y).wait_recv()
+            x_part(zz, chip_d, mid_row, rows - mid_row, g, 3, chip_x).wait_recv()
 
         for s in range(1, half):
             h = lax.rem(me + half - s, half)
@@ -547,11 +544,15 @@
 
         block(zz, core, 0, hold, hold_o, hold_g, slot)
         if square:
-            for k in range(2, nz):
-
-                @pl.when(g == k - 2)
-                def _():
-                    z_diag(z, k, lax.rem(z + k, nz)).start()
+
+            @pl.when(g == 0)
+            def _():
+                for k in range(3, nz):
+                    z_push(k)
+
+            @pl.when(g < nz - 1)
+            def _():
+                relay_pieces(g + 1)
 
 
         @pl.when(g < nz - 1)
@@ -653,11 +654,6 @@
 
     for copy in grads:
         copy.wait()
-    if square:
-        for copy in relays():
-            copy.wait_send()
-        for k in range(1, nz):
-            z_diag(z, k, z).wait_send()
     for k in range(1, nz):
         z_row(z, k, z).wait_send()
         z_small(z, k, z).wait_send()
@@ -672,7 +668,7 @@
         if square:
             x_part(z, me, 0, rows, g, 0, chip_x).wait_send()
             x_part(z, me, 0, rows, g, 1, chip_y).wait_send()
-            for copy in half_copies(g):
+            for copy in relays(g) + tuple(half_copies(g)):
                 copy.wait_send()
         for s in range(1, half):
             if not square:
@@ -771,7 +767,7 @@
     scratch += [dma((2,))] * 6
     scratch += [dma((nz, 6 if half == 4 else half - 1))] * 2
     scratch += [dma((nz, half - 1))] * 2
-    scratch += [dma((nz - 1,))] * 6 + [pltpu.VMEM((nz * rows, 128), f32)]
+    scratch += [dma((nz - 1,))] * 4 + [pltpu.VMEM((nz * rows, 128), f32)]
     return pl.pallas_call(
         functools.partial(expert_kernel, n, nz, big),
         out_shape=out_shape,

time: 264 us -> 259 us (0.981)
  Pallas kernels: 232 us -> 226 us
    pallas_call x1, Pallas kernels: 86.3 us -> 81.5 us  [expert_layer(): pl.pallas_call(functools.partial(expert_kernel, n, nz, big), out_shape=ou...]
  transfers between devices with their start and end apart: 1 -> 1, of which waited for: 1 -> 1; matrix products, arithmetic and copies ran while one was open for 1% -> 1% of each run, Pallas kernels for 14% -> 15%
where the time goes in v9:
time: 259 us; the launch traced here: 258 us
  Pallas kernels  226 us (87%)
  between operations  14.1 us (5%)
  waiting for transfers between devices  13.1 us (5%)
  other arithmetic  4.51 us (2%)
    pallas_call x1, Pallas kernels, return_layer(): pl.pallas_call(functools.partial(return_kernel, n, nz), out_shape=[sds((t...  98 us
    pallas_call x1, Pallas kernels, expert_layer(): pl.pallas_call(functools.partial(expert_kernel, n, nz, big), out_shape=ou...  81.5 us
    pallas_call x1, Pallas kernels, attend_layer(): pl.pallas_call(functools.partial(attend_kernel, n, nz), out_shape=[sds((r...  37.5 us
    all_gather x1, waiting for transfers between devices, shards(): lax.all_gather(cotangent.astype(bf16), 'expert', axis=0, tiled=True)  13.1 us
    pallas_call x1, Pallas kernels, finish_layer(): pl.pallas_call(finish_kernel, out_shape=[sds((tok, width), f32), sds((tok...  9.46 us
  transfers between devices with their start and end apart: 1, of which 1 were waited for; matrix products, arithmetic and copies ran while one was open for 1% of the time, Pallas kernels for 15%

profile of v9, /device:TPU:0, one launch (start us, length us, event | category | flops | bytes accessed | tf_op | source)
XLA Modules:
  0.0 258.2 jit_solution(796061984879205693)
XLA Ops:
  7.2 0.0 all-gather.2.cloned.1.call-start
  7.2 2.4 convert_element_type.11
  9.6 0.0 all-gather.2.cloned.1.call-update
  9.7 2.1 fusion
  11.8 37.5 %attend.1 = (f32[96,1024]{1,0:T(8,128)}, bf16[384,256]{1,0:T(8,128)(2,1)}, bf16[2,1536,256]{2,1,0:T(8,128)(2,1)}, f32[4,8,384]{2,1,0:T(8,128)}, f32[384,256]{1,0:T(8,128)}) custom-call(bf16[384,1024]{1,0:T(8,128)(2,1)} %x_ref.3, f32[1,1024]{1,0:T(1,128)} %bitcast.13, bf16[1024,256]{1,0:T(8,128)(2,1)} %wq_ref.3, bf16[1024,128]{1,0:T(8,128)(2,1)} %wk_ref.3, ...), custom_call_target="tpu_custom_call" | custom-call | tf_op jit(solution)/shard_map/attend/pallas_call | solution.py:1013
  49.2 13.1 %all-gather.2.cloned.1.call-done.cot_all = bf16[3072,1024]{1,0:T(8,128)(2,1)} async-done(((bf16[384,1024]{1,0:T(8,128)(2,1)}), bf16[3072,1024]{1,0:T(8,128)(2,1)}) %all-gather.2.cloned.1.call-update) | async-done | bytes 6291472 | tf_op jit(solution)/shard_map/all_gather | solution.py:1914
  62.3 81.5 %experts.1 = (f32[96,1024]{1,0:T(8,128)}, bf16[32,128]{1,0:T(8,128)(2,1)}, f32[1,1024]{1,0:T(1,128)}, f32[1,32]{1,0:T(1,128)}, f32[4,1024,128]{2,1,0:T(8,128)}, ...) custom-call(f32[96,1024]{1,0:T(8,128)} %get-tuple-element.47.mid_ref, ...), custom_call_target="tpu_custom_call" | custom-call | tf_op jit(solution)/shard_map/experts/pallas_call | solution.py:771
  143.9 98.0 %attend_back.1 = (bf16[384,1024]{1,0:T(8,128)(2,1)}, bf16[384,1024]{1,0:T(8,128)(2,1)}, bf16[8,128,512]{2,1,0:T(8,128)(2,1)}, bf16[8,128,256]{2,1,0:T(8,128)(2,1)}, f32[48,1024]{1,0:T(8,128)}) custom-call(f32[96,1024]{1,0:T(8,128)} %get-tuple-element.48.gmid_ref, f32[96,1024]{1,0:T(8,128)} %get-tuple-element.47.mid_ref, ...), custom_call_target="tpu_custom_call" | custom-call | tf_op jit(solution)/shard_map/attend_back/pallas_call | solution.py:1719
  241.8 9.5 %finish.1 = (f32[384,1024]{1,0:T(8,128)}, f32[384,1024]{1,0:T(8,128)}, f32[1024,256]{1,0:T(8,128)}, f32[1024,128]{1,0:T(8,128)}, f32[1024,128]{1,0:T(8,128)}, /*...) custom-call(bf16[384,1024]{1,0:T(8,128)(2,1)} %get-tuple-element.57., ...), custom_call_target="tpu_custom_call" | custom-call | tf_op jit(solution)/shard_map/finish/pallas_call | solution.py:1856
  (4 shorter events, 0.0 us)
Async XLA Ops:
  7.2 55.2 %all-gather.2.cloned.1.call-start = ((), (), s32[]{:S(2)}) async-start(), calls=%async_computation | async-start | bytes 7077888 | tf_op jit(solution)/shard_map/all_gather | solution.py:1914
Sparse Core Ops, SparseCore 0:
  10.5 51.8 all-gather.1

commit v10 on v9

--- a/solution.py
+++ b/solution.py
@@ -792,12 +792,14 @@
     wo_ref,
     cos_ref,
     sin_ref,
+    cot_ref,
     lens_ref,
     mid_ref,
     q_ref,
     kv_ref,
     lrow_ref,
     att_ref,
+    cot_hbm,
     wqkv,
     wfull,
     qst_s,
@@ -816,12 +818,19 @@
     gor,
     gps,
     gpr,
+    cot_low,
+    cs,
+    cr,
+    cps,
+    cpr,
+    csem,
 ):
     e = lax.axis_index("expert")
     z = lax.axis_index("tensor")
     core = lax.rem(e, 2)
     sib = e + 1 - 2 * core
     half = n // 2
+    me = e // 2
     tok, width = x_ref.shape
     rows = tok // nz
     qw = wq_ref.shape[1]
@@ -845,6 +854,11 @@
         kv_ref[s, pl.ds(pl.multiple_of(e * span, 16), span)] = turned[
             s * span : (s + 1) * span, qw:
         ]
+    cot_low[...] = cot_ref[...].astype(bf16)
+    cot_local = pltpu.make_async_copy(
+        cot_low, cot_hbm.at[pl.ds(pl.multiple_of(e * tok, 16), tok)], csem
+    )
+    cot_local.start()
     pl.semaphore_wait(barrier, half + nz - 1)
 
     def rows_of(j, s):
@@ -876,6 +890,42 @@
         remote(rows_of(e, s), rows_of(e, s), kfs.at[0, s], kfr.at[0, s], (sib, z)).start()
     for k in range(1, nz):
         weight_send(k).start()
+
+    square = half == 4
+    chip_x = me + 1 - 2 * lax.rem(me, 2)
+    chip_y = lax.rem(me + 2, 4)
+    chip_d = 3 - me
+    low_rows = tok // 2
+
+    def cot_at(chip, first=0, count=tok):
+        start = (2 * chip + core) * tok + first
+        return cot_hbm.at[pl.ds(pl.multiple_of(start, 16), count)]
+
+    def cot_send(i, chip):
+        return remote(cot_low, cot_at(me), cs.at[i], cr.at[i], (2 * chip + core, z))
+
+    def cot_recv(i, chip):
+        return remote(cot_at(chip), cot_at(chip), cs.at[i], cr.at[i], (2 * chip + core, z))
+
+    def cot_relay(i, chip, to):
+        ref = cot_at(chip, 0, low_rows) if i == 2 else cot_at(chip, low_rows, tok - low_rows)
+        return remote(ref, ref, cs.at[i], cr.at[i], (2 * to + core, z))
+
+    def cot_pass(t, chip, parity):
+        start = (2 * chip + parity) * tok
+        ref = cot_hbm.at[pl.ds(pl.multiple_of(start, 16), tok)]
+        return remote(ref, ref, cps.at[t], cpr.at[t], (sib, z))
+
+    if square:
+        cot_pushes = [cot_send(0, chip_x), cot_send(1, chip_y)]
+        cot_chips = [me, chip_x, chip_y, chip_d]
+    else:
+        cot_pushes = [cot_send(t - 1, lax.rem(me + t, half)) for t in range(1, half)]
+        cot_chips = [lax.rem(me + half - t, half) for t in range(half)]
+    for copy in cot_pushes:
+        copy.start()
+    cot_local.wait()
+    cot_pass(0, me, core).start()
     wfull[z] = wo_ref[...]
 
     def forward(t, carry):
@@ -971,6 +1021,17 @@
         zz = lax.rem(z + nz - k, nz)
         weight_copy(zz, k, zz).wait_recv()
         weight_pass(zz, core, k).start()
+    if square:
+        cot_recv(0, chip_x).wait_recv()
+        cot_relay(2, chip_x, chip_y).start()
+        cot_pass(1, chip_x, core).start()
+        cot_recv(1, chip_y).wait_recv()
+        cot_relay(3, chip_y, chip_x).start()
+        cot_pass(2, chip_y, core).start()
+    else:
+        for t in range(1, half):
+            cot_recv(t - 1, cot_chips[t]).wait_recv()
+            cot_pass(t, cot_chips[t], core).start()
     for k in range(1, nz):
         row_copy(k, lax.rem(z + nz - k, nz)).wait_recv()
         weight_pass(lax.rem(z + nz - k, nz), 1 - core, k).wait_recv()
@@ -978,6 +1039,17 @@
     for zz in range(nz):
         mid = mid + dot_nn(acol[zz], wfull[zz])
     mid_ref[...] = mid
+    if square:
+        cot_relay(2, chip_d, chip_y).wait_recv()
+        cot_relay(3, chip_d, chip_x).wait_recv()
+        cot_pass(3, chip_d, core).start()
+        cot_relay(2, chip_x, chip_y).wait_send()
+        cot_relay(3, chip_y, chip_x).wait_send()
+    for copy in cot_pushes:
+        copy.wait_send()
+    for t in range(half):
+        cot_pass(t, cot_chips[t], 1 - core).wait_recv()
+        cot_pass(t, cot_chips[t], core).wait_send()
     for k in range(1, nz):
         row_copy(k, lax.rem(z + k, nz)).wait_send()
         weight_send(k).wait_send()
@@ -998,7 +1070,7 @@
     lax.fori_loop(0, half, sent, 0)
 
 
-def attend_layer(n, nz, x, gain, wq, wk, wv, wo, cos, sin, lens):
+def attend_layer(n, nz, x, gain, wq, wk, wv, wo, cos, sin, cot, lens):
     tok, width = x.shape
     rows = tok // nz
     qw, kw = wq.shape[1], wk.shape[1]
@@ -1018,9 +1090,10 @@
             sds((seqs, n * span, 2 * kw), bf16),
             sds((seqs * (kw // HD), 8, stacked), f32),
             sds((tok, qw), f32),
+            sds((n * tok, width), bf16),
         ],
-        in_specs=[vmem] * 8 + [pl.BlockSpec(memory_space=pltpu.SMEM)],
-        out_specs=[vmem] * 5,
+        in_specs=[vmem] * 9 + [pl.BlockSpec(memory_space=pltpu.SMEM)],
+        out_specs=[vmem] * 5 + [pl.BlockSpec(memory_space=pl.ANY)],
         scratch_shapes=[
             pltpu.VMEM((width, qw + 2 * kw), bf16),
             pltpu.VMEM((nz, qw, width), bf16),
@@ -1032,12 +1105,15 @@
             pltpu.VMEM((nz, rows, qw), bf16),
         ]
         + [dma((half, seqs))] * 4
-        + [dma((nz - 1,))] * 6,
+        + [dma((nz - 1,))] * 6
+        + [pltpu.VMEM((tok, width), bf16)]
+        + [dma((max(half, 4),))] * 4
+        + [dma],
         compiler_params=pltpu.CompilerParams(
             collective_id=2, has_side_effects=True, vmem_limit_bytes=60 << 20
         ),
         name="attend",
-    )(x, gain[None], wq, wk, wv, wo, cos, sin, lens)
+    )(x, gain[None], wq, wk, wv, wo, cos, sin, cot, lens)
 
 
 def return_kernel(
@@ -1911,10 +1987,9 @@
     angles = (lax.axis_index("expert") * span_rows + row).astype(f32) * frequency
     cosines = jnp.cos(angles)
     sines = jnp.sin(angles)
-    cot_all = lax.all_gather(cotangent.astype(bf16), "expert", axis=0, tiled=True)
     weights = (query_weight, key_weight, value_weight, out_weight, cosines, sines)
-    middle, queries, pairs, logs, attended = attend_layer(
-        n, nz, inputs, attention_gain, *weights, seq_lens
+    middle, queries, pairs, logs, attended, cot_all = attend_layer(
+        n, nz, inputs, attention_gain, *weights, cotangent, seq_lens
     )
     (
         grad_middle,

time: 259 us -> 243 us (0.938)
  Pallas kernels: 226 us -> 240 us
  between operations: 14.1 us -> 0.88 us
  waiting for transfers between devices: 13.1 us -> 0 us
    all_gather x1 -> x0, waiting for transfers between devices: 13.1 us -> none  [shards(): lax.all_gather(cotangent.astype(bf16), 'expert', axis=0, tiled=True)]
    pallas_call x1, Pallas kernels: 37.5 us -> 49.4 us  [attend_layer(): pl.pallas_call(functools.partial(attend_kernel, n, nz), out_shape=[sds((r...]
  transfers between devices with their start and end apart: 1 -> 0, of which waited for: 1 -> 0; matrix products, arithmetic and copies ran while one was open for 1% -> 0% of each run, Pallas kernels for 15% -> 0%
where the time goes in v10:
time: 243 us
  Pallas kernels  240 us (99%)
    pallas_call x1, Pallas kernels, return_layer(): pl.pallas_call(functools.partial(return_kernel, n, nz), out_shape=[sds((t...  99 us
    pallas_call x1, Pallas kernels, expert_layer(): pl.pallas_call(functools.partial(expert_kernel, n, nz, big), out_shape=ou...  82.3 us
    pallas_call x1, Pallas kernels, attend_layer(): pl.pallas_call(functools.partial(attend_kernel, n, nz), out_shape=[sds((r...  49.4 us
    pallas_call x1, Pallas kernels, finish_layer(): pl.pallas_call(finish_kernel, out_shape=[sds((tok, width), f32), sds((tok...  9.46 us

profile of v10, /device:TPU:0, one launch (start us, length us, event | category | flops | bytes accessed | tf_op | source)
XLA Modules:
  0.0 243.1 jit_solution(10556506008722635266)
XLA Ops:
  0.7 2.1 fusion
  2.8 49.4 %attend.1 = (f32[96,1024]{1,0:T(8,128)}, bf16[384,256]{1,0:T(8,128)(2,1)}, bf16[2,1536,256]{2,1,0:T(8,128)(2,1)}, f32[4,8,384]{2,1,0:T(8,128)}, f32[384,256]{1,0:T(8,128)}, /*index=5*/bf16[3072,1024]{1,0:T(8,128)(2,1)}) custom-call(bf16[384,1024]{1,0:T(8,128)(2,1)} %x_ref.3, f32[1,1024]{1,0:T(1,128)} %bitcast.13, bf16[1024,256]{1,0:T(8,128)(2,1)} %wq_ref.3, ...), custom_call_target="tpu_custom_call" | custom-call | tf_op jit(solution)/shard_map/attend/pallas_call | solution.py:1085
  52.2 82.3 %experts.1 = (f32[96,1024]{1,0:T(8,128)}, bf16[32,128]{1,0:T(8,128)(2,1)}, f32[1,1024]{1,0:T(1,128)}, f32[1,32]{1,0:T(1,128)}, f32[4,1024,128]{2,1,0:T(8,128)}, ...) custom-call(f32[96,1024]{1,0:T(8,128)} %get-tuple-element.48.mid_ref, ...), custom_call_target="tpu_custom_call" | custom-call | tf_op jit(solution)/shard_map/experts/pallas_call | solution.py:771
  134.4 99.0 %attend_back.1 = (bf16[384,1024]{1,0:T(8,128)(2,1)}, bf16[384,1024]{1,0:T(8,128)(2,1)}, bf16[8,128,512]{2,1,0:T(8,128)(2,1)}, bf16[8,128,256]{2,1,0:T(8,128)(2,1)}, f32[48,1024]{1,0:T(8,128)}) custom-call(f32[96,1024]{1,0:T(8,128)} %get-tuple-element.50.gmid_ref, f32[96,1024]{1,0:T(8,128)} %get-tuple-element.48.mid_ref, ...), custom_call_target="tpu_custom_call" | custom-call | tf_op jit(solution)/shard_map/attend_back/pallas_call | solution.py:1795
  233.5 9.5 %finish.1 = (f32[384,1024]{1,0:T(8,128)}, f32[384,1024]{1,0:T(8,128)}, f32[1024,256]{1,0:T(8,128)}, f32[1024,128]{1,0:T(8,128)}, f32[1024,128]{1,0:T(8,128)}, /*...) custom-call(bf16[384,1024]{1,0:T(8,128)(2,1)} %get-tuple-element.59., ...), custom_call_target="tpu_custom_call" | custom-call | tf_op jit(solution)/shard_map/finish/pallas_call | solution.py:1932
  (4 shorter events, 0.0 us)

commit v11 on v10

--- a/solution.py
+++ b/solution.py
@@ -1489,7 +1489,10 @@
                 w2.pack[j] = pair_part[j * dn : (j + 1) * dn].astype(bf16)
             w2.give()
             w1.total()
-    w2.spread()
+        if hop == 1:
+            w2.spread()
+    if nz == 2:
+        w2.spread()
     normed_sum.total(sums, normed_part)
 
     own_x = x_ref[own_rows, :].astype(f32)
@@ -1507,6 +1510,7 @@
     igrad_line.start()
     out_line.hop(nz - 1)
 
+    w2.total()
     w1.forward()
     for copy in z_arrivals(slot_of(sz2), z2s, z2r):
         copy.wait_recv()
@@ -1528,12 +1532,10 @@
     for t in range(1, half):
         small_send(t).start()
 
-    w2.total()
     for hop in range(2, nz - 1):
         igrad_line.hop(hop)
+    w2.forward()
     igrad_line.hop(nz - 1)
-
-    w2.forward()
     for t in range(1, half):
         src = lax.rem(me + half - t, half)
         remote(

time: 243 us -> 240 us (0.988)
  Pallas kernels: 240 us -> 236 us
    pallas_call x1, Pallas kernels: 99 us -> 95.3 us  [return_layer(): pl.pallas_call(functools.partial(return_kernel, n, nz), out_shape=[sds((t...]
where the time goes in v11:
time: 240 us; the launch traced here: 239 us
  Pallas kernels  236 us (98%)
    pallas_call x1, Pallas kernels, return_layer(): pl.pallas_call(functools.partial(return_kernel, n, nz), out_shape=[sds((t...  95.3 us
    pallas_call x1, Pallas kernels, expert_layer(): pl.pallas_call(functools.partial(expert_kernel, n, nz, big), out_shape=ou...  82.3 us
    pallas_call x1, Pallas kernels, attend_layer(): pl.pallas_call(functools.partial(attend_kernel, n, nz), out_shape=[sds((r...  49.4 us
    pallas_call x1, Pallas kernels, finish_layer(): pl.pallas_call(finish_kernel, out_shape=[sds((tok, width), f32), sds((tok...  9.46 us

profile of v11, /device:TPU:0, one launch (start us, length us, event | category | flops | bytes accessed | tf_op | source)
XLA Modules:
  0.0 239.3 jit_solution(849103259022453517)
XLA Ops:
  0.7 2.1 fusion
  2.8 49.4 %attend.1 = (f32[96,1024]{1,0:T(8,128)}, bf16[384,256]{1,0:T(8,128)(2,1)}, bf16[2,1536,256]{2,1,0:T(8,128)(2,1)}, f32[4,8,384]{2,1,0:T(8,128)}, f32[384,256]{1,0:T(8,128)}, /*index=5*/bf16[3072,1024]{1,0:T(8,128)(2,1)}) custom-call(bf16[384,1024]{1,0:T(8,128)(2,1)} %x_ref.3, f32[1,1024]{1,0:T(1,128)} %bitcast.13, bf16[1024,256]{1,0:T(8,128)(2,1)} %wq_ref.3, ...), custom_call_target="tpu_custom_call" | custom-call | tf_op jit(solution)/shard_map/attend/pallas_call | solution.py:1085
  52.2 82.3 %experts.1 = (f32[96,1024]{1,0:T(8,128)}, bf16[32,128]{1,0:T(8,128)(2,1)}, f32[1,1024]{1,0:T(1,128)}, f32[1,32]{1,0:T(1,128)}, f32[4,1024,128]{2,1,0:T(8,128)}, ...) custom-call(f32[96,1024]{1,0:T(8,128)} %get-tuple-element.48.mid_ref, ...), custom_call_target="tpu_custom_call" | custom-call | tf_op jit(solution)/shard_map/experts/pallas_call | solution.py:771
  134.4 95.3 %attend_back.1 = (bf16[384,1024]{1,0:T(8,128)(2,1)}, bf16[384,1024]{1,0:T(8,128)(2,1)}, bf16[8,128,512]{2,1,0:T(8,128)(2,1)}, bf16[8,128,256]{2,1,0:T(8,128)(2,1)}, f32[48,1024]{1,0:T(8,128)}) custom-call(f32[96,1024]{1,0:T(8,128)} %get-tuple-element.50.gmid_ref, f32[96,1024]{1,0:T(8,128)} %get-tuple-element.48.mid_ref, ...), custom_call_target="tpu_custom_call" | custom-call | tf_op jit(solution)/shard_map/attend_back/pallas_call | solution.py:1797
  229.7 9.5 %finish.1 = (f32[384,1024]{1,0:T(8,128)}, f32[384,1024]{1,0:T(8,128)}, f32[1024,256]{1,0:T(8,128)}, f32[1024,128]{1,0:T(8,128)}, f32[1024,128]{1,0:T(8,128)}, /*...) custom-call(bf16[384,1024]{1,0:T(8,128)(2,1)} %get-tuple-element.59., ...), custom_call_target="tpu_custom_call" | custom-call | tf_op jit(solution)/shard_map/finish/pallas_call | solution.py:1934
  (4 shorter events, 0.0 us)

commit v12 on v11

--- a/solution.py
+++ b/solution.py
@@ -1493,6 +1493,15 @@
             w2.spread()
     if nz == 2:
         w2.spread()
+    w1.forward()
+    for copy in z_arrivals(slot_of(sz2), z2s, z2r):
+        copy.wait_recv()
+    second = sz2[0].astype(f32)
+    for zz in range(1, nz):
+        second = second + sz2[zz].astype(f32)
+    sown[experts:, :] = second.astype(bf16)
+    small_sib = remote(sown, ssib, sbs, sbr, (sib, z))
+    small_sib.start()
     normed_sum.total(sums, normed_part)
 
     own_x = x_ref[own_rows, :].astype(f32)
@@ -1511,17 +1520,6 @@
     out_line.hop(nz - 1)
 
     w2.total()
-    w1.forward()
-    for copy in z_arrivals(slot_of(sz2), z2s, z2r):
-        copy.wait_recv()
-    second = sz2[0].astype(f32)
-    for zz in range(1, nz):
-        second = second + sz2[zz].astype(f32)
-    sown[experts:, :] = second.astype(bf16)
-    small_sib = remote(sown, ssib, sbs, sbr, (sib, z))
-    small_sib.start()
-    if nz > 2:
-        igrad_line.hop(1)
     small_sib.wait_recv()
     schip[me] = (sown[...].astype(f32) + ssib[...].astype(f32)).astype(bf16)
 
@@ -1532,7 +1530,7 @@
     for t in range(1, half):
         small_send(t).start()
 
-    for hop in range(2, nz - 1):
+    for hop in range(1, nz - 1):
         igrad_line.hop(hop)
     w2.forward()
     igrad_line.hop(nz - 1)

time: 240 us -> 239 us (level)
  no operation moved by 1% of the time
where the time goes in v12:
time: 239 us; the launch traced here: 238 us
  Pallas kernels  235 us (98%)
    pallas_call x1, Pallas kernels, return_layer(): pl.pallas_call(functools.partial(return_kernel, n, nz), out_shape=[sds((t...  93.8 us
    pallas_call x1, Pallas kernels, expert_layer(): pl.pallas_call(functools.partial(expert_kernel, n, nz, big), out_shape=ou...  82.3 us
    pallas_call x1, Pallas kernels, attend_layer(): pl.pallas_call(functools.partial(attend_kernel, n, nz), out_shape=[sds((r...  49.4 us
    pallas_call x1, Pallas kernels, finish_layer(): pl.pallas_call(finish_kernel, out_shape=[sds((tok, width), f32), sds((tok...  9.46 us

profile of v12, /device:TPU:0, one launch (start us, length us, event | category | flops | bytes accessed | tf_op | source)
XLA Modules:
  0.0 237.9 jit_solution(14431544008811361148)
XLA Ops:
  0.7 2.1 fusion
  2.8 49.4 %attend.1 = (f32[96,1024]{1,0:T(8,128)}, bf16[384,256]{1,0:T(8,128)(2,1)}, bf16[2,1536,256]{2,1,0:T(8,128)(2,1)}, f32[4,8,384]{2,1,0:T(8,128)}, f32[384,256]{1,0:T(8,128)}, /*index=5*/bf16[3072,1024]{1,0:T(8,128)(2,1)}) custom-call(bf16[384,1024]{1,0:T(8,128)(2,1)} %x_ref.3, f32[1,1024]{1,0:T(1,128)} %bitcast.13, bf16[1024,256]{1,0:T(8,128)(2,1)} %wq_ref.3, ...), custom_call_target="tpu_custom_call" | custom-call | tf_op jit(solution)/shard_map/attend/pallas_call | solution.py:1085
  52.2 82.3 %experts.1 = (f32[96,1024]{1,0:T(8,128)}, bf16[32,128]{1,0:T(8,128)(2,1)}, f32[1,1024]{1,0:T(1,128)}, f32[1,32]{1,0:T(1,128)}, f32[4,1024,128]{2,1,0:T(8,128)}, ...) custom-call(f32[96,1024]{1,0:T(8,128)} %get-tuple-element.48.mid_ref, ...), custom_call_target="tpu_custom_call" | custom-call | tf_op jit(solution)/shard_map/experts/pallas_call | solution.py:771
  134.4 93.8 %attend_back.1 = (bf16[384,1024]{1,0:T(8,128)(2,1)}, bf16[384,1024]{1,0:T(8,128)(2,1)}, bf16[8,128,512]{2,1,0:T(8,128)(2,1)}, bf16[8,128,256]{2,1,0:T(8,128)(2,1)}, f32[48,1024]{1,0:T(8,128)}) custom-call(f32[96,1024]{1,0:T(8,128)} %get-tuple-element.50.gmid_ref, f32[96,1024]{1,0:T(8,128)} %get-tuple-element.48.mid_ref, ...), custom_call_target="tpu_custom_call" | custom-call | tf_op jit(solution)/shard_map/attend_back/pallas_call | solution.py:1795
  228.2 9.5 %finish.1 = (f32[384,1024]{1,0:T(8,128)}, f32[384,1024]{1,0:T(8,128)}, f32[1024,256]{1,0:T(8,128)}, f32[1024,128]{1,0:T(8,128)}, f32[1024,128]{1,0:T(8,128)}, /*...) custom-call(bf16[384,1024]{1,0:T(8,128)(2,1)} %get-tuple-element.59., ...), custom_call_target="tpu_custom_call" | custom-call | tf_op jit(solution)/shard_map/finish/pallas_call | solution.py:1932
  (4 shorter events, 0.0 us)
